TPU v7x, 32 devices: a whole 2x2x4 slice. The times are simulated.
32 devices in a mesh: batch: 4 (over z), seq: 8 (over y, x, core).
Axes of the slice: x: 2, y: 2, z: 4, core: 2. Of those that a mesh axis runs over, the one named last changes fastest.
Arguments:
- tokens: bfloat16 [4, 2048, 512], P('batch', 'seq'), may hold values from -6 to 6
- cotangent: bfloat16 [4, 2048, 512], P('batch', 'seq'), may hold values from -6 to 6
- item_start: int32 [4, 2], P('batch'), may hold values from 0 to 1024, as said below
- first_gain: float32 [512], replicated, may hold values from 0.5 to 1.5
- first_shift: float32 [512], replicated, may hold values from -4 to 4
- query_weight: bfloat16 [512, 512], replicated, may hold values from -0.25 to 0.25
- query_bias: float32 [512], replicated, may hold values from -4 to 4
- key_weight: bfloat16 [512, 512], replicated, may hold values from -0.25 to 0.25
- value_weight: bfloat16 [512, 512], replicated, may hold values from -0.25 to 0.25
- value_bias: float32 [512], replicated, may hold values from -4 to 4
- out_weight: bfloat16 [512, 512], replicated, may hold values from -0.75 to 0.75
- out_bias: float32 [512], replicated, may hold values from -4 to 4
- second_gain: float32 [512], replicated, may hold values from 0.5 to 1.5
- second_shift: float32 [512], replicated, may hold values from -4 to 4
- up_weight: bfloat16 [512, 2048], replicated, may hold values from -0.25 to 0.25
- up_bias: float32 [2048], replicated, may hold values from -4 to 4
- down_weight: bfloat16 [2048, 512], replicated, may hold values from -0.125 to 0.125
- down_bias: float32 [512], replicated, may hold values from -4 to 4
Outputs:
- output: bfloat16 [4, 2048, 512], P('batch', 'seq')
- grad_tokens: float32 [4, 2048, 512], P('batch', 'seq')
- grad_query_weight: float32 [512, 512], replicated
- grad_key_weight: float32 [512, 512], replicated
- grad_value_weight: float32 [512, 512], replicated
- grad_out_weight: float32 [512, 512], replicated
- grad_up_weight: float32 [512, 2048], replicated
- grad_down_weight: float32 [2048, 512], replicated
- grad_query_bias: float32 [512], replicated
- grad_value_bias: float32 [512], replicated
- grad_out_bias: float32 [512], replicated
- grad_up_bias: float32 [2048], replicated
- grad_down_bias: float32 [512], replicated
- grad_first_gain: float32 [512], replicated
- grad_first_shift: float32 [512], replicated
- grad_second_gain: float32 [512], replicated
- grad_second_shift: float32 [512], replicated
Inputs may be any that keep to these rules, and one draw needn't show every extreme that they name: `item_start`: A stream is either one item of 2048 tokens or items of 1024 tokens each; some stream of every draw is one item, and some other is made of short items.
All inputs are finite; a program needn't handle non-finite values.
Results may differ from a plain program's by a relative error of at most 0.012.
Values may be sent and summed in bfloat16 or wider, within the bound.
No kernel may reach another device: no remote copies, remote signals or barrier semaphores. Data moves between devices by JAX's collectives and lax.ppermute only.
A program may use at most 320 MiB of HBM per device.

v0:
```python
import math

import jax
import jax.numpy as jnp
from jax import lax
from jax.sharding import PartitionSpec as P

HEADS = 8
BLOCK = 16
UNIT = 1024


NORM_EPS = 1e-05
LOG_TWO = math.log(2.0)


def with_halo(block, sides, width):
    for axis, dim in sides:
        count = lax.axis_size(axis)
        forward = [(i, i + 1) for i in range(count - 1)]
        backward = [(target, source) for source, target in forward]
        low = lax.ppermute(
            lax.slice_in_dim(block, block.shape[dim] - width, None, axis=dim), axis, forward
        )
        high = lax.ppermute(lax.slice_in_dim(block, 0, width, axis=dim), axis, backward)
        block = jnp.concatenate([low, block, high], axis=dim)
    return block


def from_behind(array, axis, by):
    peers = lax.axis_size(axis)
    pairs = [(i, i + by) for i in range(peers) if 0 <= i + by < peers]
    return lax.ppermute(array, axis, pairs)


def layer_norm(values, gain, shift):
    centre = jnp.mean(values, axis=-1, keepdims=True)
    centred = values - centre
    spread = jnp.mean(centred * centred, axis=-1, keepdims=True)
    return centred * lax.rsqrt(spread + NORM_EPS) * gain + shift


def gelu_exact(values):
    return jax.nn.gelu(values, approximate=False)


def product(left, right):
    return jnp.dot(left, right, preferred_element_type=jnp.float32)


def left_product(left, right):
    return lax.dot_general(
        left, right, (((0,), (0,)), ((), ())), preferred_element_type=jnp.float32
    )


def right_product(left, right):
    return lax.dot_general(
        left, right, (((1,), (1,)), ((), ())), preferred_element_type=jnp.float32
    )


def start_lookup(positions, start_table):
    unit_ids = positions // UNIT
    slot_ids = jnp.arange(start_table.shape[0], dtype=jnp.int32)
    matches = unit_ids[..., None] == slot_ids
    return jnp.sum(jnp.where(matches, start_table, 0), axis=-1)


def banded(padded, row_count):
    blocks = row_count // BLOCK
    sections = [
        padded[offset * BLOCK : offset * BLOCK + row_count].reshape(
            (blocks, BLOCK) + padded.shape[1:]
        )
        for offset in range(3)
    ]
    return jnp.concatenate(sections, axis=1)


def unbanded(grad_band, row_count):
    summed = jnp.zeros((row_count + 2 * BLOCK, grad_band.shape[-1]), jnp.float32)
    for offset in range(3):
        section = grad_band[:, offset * BLOCK : (offset + 1) * BLOCK].reshape(row_count, -1)
        summed = summed + jnp.pad(section, ((offset * BLOCK, (2 - offset) * BLOCK), (0, 0)))
    return summed


def pool_pieces(rows, levels):
    piece_count, row_count, width = rows.shape
    pooled = []
    for level_id in range(1, levels + 1):
        pool_size = 2**level_id
        pool_rows = row_count // pool_size
        pooled.append(
            jnp.mean(
                rows.reshape(piece_count, pool_rows, pool_size, width), axis=2, dtype=jnp.float32
            )
        )
    return jnp.concatenate(pooled, axis=1).astype(jnp.bfloat16)


def spread_pooled(grads, levels, row_count):
    piece_count = grads.shape[0]
    width = grads.shape[2]
    total = jnp.zeros((piece_count, row_count, width), jnp.float32)
    start_row = 0
    for level_id in range(1, levels + 1):
        pool_size = 2**level_id
        pool_rows = row_count // pool_size
        section = grads[:, start_row : start_row + pool_rows] / pool_size
        total = total + jnp.broadcast_to(
            section[:, :, None, :], (piece_count, pool_rows, pool_size, width)
        ).reshape(piece_count, row_count, width)
        start_row += pool_rows
    return total


def head_scores(query_rows, key_band, far_key, near_mask, far_mask, far_bias, score_scale):
    blocks = key_band.shape[0]
    query_blocks = query_rows.reshape(blocks, BLOCK, -1)
    near_score = (
        jnp.einsum("iae,ibe->iab", query_blocks, key_band, preferred_element_type=jnp.float32)
        * score_scale
    )
    near_score = jnp.where(near_mask, near_score, -jnp.inf)
    far_score = right_product(query_rows, far_key) * score_scale + far_bias
    far_score = jnp.where(far_mask, far_score, -jnp.inf)
    return (near_score, far_score)


def on_device(
    tokens,
    cotangent,
    item_start,
    first_gain,
    first_shift,
    query_weight,
    query_bias,
    key_weight,
    value_weight,
    value_bias,
    out_weight,
    out_bias,
    second_gain,
    second_shift,
    up_weight,
    up_bias,
    down_weight,
    down_bias,
):
    row_count = tokens.shape[1]
    model_width = tokens.shape[2]
    head_dim = model_width // HEADS
    score_scale = 1.0 / math.sqrt(head_dim)
    blocks = row_count // BLOCK
    seq_place = lax.axis_index("seq")
    seq_count = lax.axis_size("seq")
    stream_len = row_count * seq_count
    levels = (stream_len // (4 * BLOCK)).bit_length() - 1
    start_table = item_start[0]
    row_base = seq_place * row_count
    own_start = start_lookup(row_base, start_table)
    inputs = tokens[0].astype(jnp.float32)
    normed_first = layer_norm(inputs, first_gain, first_shift)
    low_first = normed_first.astype(jnp.bfloat16)
    query = (product(low_first, query_weight) + query_bias).astype(jnp.bfloat16)
    key_rows = product(low_first, key_weight).astype(jnp.bfloat16)
    value_rows = (product(low_first, value_weight) + value_bias).astype(jnp.bfloat16)
    key_value = jnp.concatenate([key_rows, value_rows], axis=1)
    padded = with_halo(key_value, (("seq", 0),), BLOCK)
    summary = pool_pieces(key_value[None], levels)
    window = lax.all_gather(summary, "seq", axis=0, tiled=True)
    near_band = banded(padded, row_count)
    pad_pos = row_base - BLOCK + jnp.arange(row_count + 2 * BLOCK, dtype=jnp.int32)
    pad_valid = (
        (pad_pos >= 0) & (pad_pos < stream_len) & (start_lookup(pad_pos, start_table) == own_start)
    )
    near_mask = banded(pad_valid, row_count)[:, None, :]
    level_list = []
    offset_list = []
    for level_id in range(1, levels + 1):
        pool_size = 2**level_id
        pool_rows = row_count // pool_size
        level_list.append(jnp.full((pool_rows,), level_id, jnp.int32))
        offset_list.append(jnp.arange(pool_rows, dtype=jnp.int32) * pool_size)
    row_levels = jnp.concatenate(level_list)
    row_offsets = jnp.concatenate(offset_list)
    summary_rows = row_levels.shape[0]
    far_rows = seq_count * summary_rows
    window_flat = window.reshape(far_rows, 2 * model_width)
    piece_base = jnp.arange(seq_count, dtype=jnp.int32) * row_count
    far_pos = (piece_base[:, None] + row_offsets[None, :]).reshape(far_rows)
    far_level = jnp.tile(row_levels, seq_count)
    far_span = BLOCK * jnp.left_shift(jnp.int32(1), far_level)
    query_pos = row_base + jnp.arange(row_count, dtype=jnp.int32) - own_start
    query_block = query_pos[:, None] // far_span[None, :]
    far_block = (far_pos - own_start) // far_span
    parent_gap = far_block[None, :] // 2 - query_block // 2
    far_mask = (
        (start_lookup(far_pos, start_table) == own_start)[None, :]
        & (jnp.abs(parent_gap) <= 1)
        & (jnp.abs(far_block[None, :] - query_block) >= 2)
    )
    far_bias = far_level.astype(jnp.float32) * LOG_TWO
    head_query = query.reshape(row_count, HEADS, head_dim).transpose(1, 0, 2)
    head_key_band = (
        near_band[..., :model_width]
        .reshape(blocks, 3 * BLOCK, HEADS, head_dim)
        .transpose(2, 0, 1, 3)
    )
    head_value_band = (
        near_band[..., model_width:]
        .reshape(blocks, 3 * BLOCK, HEADS, head_dim)
        .transpose(2, 0, 1, 3)
    )
    head_far_key = (
        window_flat[:, :model_width].reshape(far_rows, HEADS, head_dim).transpose(1, 0, 2)
    )
    head_far_value = (
        window_flat[:, model_width:].reshape(far_rows, HEADS, head_dim).transpose(1, 0, 2)
    )

    def head_forward(head_inputs):
        query_rows, key_band, value_band, far_key, far_value = head_inputs
        near_score, far_score = head_scores(
            query_rows, key_band, far_key, near_mask, far_mask, far_bias, score_scale
        )
        row_top = jnp.maximum(
            jnp.max(near_score, axis=2).reshape(row_count), jnp.max(far_score, axis=1)
        )
        row_total = jnp.sum(
            jnp.exp(near_score - row_top.reshape(blocks, BLOCK, 1)), axis=2
        ).reshape(row_count)
        row_total = row_total + jnp.sum(jnp.exp(far_score - row_top[:, None]), axis=1)
        log_total = row_top + jnp.log(row_total)
        near_weight = jnp.exp(near_score - log_total.reshape(blocks, BLOCK, 1)).astype(jnp.bfloat16)
        far_weight = jnp.exp(far_score - log_total[:, None]).astype(jnp.bfloat16)
        mixed = jnp.einsum(
            "iab,ibe->iae", near_weight, value_band, preferred_element_type=jnp.float32
        ).reshape(row_count, head_dim)
        mixed = mixed + product(far_weight, far_value)
        return (mixed, log_total)

    head_mixed, head_log = lax.map(
        head_forward, (head_query, head_key_band, head_value_band, head_far_key, head_far_value)
    )
    attended = head_mixed.transpose(1, 0, 2).reshape(row_count, model_width).astype(jnp.bfloat16)
    mid = inputs + product(attended, out_weight) + out_bias
    normed_second = layer_norm(mid, second_gain, second_shift)
    low_second = normed_second.astype(jnp.bfloat16)
    upper = product(low_second, up_weight) + up_bias
    active, gelu_back = jax.vjp(gelu_exact, upper)
    active_low = active.astype(jnp.bfloat16)
    result = mid + product(active_low, down_weight) + down_bias
    output = result.astype(jnp.bfloat16)
    grad_out = cotangent[0]
    grad_down = left_product(active_low, grad_out)
    grad_down_bias = jnp.sum(grad_out.astype(jnp.float32), axis=0)
    grad_active = right_product(grad_out, down_weight)
    grad_upper = gelu_back(grad_active)[0].astype(jnp.bfloat16)
    grad_up = left_product(low_second, grad_upper)
    grad_up_bias = jnp.sum(grad_upper.astype(jnp.float32), axis=0)
    grad_normed_second = right_product(grad_upper, up_weight)
    second_norm_back = jax.vjp(layer_norm, mid, second_gain, second_shift)[1]
    grad_mid_norm, grad_second_gain, grad_second_shift = second_norm_back(grad_normed_second)
    grad_mid = grad_out.astype(jnp.float32) + grad_mid_norm
    grad_branch = grad_mid.astype(jnp.bfloat16)
    grad_out_w = left_product(attended, grad_branch)
    grad_out_bias = jnp.sum(grad_branch.astype(jnp.float32), axis=0)
    grad_attended = right_product(grad_branch, out_weight).astype(jnp.bfloat16)
    head_grad = grad_attended.reshape(row_count, HEADS, head_dim).transpose(1, 0, 2)

    def head_backward(head_inputs):
        query_rows, key_band, value_band, far_key, far_value, log_total, grad_rows = head_inputs
        near_score, far_score = head_scores(
            query_rows, key_band, far_key, near_mask, far_mask, far_bias, score_scale
        )
        near_prob = jnp.exp(near_score - log_total.reshape(blocks, BLOCK, 1))
        far_prob = jnp.exp(far_score - log_total[:, None])
        grad_blocks = grad_rows.reshape(blocks, BLOCK, head_dim)
        near_dprob = jnp.einsum(
            "iae,ibe->iab", grad_blocks, value_band, preferred_element_type=jnp.float32
        )
        far_dprob = right_product(grad_rows, far_value)
        row_delta = jnp.sum(near_prob * near_dprob, axis=2).reshape(row_count) + jnp.sum(
            far_prob * far_dprob, axis=1
        )
        near_dscore = (near_prob * (near_dprob - row_delta.reshape(blocks, BLOCK, 1))).astype(
            jnp.bfloat16
        )
        far_dscore = (far_prob * (far_dprob - row_delta[:, None])).astype(jnp.bfloat16)
        query_blocks = query_rows.reshape(blocks, BLOCK, head_dim)
        grad_query_rows = jnp.einsum(
            "iab,ibe->iae", near_dscore, key_band, preferred_element_type=jnp.float32
        ).reshape(row_count, head_dim)
        grad_query_rows = (grad_query_rows + product(far_dscore, far_key)) * score_scale
        grad_key_band = (
            jnp.einsum(
                "iab,iae->ibe", near_dscore, query_blocks, preferred_element_type=jnp.float32
            )
            * score_scale
        )
        grad_value_band = jnp.einsum(
            "iab,iae->ibe",
            near_prob.astype(jnp.bfloat16),
            grad_blocks,
            preferred_element_type=jnp.float32,
        )
        grad_far_key = left_product(far_dscore, query_rows) * score_scale
        grad_far_value = left_product(far_prob.astype(jnp.bfloat16), grad_rows)
        return (grad_query_rows, grad_key_band, grad_value_band, grad_far_key, grad_far_value)

    head_grads = lax.map(
        head_backward,
        (
            head_query,
            head_key_band,
            head_value_band,
            head_far_key,
            head_far_value,
            head_log,
            head_grad,
        ),
    )
    grad_query = (
        head_grads[0].transpose(1, 0, 2).reshape(row_count, model_width).astype(jnp.bfloat16)
    )
    grad_band = jnp.concatenate(
        [
            head_grads[1].transpose(1, 2, 0, 3).reshape(blocks, 3 * BLOCK, model_width),
            head_grads[2].transpose(1, 2, 0, 3).reshape(blocks, 3 * BLOCK, model_width),
        ],
        axis=2,
    )
    grad_padded = unbanded(grad_band, row_count)
    grad_far = jnp.concatenate(
        [
            head_grads[3].transpose(1, 0, 2).reshape(far_rows, model_width),
            head_grads[4].transpose(1, 0, 2).reshape(far_rows, model_width),
        ],
        axis=1,
    )
    grad_far = grad_far.reshape(seq_count, summary_rows, 2 * model_width)
    head_rim = grad_padded[:BLOCK]
    tail_rim = grad_padded[row_count + BLOCK :]
    from_next = from_behind(head_rim.astype(jnp.bfloat16), "seq", -1).astype(head_rim.dtype)
    from_prev = from_behind(tail_rim.astype(jnp.bfloat16), "seq", 1).astype(tail_rim.dtype)
    grad_key_value = grad_padded[BLOCK : row_count + BLOCK]
    grad_key_value = grad_key_value + jnp.pad(from_prev, ((0, row_count - BLOCK), (0, 0)))
    grad_key_value = grad_key_value + jnp.pad(from_next, ((row_count - BLOCK, 0), (0, 0)))
    grad_summary = lax.psum_scatter(grad_far, "seq", scatter_dimension=0, tiled=True)
    grad_key_value = grad_key_value + spread_pooled(grad_summary, levels, row_count)[0]
    grad_key = grad_key_value[:, :model_width].astype(jnp.bfloat16)
    grad_value = grad_key_value[:, model_width:].astype(jnp.bfloat16)
    grad_query_w = left_product(low_first, grad_query)
    grad_key_w = left_product(low_first, grad_key)
    grad_value_w = left_product(low_first, grad_value)
    grad_query_bias = jnp.sum(grad_query.astype(jnp.float32), axis=0)
    grad_value_bias = jnp.sum(grad_value.astype(jnp.float32), axis=0)
    grad_normed_first = (
        right_product(grad_query, query_weight)
        + right_product(grad_key, key_weight)
        + right_product(grad_value, value_weight)
    )
    first_norm_back = jax.vjp(layer_norm, inputs, first_gain, first_shift)[1]
    grad_input_norm, grad_first_gain, grad_first_shift = first_norm_back(grad_normed_first)
    grad_tokens = grad_mid + grad_input_norm
    totals = lax.psum(
        (
            grad_query_w,
            grad_key_w,
            grad_value_w,
            grad_out_w,
            grad_up,
            grad_down,
            grad_query_bias,
            grad_value_bias,
            grad_out_bias,
            grad_up_bias,
            grad_down_bias,
            grad_first_gain,
            grad_first_shift,
            grad_second_gain,
            grad_second_shift,
        ),
        ("batch", "seq"),
    )
    return (output[None], grad_tokens[None]) + tuple(totals)


def solution(mesh):
    in_specs = (
        P("batch", "seq", None),
        P("batch", "seq", None),
        P("batch", None),
        P(),
        P(),
        P(),
        P(),
        P(),
        P(),
        P(),
        P(),
        P(),
        P(),
        P(),
        P(),
        P(),
        P(),
        P(),
    )
    out_specs = (
        P("batch", "seq", None),
        P("batch", "seq", None),
        P(),
        P(),
        P(),
        P(),
        P(),
        P(),
        P(),
        P(),
        P(),
        P(),
        P(),
        P(),
        P(),
        P(),
        P(),
    )
    return jax.shard_map(
        on_device, mesh=mesh, in_specs=in_specs, out_specs=out_specs, check_vma=False
    )
```

profile of v0, /device:TPU:0, one launch (start us, length us, event | category | flops | bytes accessed | tf_op | source)
XLA Modules:
  0.0 1087.4 jit_solution(3263631241279714879)
XLA Ops:
  65.0 11.5 %all-gather.2.cloned.1.call-done = bf16[8,248,1024]{2,1,0:T(8,128)(2,1)} async-done(((bf16[1,248,1024]{2,1,0:T(8,128)(2,1)}), bf16[8,248,1024]{2,1,0:T(8,128)(2,1)}) %all-gather.2.cloned.1.call-update) | async-done | bytes 4063248 | tf_op jit(solution)/shard_map/all_gather | solution.py:173
  98.2 271.0 %while.32 = (s32[]{:T(128)}, bf16[8,256,64]{1,2,0:T(8,128)(2,1)S(1)}, f32[8,256]{1,0:T(8,128)}, pred[16,1,48]{2,0,1:T(8,128)(4,1)S(1)}, bf16[8,256,64]{2,1,0:T(8...) while((s32[]{:T(128)}, ...), condition=%wide.region_15.16_spmd.clone, body=%wide.region_10.15_spmd.clone.sunk | while | flops 152573184 | bytes 8258389 | solution.py:245
  98.3 24.3 %fusion.264 = (f32[256]{0:T(256)S(1)}, f32[256,1984]{0,1:T(8,128)}) fusion(f32[1984]{0:T(1024)S(1)} %mul.550, bf16[8,1984,64]{2,1,0:T(8,128)(2,1)} %get-tuple-element.875, s32[]{:T(128)} %get-tuple-element.850, bf16[8,256,64]{2,1,0:T(8,128)(2,1)} %get-tuple-element.873, s32[1984]{0:T(1024)} %get-tuple-element.885, s32[1984]{0:T(1024)} %get-tuple-element.883, ...), kind=kOutput, calls=%fused_computation.323.clone.1 | convolution fusion | flops 82280192 | bytes 2651840 | tf_op jit(solution)/shard_map/while/body/eval_jaxpr/dot_general | solution.py:58
  132.1 24.3 %fusion.264 = (f32[256]{0:T(256)S(1)}, f32[256,1984]{0,1:T(8,128)}) fusion(f32[1984]{0:T(1024)S(1)} %mul.550, bf16[8,1984,64]{2,1,0:T(8,128)(2,1)} %get-tuple-element.875, s32[]{:T(128)} %get-tuple-element.850, bf16[8,256,64]{2,1,0:T(8,128)(2,1)} %get-tuple-element.873, s32[1984]{0:T(1024)} %get-tuple-element.885, s32[1984]{0:T(1024)} %get-tuple-element.883, ...), kind=kOutput, calls=%fused_computation.323.clone.1 | convolution fusion | flops 82280192 | bytes 2651840 | tf_op jit(solution)/shard_map/while/body/eval_jaxpr/dot_general | solution.py:58
  166.0 24.3 %fusion.264 = (f32[256]{0:T(256)S(1)}, f32[256,1984]{0,1:T(8,128)}) fusion(f32[1984]{0:T(1024)S(1)} %mul.550, bf16[8,1984,64]{2,1,0:T(8,128)(2,1)} %get-tuple-element.875, s32[]{:T(128)} %get-tuple-element.850, bf16[8,256,64]{2,1,0:T(8,128)(2,1)} %get-tuple-element.873, s32[1984]{0:T(1024)} %get-tuple-element.885, s32[1984]{0:T(1024)} %get-tuple-element.883, ...), kind=kOutput, calls=%fused_computation.323.clone.1 | convolution fusion | flops 82280192 | bytes 2651840 | tf_op jit(solution)/shard_map/while/body/eval_jaxpr/dot_general | solution.py:58
  199.9 24.3 %fusion.264 = (f32[256]{0:T(256)S(1)}, f32[256,1984]{0,1:T(8,128)}) fusion(f32[1984]{0:T(1024)S(1)} %mul.550, bf16[8,1984,64]{2,1,0:T(8,128)(2,1)} %get-tuple-element.875, s32[]{:T(128)} %get-tuple-element.850, bf16[8,256,64]{2,1,0:T(8,128)(2,1)} %get-tuple-element.873, s32[1984]{0:T(1024)} %get-tuple-element.885, s32[1984]{0:T(1024)} %get-tuple-element.883, ...), kind=kOutput, calls=%fused_computation.323.clone.1 | convolution fusion | flops 82280192 | bytes 2651840 | tf_op jit(solution)/shard_map/while/body/eval_jaxpr/dot_general | solution.py:58
  233.7 24.3 %fusion.264 = (f32[256]{0:T(256)S(1)}, f32[256,1984]{0,1:T(8,128)}) fusion(f32[1984]{0:T(1024)S(1)} %mul.550, bf16[8,1984,64]{2,1,0:T(8,128)(2,1)} %get-tuple-element.875, s32[]{:T(128)} %get-tuple-element.850, bf16[8,256,64]{2,1,0:T(8,128)(2,1)} %get-tuple-element.873, s32[1984]{0:T(1024)} %get-tuple-element.885, s32[1984]{0:T(1024)} %get-tuple-element.883, ...), kind=kOutput, calls=%fused_computation.323.clone.1 | convolution fusion | flops 82280192 | bytes 2651840 | tf_op jit(solution)/shard_map/while/body/eval_jaxpr/dot_general | solution.py:58
  267.6 24.3 %fusion.264 = (f32[256]{0:T(256)S(1)}, f32[256,1984]{0,1:T(8,128)}) fusion(f32[1984]{0:T(1024)S(1)} %mul.550, bf16[8,1984,64]{2,1,0:T(8,128)(2,1)} %get-tuple-element.875, s32[]{:T(128)} %get-tuple-element.850, bf16[8,256,64]{2,1,0:T(8,128)(2,1)} %get-tuple-element.873, s32[1984]{0:T(1024)} %get-tuple-element.885, s32[1984]{0:T(1024)} %get-tuple-element.883, ...), kind=kOutput, calls=%fused_computation.323.clone.1 | convolution fusion | flops 82280192 | bytes 2651840 | tf_op jit(solution)/shard_map/while/body/eval_jaxpr/dot_general | solution.py:58
  301.5 24.3 %fusion.264 = (f32[256]{0:T(256)S(1)}, f32[256,1984]{0,1:T(8,128)}) fusion(f32[1984]{0:T(1024)S(1)} %mul.550, bf16[8,1984,64]{2,1,0:T(8,128)(2,1)} %get-tuple-element.875, s32[]{:T(128)} %get-tuple-element.850, bf16[8,256,64]{2,1,0:T(8,128)(2,1)} %get-tuple-element.873, s32[1984]{0:T(1024)} %get-tuple-element.885, s32[1984]{0:T(1024)} %get-tuple-element.883, ...), kind=kOutput, calls=%fused_computation.323.clone.1 | convolution fusion | flops 82280192 | bytes 2651840 | tf_op jit(solution)/shard_map/while/body/eval_jaxpr/dot_general | solution.py:58
  335.4 24.3 %fusion.264 = (f32[256]{0:T(256)S(1)}, f32[256,1984]{0,1:T(8,128)}) fusion(f32[1984]{0:T(1024)S(1)} %mul.550, bf16[8,1984,64]{2,1,0:T(8,128)(2,1)} %get-tuple-element.875, s32[]{:T(128)} %get-tuple-element.850, bf16[8,256,64]{2,1,0:T(8,128)(2,1)} %get-tuple-element.873, s32[1984]{0:T(1024)} %get-tuple-element.885, s32[1984]{0:T(1024)} %get-tuple-element.883, ...), kind=kOutput, calls=%fused_computation.323.clone.1 | convolution fusion | flops 82280192 | bytes 2651840 | tf_op jit(solution)/shard_map/while/body/eval_jaxpr/dot_general | solution.py:58
  382.9 332.0 %while.33 = (s32[]{:T(128)}, bf16[8,256,64]{1,2,0:T(8,128)(2,1)}, f32[8,16,48,64]{3,2,1,0:T(8,128)}, f32[8,16,48,64]{3,2,1,0:T(8,128)}, f32[8,1984,64]{1,2,0:T(8...) while((s32[]{:T(128)}, bf16[8,256,64]{1,2,0:T(8,128)(2,1)}, ...), condition=%wide.region_23.24_spmd.clone, body=%wide.region_20.23_spmd.clone.sunk | while | flops 353558528 | bytes 20505996 | solution.py:314
  390.6 23.9 %multiply_reduce_fusion.8 = (f32[256]{0:T(256)S(1)}, f32[256,1984]{0,1:T(8,128)S(1)}) fusion(f32[256,1984]{0,1:T(8,128)S(1)} %fusion.286, f32[256]{0:T(256)S(1)} %bitcast.379, f32[1984]{0:T(1024)S(1)} %mul.558, bf16[8,1984,64]{2,1,0:T(8,128)(2,1)} %get-tuple-element.948, s32[]{:T(128)} %get-tuple-element.912, ...), kind=kOutput, calls=%fused_computation.74.clone.1 | convolution fusion | flops 83296000 | bytes 4684480 | tf_op jit(solution)/shard_map/while/body/eval_jaxpr/dot_general | solution.py:58
  432.1 23.9 %multiply_reduce_fusion.8 = (f32[256]{0:T(256)S(1)}, f32[256,1984]{0,1:T(8,128)S(1)}) fusion(f32[256,1984]{0,1:T(8,128)S(1)} %fusion.286, f32[256]{0:T(256)S(1)} %bitcast.379, f32[1984]{0:T(1024)S(1)} %mul.558, bf16[8,1984,64]{2,1,0:T(8,128)(2,1)} %get-tuple-element.948, s32[]{:T(128)} %get-tuple-element.912, ...), kind=kOutput, calls=%fused_computation.74.clone.1 | convolution fusion | flops 83296000 | bytes 4684480 | tf_op jit(solution)/shard_map/while/body/eval_jaxpr/dot_general | solution.py:58
  473.6 23.9 %multiply_reduce_fusion.8 = (f32[256]{0:T(256)S(1)}, f32[256,1984]{0,1:T(8,128)S(1)}) fusion(f32[256,1984]{0,1:T(8,128)S(1)} %fusion.286, f32[256]{0:T(256)S(1)} %bitcast.379, f32[1984]{0:T(1024)S(1)} %mul.558, bf16[8,1984,64]{2,1,0:T(8,128)(2,1)} %get-tuple-element.948, s32[]{:T(128)} %get-tuple-element.912, ...), kind=kOutput, calls=%fused_computation.74.clone.1 | convolution fusion | flops 83296000 | bytes 4684480 | tf_op jit(solution)/shard_map/while/body/eval_jaxpr/dot_general | solution.py:58
  515.0 23.9 %multiply_reduce_fusion.8 = (f32[256]{0:T(256)S(1)}, f32[256,1984]{0,1:T(8,128)S(1)}) fusion(f32[256,1984]{0,1:T(8,128)S(1)} %fusion.286, f32[256]{0:T(256)S(1)} %bitcast.379, f32[1984]{0:T(1024)S(1)} %mul.558, bf16[8,1984,64]{2,1,0:T(8,128)(2,1)} %get-tuple-element.948, s32[]{:T(128)} %get-tuple-element.912, ...), kind=kOutput, calls=%fused_computation.74.clone.1 | convolution fusion | flops 83296000 | bytes 4684480 | tf_op jit(solution)/shard_map/while/body/eval_jaxpr/dot_general | solution.py:58
  556.5 23.9 %multiply_reduce_fusion.8 = (f32[256]{0:T(256)S(1)}, f32[256,1984]{0,1:T(8,128)S(1)}) fusion(f32[256,1984]{0,1:T(8,128)S(1)} %fusion.286, f32[256]{0:T(256)S(1)} %bitcast.379, f32[1984]{0:T(1024)S(1)} %mul.558, bf16[8,1984,64]{2,1,0:T(8,128)(2,1)} %get-tuple-element.948, s32[]{:T(128)} %get-tuple-element.912, ...), kind=kOutput, calls=%fused_computation.74.clone.1 | convolution fusion | flops 83296000 | bytes 4684480 | tf_op jit(solution)/shard_map/while/body/eval_jaxpr/dot_general | solution.py:58
  598.0 23.9 %multiply_reduce_fusion.8 = (f32[256]{0:T(256)S(1)}, f32[256,1984]{0,1:T(8,128)S(1)}) fusion(f32[256,1984]{0,1:T(8,128)S(1)} %fusion.286, f32[256]{0:T(256)S(1)} %bitcast.379, f32[1984]{0:T(1024)S(1)} %mul.558, bf16[8,1984,64]{2,1,0:T(8,128)(2,1)} %get-tuple-element.948, s32[]{:T(128)} %get-tuple-element.912, ...), kind=kOutput, calls=%fused_computation.74.clone.1 | convolution fusion | flops 83296000 | bytes 4684480 | tf_op jit(solution)/shard_map/while/body/eval_jaxpr/dot_general | solution.py:58
  639.6 23.9 %multiply_reduce_fusion.8 = (f32[256]{0:T(256)S(1)}, f32[256,1984]{0,1:T(8,128)S(1)}) fusion(f32[256,1984]{0,1:T(8,128)S(1)} %fusion.286, f32[256]{0:T(256)S(1)} %bitcast.379, f32[1984]{0:T(1024)S(1)} %mul.558, bf16[8,1984,64]{2,1,0:T(8,128)(2,1)} %get-tuple-element.948, s32[]{:T(128)} %get-tuple-element.912, ...), kind=kOutput, calls=%fused_computation.74.clone.1 | convolution fusion | flops 83296000 | bytes 4684480 | tf_op jit(solution)/shard_map/while/body/eval_jaxpr/dot_general | solution.py:58
  681.0 23.9 %multiply_reduce_fusion.8 = (f32[256]{0:T(256)S(1)}, f32[256,1984]{0,1:T(8,128)S(1)}) fusion(f32[256,1984]{0,1:T(8,128)S(1)} %fusion.286, f32[256]{0:T(256)S(1)} %bitcast.379, f32[1984]{0:T(1024)S(1)} %mul.558, bf16[8,1984,64]{2,1,0:T(8,128)(2,1)} %get-tuple-element.948, s32[]{:T(128)} %get-tuple-element.912, ...), kind=kOutput, calls=%fused_computation.74.clone.1 | convolution fusion | flops 83296000 | bytes 4684480 | tf_op jit(solution)/shard_map/while/body/eval_jaxpr/dot_general | solution.py:58
  727.7 7.2 pad_maximum_fusion
  734.9 8.7 copy.129
  777.8 36.3 %reduce-scatter.2.cloned.1.call-done = f32[1,248,1024]{2,1,0:T(8,128)} async-done(((f32[8,248,1024]{2,1,0:T(8,128)}), f32[1,248,1024]{2,1,0:T(8,128)}) %reduce-scatter.2.cloned.1.call-update) | async-done | bytes 1015824 | tf_op jit(solution)/shard_map/reduce_scatter | solution.py:352
  838.3 41.4 %all-reduce.5 = (f32[512]{0:T(512)}, f32[512]{0:T(512)}, f32[512]{0:T(512)}, f32[2048]{0:T(1024)}, f32[512]{0:T(512)}, /*index=5*/f32[512]{0:T(512)}, f32[512]{0:T(512)}, f32[512]{0:T(512)}, f32[512]{0:T(512)}) all-reduce(f32[512]{0:T(512)S(1)} %reduce_sum.334, ...), channel_id=1, replica_groups=mesh['batch'=4,'seq'=8] {'batch','seq'}, use_global_device_ids=true, to_apply=%region_34.35 | all-reduce | flops 6144 | bytes 49152 | tf_op jit(solution)/shard_map/psum | solution.py:369
  879.7 188.7 %all-reduce.9.cloned.1.call-done = (f32[512,512]{1,0:T(8,128)}, f32[512,512]{1,0:T(8,128)}, f32[512,512]{1,0:T(8,128)}, f32[512,512]{1,0:T(8,128)}, f32[512,2048]{1,0:T(8,128)}, /*index=5*/f32[2048,512]{1,0:T(8,128)}) async-done(((f32[512,512]{1,0:T(8,128)}, f32[512,512]{1,0:T(8,128)}, f32[512,512]{1,0:T(8,128)}, f32[512,512]{1,0:T(8,128)}, f32[512,2048]{1,0:T(8,128)}, /*index=5*/f32[2048,512]{1,0:T(8,128)}), ...) | async-done | bytes 12582928 | tf_op jit(solution)/shard_map/psum | solution.py:369
  (619 shorter events, 392.0 us)
Async XLA Ops:
  7.2 362.6 %copy-start = (bf16[512,2048]{1,0:T(8,128)(2,1)S(1)}, bf16[512,2048]{1,0:T(8,128)(2,1)}, u32[]{:S(2)}) copy-start(bf16[512,2048]{1,0:T(8,128)(2,1)} %param.36) | copy-start | bytes 6291460
  7.2 69.3 %all-gather.2.cloned.1.call-start = ((), (), s32[]{:S(2)}) async-start(), calls=%async_computation.1 | async-start | bytes 4571136 | tf_op jit(solution)/shard_map/all_gather | solution.py:173
  8.5 32.8 %copy-start.36 = (f32[256]{0:T(256)}, f32[256]{0:T(256)S(1)}, u32[]{:S(2)}) copy-start(f32[256]{0:T(256)S(1)} %broadcast_multiply_fusion.1) | copy-start | bytes 3076
  10.2 31.1 %copy-start.39 = (f32[256]{0:T(256)}, f32[256]{0:T(256)S(1)}, u32[]{:S(2)}) copy-start(f32[256]{0:T(256)S(1)} %fusion.168) | copy-start | bytes 3076
  13.3 6.2 collective-permute-start
  15.6 5.2 collective-permute-start.1
  25.0 8.3 copy-start.31
  28.3 12.9 %copy-start.2 = (bf16[1,256,512]{2,1,0:T(8,128)(2,1)S(1)}, bf16[1,256,512]{2,1,0:T(8,128)(2,1)}, u32[]{:S(2)}) copy-start(bf16[1,256,512]{2,1,0:T(8,128)(2,1)} %param.22) | copy-start | bytes 786436
  28.3 13.0 %copy-start.34 = (f32[512]{0:T(512)S(1)}, f32[512]{0:T(512)}, u32[]{:S(2)}) copy-start(f32[512]{0:T(512)} %param.25) | copy-start | bytes 6148
  28.3 13.0 %copy-start.45 = (f32[512]{0:T(512)S(1)}, f32[512]{0:T(512)}, u32[]{:S(2)}) copy-start(f32[512]{0:T(512)} %param.26) | copy-start | bytes 6148
  31.5 20.5 %copy-start.22 = (bf16[256,1024]{1,0:T(8,128)(2,1)S(1)}, bf16[256,1024]{1,0:T(8,128)(2,1)}, u32[]{:S(2)}) copy-start(bf16[256,1024]{1,0:T(8,128)(2,1)} %get-tuple-element.554) | copy-start | bytes 1572868
  31.5 20.5 %copy-start.23 = (bf16[256,1024]{1,0:T(8,128)(2,1)S(1)}, bf16[256,1024]{1,0:T(8,128)(2,1)}, u32[]{:S(2)}) copy-start(bf16[256,1024]{1,0:T(8,128)(2,1)} %get-tuple-element.555) | copy-start | bytes 1572868
  36.7 777.4 %reduce-scatter.2.cloned.1.call-start = ((), (), s32[]{:S(2)}) async-start(), calls=%async_computation.2 | async-start | bytes 9142272 | tf_op jit(solution)/shard_map/reduce_scatter | solution.py:352
  98.1 271.0 %copy-start.21 = (bf16[512,512]{1,0:T(8,128)(2,1)S(1)}, bf16[512,512]{1,0:T(8,128)(2,1)}, u32[]{:S(2)}) copy-start(bf16[512,512]{1,0:T(8,128)(2,1)} %param.32) | copy-start | bytes 1572868
  98.1 271.0 %copy-start.56 = (f32[512]{0:T(512)S(1)}, f32[512]{0:T(512)}, u32[]{:S(2)}) copy-start(f32[512]{0:T(512)} %param.33) | copy-start | bytes 6148
  369.1 7.3 copy-start.19
  369.6 10.3 copy-start.4
  369.6 10.3 copy-start.43
  370.0 10.0 copy-start.48
  743.6 324.8 %all-reduce.9.cloned.1.call-start = ((), (), s32[]{:S(2)}) async-start(), calls=%async_computation.3 | async-start | bytes 25165824 | tf_op jit(solution)/shard_map/psum | solution.py:369
  764.4 7.7 copy-start.13
  764.4 7.6 copy-start.16
  765.0 60.9 %collective-permute-start.2 = (bf16[16,1024]{1,0:T(8,128)(2,1)}, bf16[16,1024]{1,0:T(8,128)(2,1)}, u32[]{:S(2)}, u32[]{:S(2)}) collective-permute-start(bf16[16,1024]{1,0:T(8,128)(2,1)} %get-tuple-element.551), channel_id=1, source_target_pairs={{0,1},{1,2},{2,3},{3,4},{4,5},{5,6},{6,7},{8,9},{9,10},{10,11},{11... | collective-permute-start | bytes 98312 | tf_op jit(solution)/shard_map/ppermute | solution.py:33
  767.7 58.2 %collective-permute-start.3 = (bf16[16,1024]{1,0:T(8,128)(2,1)}, bf16[16,1024]{1,0:T(8,128)(2,1)}, u32[]{:S(2)}, u32[]{:S(2)}) collective-permute-start(bf16[16,1024]{1,0:T(8,128)(2,1)} %get-tuple-element.552), channel_id=1, source_target_pairs={{1,0},{2,1},{3,2},{4,3},{5,4},{6,5},{7,6},{9,8},{10,9},{11,10},{12... | collective-permute-start | bytes 98312 | tf_op jit(solution)/shard_map/ppermute | solution.py:33
  (45 other events, 142.7 us)
Sparse Core Ops, SparseCore 0:
  36.8 39.6 all-gather.1
  743.7 70.3 reduce-scatter.1
  830.9 237.3 all-reduce.8
where the time goes:
time: 1100 us; the launch traced here: 1090 us
  matrix products  556 us (51%)
  waiting for transfers between devices  238 us (22%)
  local copies, waits for them, and re-layouts  159 us (14%)
  other arithmetic  68.3 us (6%)
  blocking collectives  41.4 us (4%)
  between operations  14.8 us (1%)
    dot_general x30, matrix products, right_product(): lax.dot_general(left, right, (((1,), (1,)), ((), ())), preferred_element_...  402 us
    psum x1, waiting for transfers between devices, on_device(): lax.psum((grad_query_w, grad_key_w, grad_value_w, grad_out_w, grad_up, gr...  189 us
    dot_general x22, matrix products, product(): return jnp.dot(left, right, preferred_element_type=jnp.float32)  47.6 us
    dot_general x22, matrix products, left_product(): lax.dot_general(left, right, (((0,), (0,)), ((), ())), preferred_element_...  43.7 us
    psum x1, blocking collectives, on_device(): lax.psum((grad_query_w, grad_key_w, grad_value_w, grad_out_w, grad_up, gr...  41.4 us
    reduce_scatter x1, waiting for transfers between devices, on_device(): lax.psum_scatter(grad_far, 'seq', scatter_dimension=0, tiled=True)  36.3 us
    unnamed x136, local copies, waits for them, and re-layouts  33 us
  transfers between devices with their start and end apart: 7, of which 4 were waited for; matrix products, arithmetic and copies ran while one was open for 7% of the time, Pallas kernels for 0%

commit v1 on v0

v1 whole, which is shorter than its diff:
```python
import functools
import math

import jax
import jax.numpy as jnp
import numpy as np
from jax import lax
from jax.experimental import pallas as pl
from jax.experimental.pallas import tpu as pltpu
from jax.sharding import PartitionSpec as P

HEADS = 8
BLOCK = 16
UNIT = 1024
ROWS = 256
SUB = 64
QUAD = 4
HALO = 112
LOCAL = 3
GATHER = 32
NEAR_COLS = 256
PIECES = 32
SMALL = 16

NORM_EPS = 1e-05
LOG_TWO = math.log(2.0)
NEVER = -1e30
F32 = jnp.float32
BF16 = jnp.bfloat16
VMEM_LIMIT = 56 * 1024 * 1024


def dot(left, right):
    return jnp.dot(left, right, preferred_element_type=F32)


def dot_rows(left, right):
    return lax.dot_general(left, right, (((0,), (0,)), ((), ())), preferred_element_type=F32)


def dot_cols(left, right):
    return lax.dot_general(left, right, (((1,), (1,)), ((), ())), preferred_element_type=F32)


def two_parts(values):
    high = values.astype(BF16)
    return high, (values - high.astype(F32)).astype(BF16)


def normalize(values):
    centred = values - jnp.mean(values, axis=-1, keepdims=True)
    spread = jnp.mean(centred * centred, axis=-1, keepdims=True)
    scale = lax.rsqrt(spread + NORM_EPS)
    return centred * scale, scale


def norm_back(grad, normed, scale):
    return scale * (
        grad
        - jnp.mean(grad, axis=-1, keepdims=True)
        - normed * jnp.mean(grad * normed, axis=-1, keepdims=True)
    )


def normal_parts(upper):
    far = jnp.abs(upper) * math.sqrt(0.5)
    t = 1.0 / (1.0 + 0.5 * far)
    series = (
        -1.26551223,
        1.00002368,
        0.37409196,
        0.09678418,
        -0.18628806,
        0.27886807,
        -1.13520398,
        1.48851587,
        -0.82215223,
        0.17087277,
    )
    power = jnp.full_like(t, series[-1])
    for term in series[-2::-1]:
        power = power * t + term
    square = far * far
    half_tail = 0.5 * t * jnp.exp(power - square)
    phi = jnp.exp(-square) * (1.0 / math.sqrt(2.0 * math.pi))
    return jnp.where(upper < 0.0, half_tail, 1.0 - half_tail), phi


def level_rows(level):
    return ROWS >> level


def pool_matrix(levels):
    matrix = np.zeros((ROWS, ROWS), np.float32)
    at = 0
    for level in range(1, levels + 1):
        size = 1 << level
        for row in range(level_rows(level)):
            matrix[at + row, row * size : (row + 1) * size] = 1.0 / size
        at += level_rows(level)
    return matrix


POOL_AT = {1: 0, 2: 128, 3: 192}
POOLED = 224
HALO_AT = {0: (0, 16), 1: (16, 32), 2: (48, 32), 3: (80, 32)}


def key_list(sub, levels):
    out = []

    def add(column, level, first, last):
        own = level_rows(level)
        base, width = HALO_AT[level]
        low = min(last, 0)
        if first < low:
            out.append((column, low - first, "halo", base + width + first, 1))
            column += low - first
            first = low
        mid = min(last, own)
        if first < mid:
            if level == 0:
                out.append((column, mid - first, "own", first, 0))
            else:
                out.append((column, mid - first, "pool", POOL_AT[level] + first, 0))
            column += mid - first
            first = mid
        if first < last:
            out.append((column, last - first, "halo", HALO + base + first - own, 2))

    start = SUB * sub
    add(0, 0, start - 16, start + SUB + 16)
    row = 32 * sub
    add(96, 1, row - 32, row)
    add(128, 1, row + 32, row + 64)
    row = 32 * (sub // 2)
    add(160, 2, row - 32, row - 16)
    third = row + 32 if sub % 2 == 0 else row - 16
    add(176, 2, third, third + 16)
    add(192, 2, row + 48, row + 64)
    add(208, 3, -32, -16)
    third = 32 if sub < 2 else -16
    add(224, 3, third, third + 16)
    add(240, 3, 48, 64)
    far = 48 * (levels - LOCAL)
    out.append((NEAR_COLS, far, "halo", 2 * HALO, 3))
    return out


def columns_of(levels):
    return -(-(NEAR_COLS + 48 * (levels - LOCAL)) // 128) * 128


def score_bias(levels):
    cols = columns_of(levels)
    bias = np.full((SUB, cols), NEVER, np.float32)
    block = np.arange(SUB) // BLOCK
    for col in range(96):
        bias[:, col] = np.where(np.abs(col // BLOCK - 1 - block) <= 1, 0.0, NEVER)
    bias[:, 96:160] = LOG_TWO
    bias[:32, 112:128] = NEVER
    bias[32:, 128:144] = NEVER
    bias[:, 160:208] = 2 * LOG_TWO
    bias[:, 208:256] = 3 * LOG_TWO
    for level in range(LOCAL + 1, levels + 1):
        at = NEAR_COLS + 48 * (level - LOCAL - 1)
        bias[:, at : at + 48] = level * LOG_TWO
    return bias


def column_codes(levels):
    codes = np.zeros((8, columns_of(levels)), np.int32)
    for sub in range(ROWS // SUB):
        for column, rows, _, _, code in key_list(sub, levels):
            if code == 3:
                codes[sub, column : column + rows] = 3 + np.arange(rows) // BLOCK
            else:
                codes[sub, column : column + rows] = code
    return codes


def gather_at(level):
    return sum(level_rows(other) for other in range(LOCAL + 1, level))


def item_bounds(starts, place):
    unit = place * ROWS // UNIT
    low = starts[0, unit]
    count = jnp.int32(0)
    for other in range(starts.shape[1]):
        count = count + jnp.where(starts[0, other] == low, 1, 0).astype(jnp.int32)
    return low, low + count * UNIT


def far_blocks(place, levels):
    out = []
    for level in range(LOCAL + 1, levels + 1):
        mine = place * ROWS // (BLOCK << level)
        parent = mine // 2
        odd = mine - 2 * parent
        third = jnp.where(odd == 1, 2 * parent - 1, 2 * parent + 2)
        out.append((level, (2 * parent - 2, third, 2 * parent + 3)))
    return out


def pick_matrix(place, levels, holders):
    rows = []
    column = lax.broadcasted_iota(jnp.int32, (48, holders * GATHER), 1)
    line = lax.broadcasted_iota(jnp.int32, (48, holders * GATHER), 0)
    for level, blocks in far_blocks(place, levels):
        part = line // BLOCK
        block = jnp.where(part == 0, blocks[0], jnp.where(part == 1, blocks[1], blocks[2]))
        row = block * BLOCK + (line - part * BLOCK)
        shift = 8 - level
        owner = lax.shift_right_arithmetic(row, jnp.int32(shift))
        inside = row - owner * (1 << shift)
        wanted = owner * GATHER + gather_at(level) + inside
        rows.append(jnp.where(column == wanted, 1.0, 0.0))
    return jnp.concatenate(rows, axis=0).astype(BF16)


def head_masks(quad_cols, rows):
    lane = lax.broadcasted_iota(jnp.int32, (rows, quad_cols), 1)
    width = quad_cols // QUAD
    return [(lane >= width * h) & (lane < width * (h + 1)) for h in range(QUAD)]


def stack_heads(block, masks):
    zero = jnp.zeros_like(block)
    return jnp.concatenate([jnp.where(mask, block, zero) for mask in masks], axis=0)


def unstack_heads(block, masks):
    total = None
    for h, mask in enumerate(masks):
        part = jnp.where(mask, block[SUB * h : SUB * (h + 1)], 0.0)
        total = part if total is None else total + part
    return total


def my_piece():
    return (
        (lax.axis_index("seq") % 2) * 16
        + ((lax.axis_index("seq") // 2) % 4) * 4
        + lax.axis_index("batch") % 4
    )


def first_kernel(tokens, gain, shift, pool, normed_out, next_out, prev_out, gather_out):
    normed, _ = normalize(tokens[0].astype(F32))
    normed_out[...] = (normed * gain[...] + shift[...]).astype(BF16)
    high, low = two_parts(normed)
    pooled = (dot(pool[...], high) + dot(pool[...], low)).astype(BF16)
    next_out[0:16] = high[ROWS - 16 :]
    prev_out[0:16] = high[:16]
    for level in range(1, LOCAL + 1):
        at, width = HALO_AT[level]
        base = POOL_AT[level]
        next_out[at : at + width] = pooled[base + level_rows(level) - width : base + level_rows(level)]
        prev_out[at : at + width] = pooled[base : base + width]
    gather_out[...] = pooled[POOLED:]


def project_kernel(
    normed, query_w, query_b, key_w, value_w, value_b, pool,
    query_out, key_out, value_out, key_pool, value_pool,
):
    rows = normed[...]
    query = (dot(rows, query_w[...]) + query_b[...]).astype(BF16)
    query_out[...] = query * jnp.asarray(0.125, BF16)
    key = dot(rows, key_w[...]).astype(BF16)
    value = (dot(rows, value_w[...]) + value_b[...]).astype(BF16)
    key_out[...] = key
    value_out[...] = value
    key_pool[...] = dot(pool[:POOLED], key).astype(BF16)
    value_pool[...] = dot(pool[:POOLED], value).astype(BF16)


def fill_keys(sub, levels, target, own, pool, halo):
    cols = columns_of(levels)
    used = NEAR_COLS + 48 * (levels - LOCAL)
    sources = {"own": own, "pool": pool, "halo": halo}
    for column, rows, source, row, _ in key_list(sub, levels):
        target[column : column + rows] = sources[source][row : row + rows]
    if cols > used:
        target[used:] = jnp.zeros((cols - used, target.shape[1]), BF16)


def middle_kernel(
    levels, holders,
    starts, tokens, cotangent, query, key, value, key_pool, value_pool, from_prev, from_next,
    window, gain, shift, key_w, value_w, value_b, out_w, out_b, gain2, shift2, up_w, up_b,
    down_w, down_b, bias_table, codes,
    output, attended_out, weights_out, halo_out, key_halo, value_halo, grad_mid_out, sums_out,
    key_cat, value_cat, attended, sums, small,
):
    width = tokens.shape[2]
    place = lax.axis_index("seq")
    low, high = item_bounds(starts, place)
    far = 48 * (levels - LOCAL)

    halo_out[0:HALO] = from_prev[...]
    halo_out[HALO : 2 * HALO] = from_next[...]
    halo_out[2 * HALO :] = dot(pick_matrix(place, levels, holders), window[...]).astype(BF16)
    scaled = (halo_out[...].astype(F32) * gain[...]).astype(BF16)
    shift_high, shift_low = two_parts(jnp.broadcast_to(shift[...], (16, width)))
    key_shift = (dot(shift_high, key_w[...]) + dot(shift_low, key_w[...]))[0:1]
    value_shift = (dot(shift_high, value_w[...]) + dot(shift_low, value_w[...]))[0:1]
    key_halo[...] = (dot(scaled, key_w[...]) + key_shift).astype(BF16)
    value_halo[...] = (dot(scaled, value_w[...]) + (value_shift + value_b[...])).astype(BF16)

    code = codes[...]
    allowed = [
        jnp.where(place * ROWS > low, 0.0, NEVER).astype(F32),
        jnp.where(place * ROWS + ROWS < high, 0.0, NEVER).astype(F32),
    ]
    for level, blocks in far_blocks(place, levels):
        span = BLOCK << level
        for block in blocks:
            inside = (block * span >= low) & (block * span + span <= high)
            allowed.append(jnp.where(inside, 0.0, NEVER).astype(F32))
    column_bias = jnp.zeros(code.shape, F32)
    for number, value_of in enumerate(allowed):
        column_bias = jnp.where(code == number + 1, value_of, column_bias)

    quad_cols = width * QUAD // HEADS
    masks = head_masks(quad_cols, SUB)
    for sub in range(ROWS // SUB):
        fill_keys(sub, levels, key_cat, key, key_pool, key_halo)
        fill_keys(sub, levels, value_cat, value, value_pool, value_halo)
        bias = bias_table[...] + column_bias[sub : sub + 1]
        bias = jnp.concatenate([bias] * QUAD, axis=0)
        for quad in range(HEADS // QUAD):
            lanes = slice(quad * quad_cols, (quad + 1) * quad_cols)
            stacked = stack_heads(query[SUB * sub : SUB * (sub + 1), lanes], masks)
            score = dot_cols(stacked, key_cat[:, lanes]) + bias
            score = jnp.exp(score - jnp.max(score, axis=1, keepdims=True))
            weight = score * (1.0 / jnp.sum(score, axis=1, keepdims=True))
            weight = weight.astype(BF16)
            weights_out[sub * (HEADS // QUAD) + quad] = weight
            mixed = unstack_heads(dot(weight, value_cat[:, lanes]), masks)
            attended[SUB * sub : SUB * (sub + 1), lanes] = mixed.astype(BF16)

    attended_out[...] = attended[...]
    mid = tokens[0].astype(F32) + dot(attended[...], out_w[...]) + out_b[...]
    normed, scale = normalize(mid)
    low_second = (normed * gain2[...] + shift2[...]).astype(BF16)
    cot = cotangent[0]
    hidden = up_w.shape[1]
    small[...] = jnp.zeros_like(small)

    def put(row, vector):
        for part in range(vector.shape[1] // 128):
            small[row + part : row + part + 1] = vector[:, 128 * part : 128 * (part + 1)]

    result = mid + down_b[...]
    grad_second = jnp.zeros((ROWS, width), F32)
    step = width
    for at in range(0, hidden, step):
        cols = slice(at, at + step)
        upper = dot(low_second, up_w[:, cols]) + up_b[:, cols]
        below, phi = normal_parts(upper)
        active = (upper * below).astype(BF16)
        result = result + dot(active, down_w[cols])
        grad_down = dot_rows(active, cot).astype(BF16)
        for piece in range(at // 64, (at + step) // 64):
            row = 64 * piece - at
            for part in range(width // 128):
                sums[piece, 64 * part : 64 * (part + 1)] = grad_down[
                    row : row + 64, 128 * part : 128 * (part + 1)
                ]
        grad_active = dot_cols(cot, down_w[cols])
        grad_upper = grad_active * (below + upper * phi)
        low_upper = grad_upper.astype(BF16)
        put(4 + at // 128, jnp.sum(low_upper.astype(F32), axis=0, keepdims=True))
        grad_up = dot_rows(low_second, low_upper).astype(BF16)
        for piece in range(PIECES):
            for part in range(step // 128):
                row = 256 + 16 * (at // 128 + part)
                sums[piece, row : row + 16] = grad_up[
                    16 * piece : 16 * (piece + 1), 128 * part : 128 * (part + 1)
                ]
        grad_second = grad_second + dot_cols(low_upper, up_w[:, cols])

    output[0] = result.astype(BF16)
    cot = cot.astype(F32)
    put(0, jnp.sum(cot, axis=0, keepdims=True))
    put(20, jnp.sum(grad_second * normed, axis=0, keepdims=True))
    put(24, jnp.sum(grad_second, axis=0, keepdims=True))
    grad_mid_out[...] = cot + norm_back(grad_second * gain2[...], normed, scale)
    spread_small(sums, 512, small)
    me = my_piece()
    for piece in range(PIECES):
        sums_out[jnp.bitwise_xor(me, piece)] = sums[piece]


def spread_small(sums, row, small):
    for piece in range(PIECES):
        if piece < 2:
            part = small[SMALL * piece : SMALL * (piece + 1)].astype(BF16)
        else:
            part = jnp.zeros((SMALL, 128), BF16)
        sums[piece, row : row + SMALL] = part


def back_kernel(
    levels, holders,
    tokens, normed_low, query, key, value, key_pool, value_pool, halo, key_halo, value_halo,
    weights, attended, grad_mid, gain, shift, query_w, key_w, value_w, out_w, pool,
    grad_normed_out, to_prev, to_next, to_owners, sums_out,
    key_cat, value_cat, grad_query, key_own, key_pooled, key_lent, value_own, value_pooled,
    value_lent, sums, small,
):
    width = tokens.shape[2]
    place = lax.axis_index("seq")
    far = 48 * (levels - LOCAL)
    branch = grad_mid[...].astype(BF16)
    grad_attended = dot_cols(branch, out_w[...]).astype(BF16)
    for ref in (key_own, key_pooled, key_lent, value_own, value_pooled, value_lent):
        ref[...] = jnp.zeros_like(ref)
    key_sums = {"own": key_own, "pool": key_pooled, "halo": key_lent}
    value_sums = {"own": value_own, "pool": value_pooled, "halo": value_lent}

    quad_cols = width * QUAD // HEADS
    masks = head_masks(quad_cols, SUB)
    for sub in range(ROWS // SUB):
        fill_keys(sub, levels, key_cat, key, key_pool, key_halo)
        fill_keys(sub, levels, value_cat, value, value_pool, value_halo)
        rows = slice(SUB * sub, SUB * (sub + 1))
        for quad in range(HEADS // QUAD):
            lanes = slice(quad * quad_cols, (quad + 1) * quad_cols)
            stacked = stack_heads(query[rows, lanes], masks)
            grads = stack_heads(grad_attended[rows, lanes], masks)
            weight = weights[sub * (HEADS // QUAD) + quad]
            prob = weight.astype(F32)
            dprob = dot_cols(grads, value_cat[:, lanes])
            delta = jnp.sum(prob * dprob, axis=1, keepdims=True)
            dscore = (prob * (dprob - delta)).astype(BF16)
            mixed = unstack_heads(dot(dscore, key_cat[:, lanes]), masks)
            grad_query[rows, lanes] = (mixed * 0.125).astype(BF16)
            grad_keys = dot_rows(dscore, stacked)
            grad_values = dot_rows(weight, grads)
            for column, count, source, row, _ in key_list(sub, levels):
                key_sums[source][row : row + count, lanes] += grad_keys[column : column + count]
                value_sums[source][row : row + count, lanes] += grad_values[
                    column : column + count
                ]

    low_query = grad_query[...]
    low_key = (key_own[...] + dot_rows(pool[:POOLED], key_pooled[...].astype(BF16))).astype(BF16)
    low_value = (value_own[...] + dot_rows(pool[:POOLED], value_pooled[...].astype(BF16))).astype(
        BF16
    )
    lent_key = key_lent[...].astype(BF16)
    lent_value = value_lent[...].astype(BF16)
    lent_normed = halo[...].astype(F32)
    lent_low = (lent_normed * gain[...] + shift[...]).astype(BF16)
    rows = normed_low[...]

    def pieces(base, grad):
        grad = grad.astype(BF16)
        for piece in range(PIECES):
            for part in range(width // 128):
                row = base + 16 * part
                sums[piece, row : row + 16] = grad[
                    16 * piece : 16 * (piece + 1), 128 * part : 128 * (part + 1)
                ]

    pieces(0, dot_rows(attended[...], branch))
    pieces(64, dot_rows(rows, low_query))
    pieces(128, dot_rows(rows, low_key) + dot_rows(lent_low, lent_key))
    pieces(192, dot_rows(rows, low_value) + dot_rows(lent_low, lent_value))

    small[...] = jnp.zeros_like(small)

    def put(row, vector):
        for part in range(vector.shape[1] // 128):
            small[row + part : row + part + 1] = vector[:, 128 * part : 128 * (part + 1)]

    def total(values):
        return jnp.sum(values.astype(F32), axis=0, keepdims=True)

    normed, _ = normalize(tokens[0].astype(F32))
    grad_normed = (
        dot_cols(low_query, query_w[...])
        + dot_cols(low_key, key_w[...])
        + dot_cols(low_value, value_w[...])
    )
    lent_grad = dot_cols(lent_key, key_w[...]) + dot_cols(lent_value, value_w[...])
    grad_normed_out[...] = grad_normed
    put(0, total(low_query))
    put(4, total(low_value) + total(lent_value))
    put(8, total(branch))
    put(12, total(grad_normed * normed) + total(lent_grad * lent_normed))
    put(16, total(grad_normed) + total(lent_grad))
    lent_grad = lent_grad.astype(BF16)
    to_prev[...] = lent_grad[:HALO]
    to_next[...] = lent_grad[HALO : 2 * HALO]
    to_owners[...] = dot_rows(pick_matrix(place, levels, holders), lent_grad[2 * HALO :]).astype(
        BF16
    )
    spread_small(sums, 256, small)
    me = my_piece()
    for piece in range(PIECES):
        sums_out[jnp.bitwise_xor(me, piece)] = sums[piece]


def last_kernel(
    tokens, gain, grad_mid, grad_normed, from_prev, from_next, from_users, pool, grad_tokens, pooled
):
    for level in range(1, LOCAL + 1):
        at, width = HALO_AT[level]
        base, own = POOL_AT[level], level_rows(level)
        pooled[base : base + own] = jnp.zeros((own, pooled.shape[1]), F32)
        pooled[base : base + width] += from_prev[at : at + width].astype(F32)
        pooled[base + own - width : base + own] += from_next[at : at + width].astype(F32)
    users = from_users[0].astype(F32)
    for other in range(1, from_users.shape[0]):
        users = users + from_users[other].astype(F32)
    pooled[POOLED:] = users
    high, low = two_parts(pooled[...])
    grad = grad_normed[...] + dot_rows(pool[...], high) + dot_rows(pool[...], low)
    first = from_prev[:16].astype(F32)
    last = from_next[:16].astype(F32)
    gap = jnp.zeros((ROWS - 32, first.shape[1]), F32)
    grad = grad + jnp.concatenate([first, gap, last], axis=0)
    normed, scale = normalize(tokens[0].astype(F32))
    grad_tokens[0] = grad_mid[...] + norm_back(grad * gain[...], normed, scale)


def collect_kernel(kind, *refs):
    blocks, refs = refs[:8], refs[8:]
    me = my_piece()
    if kind == 1:
        down, up, down_b, up_b, gain, shift, small = refs
        small_row = 512
    else:
        out, query, key, value, query_b, value_b, out_b, gain, shift, small = refs
        small_row = 256
    small[...] = jnp.zeros_like(small)
    for core in range(2):
        for quad in range(4):
            for depth in range(4):
                piece = jnp.bitwise_xor(me, core * 16 + quad * 4 + depth)
                block = blocks[core * 4 + quad]
                lines = pl.ds(pl.multiple_of(piece * 16, 16), 16)
                if kind == 1:
                    rows = pl.ds(pl.multiple_of(piece * 64, 64), 64)
                    for part in range(down.shape[1] // 128):
                        down[rows, 128 * part : 128 * (part + 1)] = block[
                            depth, 64 * part : 64 * (part + 1)
                        ].astype(F32)
                    for part in range(up.shape[1] // 128):
                        row = 256 + 16 * part
                        up[lines, 128 * part : 128 * (part + 1)] = block[
                            depth, row : row + 16
                        ].astype(F32)
                else:
                    for number, grad in enumerate((out, query, key, value)):
                        for part in range(grad.shape[1] // 128):
                            row = 64 * number + 16 * part
                            grad[lines, 128 * part : 128 * (part + 1)] = block[
                                depth, row : row + 16
                            ].astype(F32)

                @pl.when(piece < 2)
                def _(block=block, depth=depth, lines=lines):
                    small[lines] = block[depth, small_row : small_row + SMALL].astype(F32)

    if kind == 1:
        order = (down_b, up_b, gain, shift)
    else:
        order = (query_b, value_b, out_b, gain, shift)
    at = 0
    for ref in order:
        ref[...] = small[at : at + ref.shape[0]]
        at += ref.shape[0]


def call(kernel, inputs, outputs, scratch=(), smem=0, flops=0):
    space = [pltpu.SMEM] * smem + [pltpu.VMEM] * (len(inputs) - smem)
    size = sum(math.prod(s) * jnp.dtype(d).itemsize for s, d in outputs)
    size += sum(math.prod(a.shape) * a.dtype.itemsize for a in inputs)
    return pl.pallas_call(
        kernel,
        out_shape=[jax.ShapeDtypeStruct(s, d) for s, d in outputs],
        in_specs=[pl.BlockSpec(memory_space=s) for s in space],
        out_specs=[pl.BlockSpec(memory_space=pltpu.VMEM) for _ in outputs],
        scratch_shapes=[pltpu.VMEM(s, d) for s, d in scratch],
        compiler_params=pltpu.CompilerParams(vmem_limit_bytes=VMEM_LIMIT),
        cost_estimate=pl.CostEstimate(flops=flops, bytes_accessed=size, transcendentals=0),
    )(*inputs)


def swap(array, axis, distance):
    count = lax.axis_size(axis)
    return lax.ppermute(array, axis, [(i, i ^ distance) for i in range(count)])


def shifted(array, axis, by):
    count = lax.axis_size(axis)
    return lax.ppermute(array, axis, [(i, i + by) for i in range(count) if 0 <= i + by < count])


def add(*arrays):
    total = arrays[0].astype(F32)
    for array in arrays[1:]:
        total = total + array.astype(F32)
    return total.astype(BF16)


def sum_pieces(slots):
    rows = slots.shape[1]
    slots = slots.reshape(2, 4, 4, rows, 128)
    other = swap(slots[1], "seq", 1)
    parts = [add(slots[0, quad], other[quad]) for quad in range(4)]
    came = [swap(parts[quad], "seq", 2 * quad) for quad in range(1, 4)]
    depths = [add(*[part[depth] for part in [parts[0]] + came]) for depth in range(4)]
    came = [swap(depths[depth], "batch", depth) for depth in range(1, 4)]
    whole = add(depths[0], *came)
    distance = 8
    while distance < lax.axis_size("seq"):
        whole = add(whole, swap(whole, "seq", distance))
        distance *= 2
    column = jnp.stack([whole] + [swap(whole, "batch", depth) for depth in range(1, 4)])
    plane = [column] + [swap(column, "seq", 2 * quad) for quad in range(1, 4)]
    return plane + [swap(block, "seq", 1) for block in plane]


def on_device(
    tokens, cotangent, item_start, first_gain, first_shift, query_weight, query_bias, key_weight,
    value_weight, value_bias, out_weight, out_bias, second_gain, second_shift, up_weight, up_bias,
    down_weight, down_bias,
):
    width = tokens.shape[2]
    hidden = up_weight.shape[1]
    holders = lax.axis_size("seq")
    levels = (ROWS * holders // (4 * BLOCK)).bit_length() - 1
    far = 48 * (levels - LOCAL)
    lent = 2 * HALO + far
    cols = columns_of(levels)
    groups = (ROWS // SUB) * (HEADS // QUAD)
    pool = jnp.asarray(pool_matrix(levels), BF16)
    bias_table = jnp.asarray(score_bias(levels))
    codes = jnp.asarray(column_codes(levels))

    def row(vector):
        return vector.reshape(1, -1)

    gain, shift = row(first_gain), row(first_shift)
    normed_low, for_next, for_prev, for_all = call(
        first_kernel,
        (tokens, gain, shift, pool),
        [((ROWS, width), BF16), ((HALO, width), BF16), ((HALO, width), BF16)]
        + [((GATHER, width), BF16)],
        flops=4 * ROWS * ROWS * width,
    )
    from_prev = shifted(for_next, "seq", 1)
    from_next = shifted(for_prev, "seq", -1)
    window = lax.all_gather(for_all, "seq", axis=0, tiled=True)
    query, key, value, key_pool, value_pool = call(
        project_kernel,
        (normed_low, query_weight, row(query_bias), key_weight, value_weight, row(value_bias), pool),
        [((ROWS, width), BF16)] * 3 + [((POOLED, width), BF16)] * 2,
        flops=8 * ROWS * width * width,
    )
    (
        output, attended, weights, halo, key_halo, value_halo, grad_mid, sums,
    ) = call(
        functools.partial(middle_kernel, levels, holders),
        (
            item_start, tokens, cotangent, query, key, value, key_pool, value_pool, from_prev,
            from_next, window, gain, shift, key_weight, value_weight, row(value_bias), out_weight,
            row(out_bias), row(second_gain), row(second_shift), up_weight, row(up_bias),
            down_weight, row(down_bias), bias_table, codes,
        ),
        [
            ((1, ROWS, width), BF16),
            ((ROWS, width), BF16),
            ((groups, QUAD * SUB, cols), BF16),
            ((lent, width), BF16),
            ((lent, width), BF16),
            ((lent, width), BF16),
            ((ROWS, width), F32),
            ((PIECES, 512 + SMALL, 128), BF16),
        ],
        scratch=[
            ((cols, width), BF16),
            ((cols, width), BF16),
            ((ROWS, width), BF16),
            ((PIECES, 512 + SMALL, 128), BF16),
            ((2 * SMALL, 128), F32),
        ],
        smem=1,
        flops=12 * ROWS * width * hidden,
    )
    first_sums = sum_pieces(sums)
    grad_normed, to_prev, to_next, to_owners, sums = call(
        functools.partial(back_kernel, levels, holders),
        (
            tokens, normed_low, query, key, value, key_pool, value_pool, halo, key_halo,
            value_halo, weights, attended, grad_mid, gain, shift, query_weight, key_weight,
            value_weight, out_weight, pool,
        ),
        [
            ((ROWS, width), F32),
            ((HALO, width), BF16),
            ((HALO, width), BF16),
            ((holders * GATHER, width), BF16),
            ((PIECES, 256 + SMALL, 128), BF16),
        ],
        scratch=[
            ((cols, width), BF16),
            ((cols, width), BF16),
            ((ROWS, width), BF16),
            ((ROWS, width), F32),
            ((POOLED, width), F32),
            ((lent, width), F32),
            ((ROWS, width), F32),
            ((POOLED, width), F32),
            ((lent, width), F32),
            ((PIECES, 256 + SMALL, 128), BF16),
            ((2 * SMALL, 128), F32),
        ],
        flops=20 * ROWS * width * width,
    )
    second_sums = sum_pieces(sums)
    back_next = shifted(to_prev, "seq", -1)
    back_prev = shifted(to_next, "seq", 1)
    users = lax.all_to_all(
        to_owners.reshape(holders, GATHER, width), "seq", split_axis=0, concat_axis=0, tiled=True
    )
    (grad_tokens,) = call(
        last_kernel,
        (tokens, gain, grad_mid, grad_normed, back_prev, back_next, users, pool),
        [((1, ROWS, width), F32)],
        scratch=[((ROWS, width), F32)],
        flops=4 * ROWS * ROWS * width,
    )
    lines = width // 128
    small = ((lines, 128), F32)
    scratch = [((PIECES * SMALL, 128), F32)]
    down, up, down_b, up_b, gain2, shift2 = call(
        functools.partial(collect_kernel, 1),
        first_sums,
        [((hidden, width), F32), ((width, hidden), F32), small, ((hidden // 128, 128), F32)]
        + [small] * 2,
        scratch=scratch,
    )
    square = ((width, width), F32)
    out_w, query_w, key_w, value_w, query_b, value_b, out_b, gain1, shift1 = call(
        functools.partial(collect_kernel, 2),
        second_sums,
        [square] * 4 + [small] * 5,
        scratch=scratch,
    )
    vectors = [query_b, value_b, out_b, up_b, down_b, gain1, shift1, gain2, shift2]
    return (output, grad_tokens, query_w, key_w, value_w, out_w, up, down) + tuple(
        vector.reshape(-1) for vector in vectors
    )


def solution(mesh):
    cut = P("batch", "seq", None)
    in_specs = (cut, cut, P("batch", None)) + (P(),) * 15
    out_specs = (cut, cut) + (P(),) * 15
    return jax.shard_map(
        on_device, mesh=mesh, in_specs=in_specs, out_specs=out_specs, check_vma=False
    )
```

time: 1100 us -> 193 us (0.18); the launches traced: 1090 us -> 193 us
  matrix products: 556 us -> 0 us
  waiting for transfers between devices: 238 us -> 72.2 us
  local copies, waits for them, and re-layouts: 159 us -> 7.95 us
  other arithmetic: 68.3 us -> 1.5 us
  Pallas kernels: 0 us -> 44.4 us
  starting transfers between devices: 8.14 us -> 41.1 us
  blocking collectives: 41.4 us -> 24.5 us
  between operations: 14.8 us -> 1 us
    dot_general x130 -> x0, matrix products: 556 us -> none  [the longest x30 402 us: right_product(): lax.dot_general(left, right, (((1,), (1,)), ((), ())), preferred_element_...]
    psum x1 -> x0, waiting for transfers between devices: 189 us -> none  [on_device(): lax.psum((grad_query_w, grad_key_w, grad_value_w, grad_out_w, grad_up, gr...]
    ppermute x4 -> x38, waiting for transfers between devices: 1.4 us -> 72.2 us  [the longest x34 72.2 us: swap(): return lax.ppermute(array, axis, [(i, i ^ distance) for i in range(count)])]
    pallas_call x0 -> x7, Pallas kernels: none -> 44.4 us  [call(): pl.pallas_call(kernel, out_shape=[jax.ShapeDtypeStruct(s, d) for s, d in...]
    psum x1 -> x0, blocking collectives: 41.4 us -> none  [on_device(): lax.psum((grad_query_w, grad_key_w, grad_value_w, grad_out_w, grad_up, gr...]
    reduce_scatter x1 -> x0, waiting for transfers between devices: 36.3 us -> none  [on_device(): lax.psum_scatter(grad_far, 'seq', scatter_dimension=0, tiled=True)]
    dynamic_slice x48 -> x0, local copies, waits for them, and re-layouts: 35.7 us -> none  [the longest x32 20.7 us: on_device(): lax.map(head_forward, (head_query, head_key_band, head_value_band, head_f...]
    ppermute x4 -> x38, starting transfers between devices: 7.85 us -> 41.1 us  [the longest x34 34.8 us: swap(): return lax.ppermute(array, axis, [(i, i ^ distance) for i in range(count)])]
  transfers between devices with their start and end apart: 7 -> 38, of which waited for: 4 -> 17; matrix products, arithmetic and copies ran while one was open for 7% -> 2% of each run, Pallas kernels for 0% -> 11%
where the time goes in v1:
time: 193 us
  waiting for transfers between devices  72.2 us (37%)
  Pallas kernels  44.4 us (23%)
  starting transfers between devices  41.1 us (21%)
  blocking collectives  24.5 us (13%)
  local copies, waits for them, and re-layouts  7.95 us (4%)
    ppermute x34, waiting for transfers between devices, swap(): return lax.ppermute(array, axis, [(i, i ^ distance) for i in range(count)])  72.2 us
    pallas_call x7, Pallas kernels, call(): pl.pallas_call(kernel, out_shape=[jax.ShapeDtypeStruct(s, d) for s, d in...  44.4 us
    ppermute x34, starting transfers between devices, swap(): return lax.ppermute(array, axis, [(i, i ^ distance) for i in range(count)])  34.8 us
    all_gather x1, blocking collectives, on_device(): window = lax.all_gather(for_all, 'seq', axis=0, tiled=True)  14.5 us
    all_to_all x1, blocking collectives, on_device(): lax.all_to_all(to_owners.reshape(holders, GATHER, width), 'seq', split_ax...  9.99 us
    ppermute x4, starting transfers between devices, shifted(): lax.ppermute(array, axis, [(i, i + by) for i in range(count) if 0 <= i +...  6.34 us
    slice x2, local copies, waits for them, and re-layouts, sum_pieces(): other = swap(slots[1], 'seq', 1)  4.56 us
  transfers between devices with their start and end apart: 38, of which 17 were waited for; matrix products, arithmetic and copies ran while one was open for 2% of the time, Pallas kernels for 11%

profile of v1, /device:TPU:0, one launch (start us, length us, event | category | flops | bytes accessed | tf_op | source)
XLA Modules:
  0.0 192.7 jit_solution(12501046651502421323)
XLA Ops:
  6.7 3.0 %shard_map.333 = (bf16[256,512]{1,0:T(8,128)(2,1)}, bf16[256,512]{1,0:T(8,128)(2,1)}, bf16[256,512]{1,0:T(8,128)(2,1)}, bf16[224,512]{1,0:T(8,128)(2,1)}, bf16[224,512]{1,0:T(8,128)(2,1)}) custom-call(bf16[256,512]{1,0:T(8,128)(2,1)} %get-tuple-element.54.normed.normed_low, bf16[512,512]{1,0:T(8,128)(2,1)} %query_w.3, f32[1,512]{1,0:T(1,128)} %bitcast.156, ...), custom_call_target="tpu_custom_call" | custom-call | flops 536870912 | bytes 3215360 | tf_op jit(solution)/shard_map/pallas_call | solution.py:584
  9.7 14.5 %all_gather.3.window = bf16[256,512]{1,0:T(8,128)(2,1)} all-gather(bf16[32,512]{1,0:T(8,128)(2,1)S(1)} %copy-done.20), channel_id=1, replica_groups=mesh['batch'=4,'seq'=8] {'seq'}, dimensions={0}, use_global_device_ids=true | all-gather | bytes 294912 | tf_op jit(solution)/shard_map/all_gather | solution.py:660
  24.9 15.4 %shard_map.334 = (bf16[1,256,512]{2,1,0:T(8,128)(2,1)}, bf16[256,512]{1,0:T(8,128)(2,1)}, bf16[8,256,384]{2,1,0:T(8,128)(2,1)}, bf16[320,512]{1,0:T(8,128)(2,1)}...) custom-call(s32[1,2]{1,0:T(1,128)} %starts.1, ...), custom_call_target="tpu_custom_call" | custom-call | flops 3221225472 | bytes 16091144 | tf_op jit(solution)/shard_map/pallas_call | solution.py:584
  40.3 3.1 %slice.178 = bf16[16,528,128]{2,1,0:T(8,128)(2,1)} slice(bf16[32,528,128]{2,1,0:T(8,128)(2,1)} %get-tuple-element.79), slice={[16:32], [0:528], [0:128]} | slice | bytes 4325376 | tf_op jit(solution)/shard_map/slice | solution.py:615
  43.7 10.9 %shard_map.335 = (f32[256,512]{1,0:T(8,128)}, bf16[112,512]{1,0:T(8,128)(2,1)}, bf16[112,512]{1,0:T(8,128)(2,1)}, bf16[256,512]{1,0:T(8,128)(2,1)}, bf16[32,272,128]{2,1,0:T(8,128)(2,1)}) custom-call(bf16[1,256,512]{2,1,0:T(8,128)(2,1)} %tokens.7, bf16[256,512]{1,0:T(8,128)(2,1)} %get-tuple-element.54.normed.normed_low, ...), custom_call_target="tpu_custom_call" | custom-call | flops 1342177280 | bytes 10588160 | tf_op jit(solution)/shard_map/pallas_call | solution.py:584
  56.3 2.6 %collective-permute-done.4 = bf16[4,4,272,128]{3,2,1,0:T(8,128)(2,1)S(1)} collective-permute-done((bf16[4,4,272,128]{3,2,1,0:T(8,128)(2,1)S(1)}, bf16[4,4,272,128]{3,2,1,0:T(8,128)(2,1)S(1)}, u32[]{:S(2)}, u32[]{:S(2)}) %collective-permute-start.4) | collective-permute-done | bytes 1114144 | tf_op jit(solution)/shard_map/ppermute | solution.py:597
  65.5 4.2 %collective-permute-done.7 = bf16[4,272,128]{2,1,0:T(8,128)(2,1)S(1)} collective-permute-done((bf16[4,272,128]{2,1,0:T(8,128)(2,1)S(1)}, bf16[4,272,128]{2,1,0:T(8,128)(2,1)S(1)}, u32[]{:S(2)}, u32[]{:S(2)}) %collective-permute-start.7) | collective-permute-done | bytes 278560 | tf_op jit(solution)/shard_map/ppermute | solution.py:597
  70.3 5.4 %collective-permute-done.6 = bf16[4,272,128]{2,1,0:T(8,128)(2,1)S(1)} collective-permute-done((bf16[4,272,128]{2,1,0:T(8,128)(2,1)S(1)}, bf16[4,272,128]{2,1,0:T(8,128)(2,1)S(1)}, u32[]{:S(2)}, u32[]{:S(2)}) %collective-permute-start.6) | collective-permute-done | bytes 278560 | tf_op jit(solution)/shard_map/ppermute | solution.py:597
  80.3 3.2 %collective-permute-start.9 = (bf16[272,128]{1,0:T(8,128)(2,1)S(1)}, bf16[272,128]{1,0:T(8,128)(2,1)S(1)}, u32[]{:S(2)}, u32[]{:S(2)}) collective-permute-start(bf16[272,128]{1,0:T(8,128)(2,1)S(1)} %get-tuple-element.104), channel_id=1, source_target_pairs={{0,16},{8,24},{16,0},{24,8},{1,17},{9,25},{17,1},{25,9},{2,18},{10... | collective-permute-start | bytes 208904 | tf_op jit(solution)/shard_map/ppermute | solution.py:597
  83.8 2.9 %collective-permute-done.9 = bf16[272,128]{1,0:T(8,128)(2,1)S(1)} collective-permute-done((bf16[272,128]{1,0:T(8,128)(2,1)S(1)}, bf16[272,128]{1,0:T(8,128)(2,1)S(1)}, u32[]{:S(2)}, u32[]{:S(2)}) %collective-permute-start.9) | collective-permute-done | bytes 69664 | tf_op jit(solution)/shard_map/ppermute | solution.py:597
  86.8 3.2 %collective-permute-start.13 = (bf16[272,128]{1,0:T(8,128)(2,1)S(1)}, bf16[272,128]{1,0:T(8,128)(2,1)S(1)}, u32[]{:S(2)}, u32[]{:S(2)}) collective-permute-start(bf16[272,128]{1,0:T(8,128)(2,1)S(1)} %fusion.13), channel_id=1, source_target_pairs={{0,24},{8,16},{16,8},{24,0},{1,25},{9,17},{17,9},{25,1},{2,26},{10... | collective-permute-start | bytes 208904 | tf_op jit(solution)/shard_map/ppermute | solution.py:597
  91.2 6.8 %collective-permute-done.23 = bf16[4,528,128]{2,1,0:T(8,128)(2,1)S(1)} collective-permute-done((bf16[4,528,128]{2,1,0:T(8,128)(2,1)S(1)}, bf16[4,528,128]{2,1,0:T(8,128)(2,1)S(1)}, u32[]{:S(2)}, u32[]{:S(2)}) %collective-permute-start.23) | collective-permute-done | bytes 540704 | tf_op jit(solution)/shard_map/ppermute | solution.py:597
  103.9 6.0 %collective-permute-done.27 = bf16[528,128]{1,0:T(8,128)(2,1)S(1)} collective-permute-done((bf16[528,128]{1,0:T(8,128)(2,1)S(1)}, bf16[528,128]{1,0:T(8,128)(2,1)S(1)}, u32[]{:S(2)}, u32[]{:S(2)}) %collective-permute-start.27) | collective-permute-done | bytes 135200 | tf_op jit(solution)/shard_map/ppermute | solution.py:597
  109.8 4.9 %collective-permute-done.26 = bf16[528,128]{1,0:T(8,128)(2,1)S(1)} collective-permute-done((bf16[528,128]{1,0:T(8,128)(2,1)S(1)}, bf16[528,128]{1,0:T(8,128)(2,1)S(1)}, u32[]{:S(2)}, u32[]{:S(2)}) %collective-permute-start.26) | collective-permute-done | bytes 135200 | tf_op jit(solution)/shard_map/ppermute | solution.py:597
  114.8 2.7 %collective-permute-start.30 = (bf16[528,128]{1,0:T(8,128)(2,1)S(1)}, bf16[528,128]{1,0:T(8,128)(2,1)S(1)}, u32[]{:S(2)}, u32[]{:S(2)}) collective-permute-start(bf16[528,128]{1,0:T(8,128)(2,1)S(1)} %fusion.10), channel_id=1, source_target_pairs={{0,24},{8,16},{16,8},{24,0},{1,25},{9,17},{17,9},{25,1},{2,26},{10... | collective-permute-start | bytes 405512 | tf_op jit(solution)/shard_map/ppermute | solution.py:597
  120.6 2.6 %collective-permute-done.30 = bf16[528,128]{1,0:T(8,128)(2,1)S(1)} collective-permute-done((bf16[528,128]{1,0:T(8,128)(2,1)S(1)}, bf16[528,128]{1,0:T(8,128)(2,1)S(1)}, u32[]{:S(2)}, u32[]{:S(2)}) %collective-permute-start.30) | collective-permute-done | bytes 135200 | tf_op jit(solution)/shard_map/ppermute | solution.py:597
  124.5 3.3 %collective-permute-done.29 = bf16[528,128]{1,0:T(8,128)(2,1)S(1)} collective-permute-done((bf16[528,128]{1,0:T(8,128)(2,1)S(1)}, bf16[528,128]{1,0:T(8,128)(2,1)S(1)}, u32[]{:S(2)}, u32[]{:S(2)}) %collective-permute-start.29) | collective-permute-done | bytes 135200 | tf_op jit(solution)/shard_map/ppermute | solution.py:597
  133.6 4.8 %collective-permute-done.16.refs_3_ = bf16[4,272,128]{2,1,0:T(8,128)(2,1)S(1)} collective-permute-done((bf16[4,272,128]{2,1,0:T(8,128)(2,1)S(1)}, bf16[4,272,128]{2,1,0:T(8,128)(2,1)S(1)}, u32[]{:S(2)}, u32[]{:S(2)}) %collective-permute-start.16) | collective-permute-done | bytes 278560 | tf_op jit(solution)/shard_map/ppermute | solution.py:597
  139.0 15.6 %collective-permute-done.15.refs_2_ = bf16[4,272,128]{2,1,0:T(8,128)(2,1)S(1)} collective-permute-done((bf16[4,272,128]{2,1,0:T(8,128)(2,1)S(1)}, bf16[4,272,128]{2,1,0:T(8,128)(2,1)S(1)}, u32[]{:S(2)}, u32[]{:S(2)}) %collective-permute-start.15) | collective-permute-done | bytes 278560 | tf_op jit(solution)/shard_map/ppermute | solution.py:597
  154.7 10.6 %collective-permute-done.14.refs_1_ = bf16[4,272,128]{2,1,0:T(8,128)(2,1)S(1)} collective-permute-done((bf16[4,272,128]{2,1,0:T(8,128)(2,1)S(1)}, bf16[4,272,128]{2,1,0:T(8,128)(2,1)S(1)}, u32[]{:S(2)}, u32[]{:S(2)}) %collective-permute-start.14) | collective-permute-done | bytes 278560 | tf_op jit(solution)/shard_map/ppermute | solution.py:597
  167.0 10.0 %all_to_all.5.from_users = bf16[8,32,512]{2,1,0:T(8,128)(2,1)} all-to-all(bf16[8,32,512]{2,1,0:T(8,128)(2,1)S(1)} %bitcast.140), channel_id=1, replica_groups=mesh['batch'=4,'seq'=8] {'seq'}, dimensions={0} | all-to-all | bytes 524288 | tf_op jit(solution)/shard_map/all_to_all | solution.py:730
  177.0 2.7 %shard_map.336 = f32[1,256,512]{2,1,0:T(8,128)} custom-call(bf16[1,256,512]{2,1,0:T(8,128)(2,1)} %tokens.7, f32[1,512]{1,0:T(1,128)} %bitcast.150, f32[256,512]{1,0:T(8,128)} %get-tuple-element.64.grad_mid, f32[256,512]{1,0:T(8,128)} %get-tuple-element.70.grad_normed, bf16[112,512]{1,0:T(8,128)(2,1)} %copy-done.18, bf16[112,512]{1,0:T(8,128)(2,1)} %copy-done.19, ...), custom_call_target="tpu_custom_call" | custom-call | flops 134217728 | bytes 2459648 | tf_op jit(solution)/shard_map/pallas_call | solution.py:584
  180.6 3.9 %shard_map.337 = (f32[512,512]{1,0:T(8,128)}, f32[512,512]{1,0:T(8,128)}, f32[512,512]{1,0:T(8,128)}, f32[512,512]{1,0:T(8,128)}, f32[4,128]{1,0:T(4,128)}, /*in...) custom-call(bf16[4,272,128]{2,1,0:T(8,128)(2,1)} %copy-done.2, ...), custom_call_target="tpu_custom_call" | custom-call | bytes 6432768 | tf_op jit(solution)/shard_map/pallas_call | solution.py:584
  186.5 6.2 %shard_map.338 = (f32[2048,512]{1,0:T(8,128)}, f32[512,2048]{1,0:T(8,128)}, f32[4,128]{1,0:T(4,128)}, f32[16,128]{1,0:T(8,128)}, f32[4,128]{1,0:T(4,128)}, /*index=5*/f32[4,128]{1,0:T(4,128)}) custom-call(bf16[4,528,128]{2,1,0:T(8,128)(2,1)} %copy-done.1, bf16[4,528,128]{2,1,0:T(8,128)(2,1)} %copy-done.5, bf16[4,528,128]{2,1,0:T(8,128)(2,1)} %copy-done.4, ...), custom_call_target="tpu_custom_call" | custom-call | bytes 12728320 | tf_op jit(solution)/shard_map/pallas_call | solution.py:584
  (126 shorter events, 42.9 us)
Async XLA Ops:
  2.9 21.3 %collective-permute-start = (bf16[112,512]{1,0:T(8,128)(2,1)}, bf16[112,512]{1,0:T(8,128)(2,1)S(1)}, u32[]{:S(2)}, u32[]{:S(2)}) collective-permute-start(bf16[112,512]{1,0:T(8,128)(2,1)} %get-tuple-element.60), channel_id=1, source_target_pairs={{0,1},{1,2},{2,3},{3,4},{4,5},{5,6},{6,7},{8,9},{9,10},{10,11},{11... | collective-permute-start | bytes 344072 | tf_op jit(solution)/shard_map/ppermute | solution.py:602
  5.4 18.8 %collective-permute-start.1 = (bf16[112,512]{1,0:T(8,128)(2,1)}, bf16[112,512]{1,0:T(8,128)(2,1)S(1)}, u32[]{:S(2)}, u32[]{:S(2)}) collective-permute-start(bf16[112,512]{1,0:T(8,128)(2,1)} %get-tuple-element.61), channel_id=1, source_target_pairs={{1,0},{2,1},{3,2},{4,3},{5,4},{6,5},{7,6},{9,8},{10,9},{11,10},{12... | collective-permute-start | bytes 344072 | tf_op jit(solution)/shard_map/ppermute | solution.py:602
  43.4 19.4 %collective-permute-start.21 = (bf16[4,4,528,128]{3,2,1,0:T(8,128)(2,1)}, bf16[4,4,528,128]{3,2,1,0:T(8,128)(2,1)S(1)}, u32[]{:S(2)}, u32[]{:S(2)}) collective-permute-start(bf16[4,4,528,128]{3,2,1,0:T(8,128)(2,1)} %bitcast.30), channel_id=1, source_target_pairs={{0,1},{1,0},{2,3},{3,2},{4,5},{5,4},{6,7},{7,6},{8,9},{9,8},{10,11... | collective-permute-start | bytes 6488072 | tf_op jit(solution)/shard_map/ppermute | solution.py:597
  60.8 15.0 %collective-permute-start.6 = (bf16[4,272,128]{2,1,0:T(8,128)(2,1)S(1)}, bf16[4,272,128]{2,1,0:T(8,128)(2,1)S(1)}, u32[]{:S(2)}, u32[]{:S(2)}) collective-permute-start(bf16[4,272,128]{2,1,0:T(8,128)(2,1)S(1)} %get-tuple-element.97), channel_id=1, source_target_pairs={{0,4},{1,5},{2,6},{3,7},{4,0},{5,1},{6,2},{7,3},{8,12},{9,13},{10,... | collective-permute-start | bytes 835592 | tf_op jit(solution)/shard_map/ppermute | solution.py:597
  61.4 14.4 %collective-permute-start.5 = (bf16[4,272,128]{2,1,0:T(8,128)(2,1)S(1)}, bf16[4,272,128]{2,1,0:T(8,128)(2,1)S(1)}, u32[]{:S(2)}, u32[]{:S(2)}) collective-permute-start(bf16[4,272,128]{2,1,0:T(8,128)(2,1)S(1)} %get-tuple-element.98), channel_id=1, source_target_pairs={{0,2},{1,3},{2,0},{3,1},{4,6},{5,7},{6,4},{7,5},{8,10},{9,11},{10,... | collective-permute-start | bytes 835592 | tf_op jit(solution)/shard_map/ppermute | solution.py:597
  63.4 26.6 %collective-permute-start.24 = (bf16[4,528,128]{2,1,0:T(8,128)(2,1)S(1)}, bf16[4,528,128]{2,1,0:T(8,128)(2,1)S(1)}, u32[]{:S(2)}, u32[]{:S(2)}) collective-permute-start(bf16[4,528,128]{2,1,0:T(8,128)(2,1)S(1)} %get-tuple-element.92), channel_id=1, source_target_pairs={{0,6},{1,7},{2,4},{3,5},{4,2},{5,3},{6,0},{7,1},{8,14},{9,15},{10,... | collective-permute-start | bytes 1622024 | tf_op jit(solution)/shard_map/ppermute | solution.py:597
  64.9 33.1 %collective-permute-start.23 = (bf16[4,528,128]{2,1,0:T(8,128)(2,1)S(1)}, bf16[4,528,128]{2,1,0:T(8,128)(2,1)S(1)}, u32[]{:S(2)}, u32[]{:S(2)}) collective-permute-start(bf16[4,528,128]{2,1,0:T(8,128)(2,1)S(1)} %get-tuple-element.93), channel_id=1, source_target_pairs={{0,4},{1,5},{2,6},{3,7},{4,0},{5,1},{6,2},{7,3},{8,12},{9,13},{10,... | collective-permute-start | bytes 1622024 | tf_op jit(solution)/shard_map/ppermute | solution.py:597
  69.7 28.3 %collective-permute-start.22 = (bf16[4,528,128]{2,1,0:T(8,128)(2,1)S(1)}, bf16[4,528,128]{2,1,0:T(8,128)(2,1)S(1)}, u32[]{:S(2)}, u32[]{:S(2)}) collective-permute-start(bf16[4,528,128]{2,1,0:T(8,128)(2,1)S(1)} %get-tuple-element.94), channel_id=1, source_target_pairs={{0,2},{1,3},{2,0},{3,1},{4,6},{5,7},{6,4},{7,5},{8,10},{9,11},{10,... | collective-permute-start | bytes 1622024 | tf_op jit(solution)/shard_map/ppermute | solution.py:597
  86.8 15.6 %collective-permute-start.13 = (bf16[272,128]{1,0:T(8,128)(2,1)S(1)}, bf16[272,128]{1,0:T(8,128)(2,1)S(1)}, u32[]{:S(2)}, u32[]{:S(2)}) collective-permute-start(bf16[272,128]{1,0:T(8,128)(2,1)S(1)} %fusion.13), channel_id=1, source_target_pairs={{0,24},{8,16},{16,8},{24,0},{1,25},{9,17},{17,9},{25,1},{2,26},{10... | collective-permute-start | bytes 208904 | tf_op jit(solution)/shard_map/ppermute | solution.py:597
  89.9 12.6 %collective-permute-start.12 = (bf16[272,128]{1,0:T(8,128)(2,1)S(1)}, bf16[272,128]{1,0:T(8,128)(2,1)S(1)}, u32[]{:S(2)}, u32[]{:S(2)}) collective-permute-start(bf16[272,128]{1,0:T(8,128)(2,1)S(1)} %fusion.13), channel_id=1, source_target_pairs={{0,16},{8,24},{16,0},{24,8},{1,17},{9,25},{17,1},{25,9},{2,18},{10... | collective-permute-start | bytes 208904 | tf_op jit(solution)/shard_map/ppermute | solution.py:597
  90.0 12.6 %collective-permute-start.11 = (bf16[272,128]{1,0:T(8,128)(2,1)S(1)}, bf16[272,128]{1,0:T(8,128)(2,1)S(1)}, u32[]{:S(2)}, u32[]{:S(2)}) collective-permute-start(bf16[272,128]{1,0:T(8,128)(2,1)S(1)} %fusion.13), channel_id=1, source_target_pairs={{0,8},{8,0},{16,24},{24,16},{1,9},{9,1},{17,25},{25,17},{2,10},{10... | collective-permute-start | bytes 208904 | tf_op jit(solution)/shard_map/ppermute | solution.py:597
  102.4 12.3 %collective-permute-start.26 = (bf16[528,128]{1,0:T(8,128)(2,1)S(1)}, bf16[528,128]{1,0:T(8,128)(2,1)S(1)}, u32[]{:S(2)}, u32[]{:S(2)}) collective-permute-start(bf16[528,128]{1,0:T(8,128)(2,1)S(1)} %get-tuple-element.101), channel_id=1, source_target_pairs={{0,16},{8,24},{16,0},{24,8},{1,17},{9,25},{17,1},{25,9},{2,18},{10... | collective-permute-start | bytes 405512 | tf_op jit(solution)/shard_map/ppermute | solution.py:597
  102.6 30.4 %collective-permute-start.17 = (bf16[4,272,128]{2,1,0:T(8,128)(2,1)S(1)}, bf16[4,272,128]{2,1,0:T(8,128)(2,1)S(1)}, u32[]{:S(2)}, u32[]{:S(2)}) collective-permute-start(bf16[4,272,128]{2,1,0:T(8,128)(2,1)S(1)} %pad_maximum_fusion.1.refs_0_), channel_id=1, source_target_pairs={{0,1},{1,0},{2,3},{3,2},{4,5},{5,4},{6,7},{7,6},{8,9},{9,8},{10,11... | collective-permute-start | bytes 835592 | tf_op jit(solution)/shard_map/ppermute | solution.py:597
  117.6 11.8 %collective-permute-start.28 = (bf16[528,128]{1,0:T(8,128)(2,1)S(1)}, bf16[528,128]{1,0:T(8,128)(2,1)S(1)}, u32[]{:S(2)}, u32[]{:S(2)}) collective-permute-start(bf16[528,128]{1,0:T(8,128)(2,1)S(1)} %fusion.10), channel_id=1, source_target_pairs={{0,8},{8,0},{16,24},{24,16},{1,9},{9,1},{17,25},{25,17},{2,10},{10... | collective-permute-start | bytes 405512 | tf_op jit(solution)/shard_map/ppermute | solution.py:597
  129.3 25.3 %collective-permute-start.15 = (bf16[4,272,128]{2,1,0:T(8,128)(2,1)S(1)}, bf16[4,272,128]{2,1,0:T(8,128)(2,1)S(1)}, u32[]{:S(2)}, u32[]{:S(2)}) collective-permute-start(bf16[4,272,128]{2,1,0:T(8,128)(2,1)S(1)} %pad_maximum_fusion.1.refs_0_), channel_id=1, source_target_pairs={{0,4},{1,5},{2,6},{3,7},{4,0},{5,1},{6,2},{7,3},{8,12},{9,13},{10,... | collective-permute-start | bytes 835592 | tf_op jit(solution)/shard_map/ppermute | solution.py:597
  130.0 35.8 %collective-permute-start.33 = (bf16[4,528,128]{2,1,0:T(8,128)(2,1)S(1)}, bf16[4,528,128]{2,1,0:T(8,128)(2,1)S(1)}, u32[]{:S(2)}, u32[]{:S(2)}) collective-permute-start(bf16[4,528,128]{2,1,0:T(8,128)(2,1)S(1)} %pad_maximum_fusion.refs_0_), channel_id=1, source_target_pairs={{0,6},{1,7},{2,4},{3,5},{4,2},{5,3},{6,0},{7,1},{8,14},{9,15},{10,... | collective-permute-start | bytes 1622024 | tf_op jit(solution)/shard_map/ppermute | solution.py:597
  131.6 34.6 %collective-permute-start.32 = (bf16[4,528,128]{2,1,0:T(8,128)(2,1)S(1)}, bf16[4,528,128]{2,1,0:T(8,128)(2,1)S(1)}, u32[]{:S(2)}, u32[]{:S(2)}) collective-permute-start(bf16[4,528,128]{2,1,0:T(8,128)(2,1)S(1)} %pad_maximum_fusion.refs_0_), channel_id=1, source_target_pairs={{0,4},{1,5},{2,6},{3,7},{4,0},{5,1},{6,2},{7,3},{8,12},{9,13},{10,... | collective-permute-start | bytes 1622024 | tf_op jit(solution)/shard_map/ppermute | solution.py:597
  133.0 33.3 %collective-permute-start.31 = (bf16[4,528,128]{2,1,0:T(8,128)(2,1)S(1)}, bf16[4,528,128]{2,1,0:T(8,128)(2,1)S(1)}, u32[]{:S(2)}, u32[]{:S(2)}) collective-permute-start(bf16[4,528,128]{2,1,0:T(8,128)(2,1)S(1)} %pad_maximum_fusion.refs_0_), channel_id=1, source_target_pairs={{0,2},{1,3},{2,0},{3,1},{4,6},{5,7},{6,4},{7,5},{8,10},{9,11},{10,... | collective-permute-start | bytes 1622024 | tf_op jit(solution)/shard_map/ppermute | solution.py:597
  138.4 26.9 %collective-permute-start.14 = (bf16[4,272,128]{2,1,0:T(8,128)(2,1)S(1)}, bf16[4,272,128]{2,1,0:T(8,128)(2,1)S(1)}, u32[]{:S(2)}, u32[]{:S(2)}) collective-permute-start(bf16[4,272,128]{2,1,0:T(8,128)(2,1)S(1)} %pad_maximum_fusion.1.refs_0_), channel_id=1, source_target_pairs={{0,2},{1,3},{2,0},{3,1},{4,6},{5,7},{6,4},{7,5},{8,10},{9,11},{10,... | collective-permute-start | bytes 835592 | tf_op jit(solution)/shard_map/ppermute | solution.py:597
  165.3 19.2 %collective-permute-start.34 = (bf16[4,528,128]{2,1,0:T(8,128)(2,1)S(1)}, bf16[4,528,128]{2,1,0:T(8,128)(2,1)S(1)}, u32[]{:S(2)}, u32[]{:S(2)}) collective-permute-start(bf16[4,528,128]{2,1,0:T(8,128)(2,1)S(1)} %pad_maximum_fusion.refs_0_), channel_id=1, source_target_pairs={{0,1},{1,0},{2,3},{3,2},{4,5},{5,4},{6,7},{7,6},{8,9},{9,8},{10,11... | collective-permute-start | bytes 1622024 | tf_op jit(solution)/shard_map/ppermute | solution.py:597
  165.8 18.7 %collective-permute-start.37 = (bf16[4,528,128]{2,1,0:T(8,128)(2,1)S(1)}, bf16[4,528,128]{2,1,0:T(8,128)(2,1)S(1)}, u32[]{:S(2)}, u32[]{:S(2)}) collective-permute-start(bf16[4,528,128]{2,1,0:T(8,128)(2,1)S(1)} %collective-permute-done.33.refs_3_), channel_id=1, source_target_pairs={{0,1},{1,0},{2,3},{3,2},{4,5},{5,4},{6,7},{7,6},{8,9},{9,8},{10,11... | collective-permute-start | bytes 1622024 | tf_op jit(solution)/shard_map/ppermute | solution.py:597
  166.2 18.4 %collective-permute-start.36 = (bf16[4,528,128]{2,1,0:T(8,128)(2,1)S(1)}, bf16[4,528,128]{2,1,0:T(8,128)(2,1)S(1)}, u32[]{:S(2)}, u32[]{:S(2)}) collective-permute-start(bf16[4,528,128]{2,1,0:T(8,128)(2,1)S(1)} %collective-permute-done.32.refs_2_), channel_id=1, source_target_pairs={{0,1},{1,0},{2,3},{3,2},{4,5},{5,4},{6,7},{7,6},{8,9},{9,8},{10,11... | collective-permute-start | bytes 1622024 | tf_op jit(solution)/shard_map/ppermute | solution.py:597
  166.3 18.2 %collective-permute-start.35 = (bf16[4,528,128]{2,1,0:T(8,128)(2,1)S(1)}, bf16[4,528,128]{2,1,0:T(8,128)(2,1)S(1)}, u32[]{:S(2)}, u32[]{:S(2)}) collective-permute-start(bf16[4,528,128]{2,1,0:T(8,128)(2,1)S(1)} %collective-permute-done.31.refs_1_), channel_id=1, source_target_pairs={{0,1},{1,0},{2,3},{3,2},{4,5},{5,4},{6,7},{7,6},{8,9},{9,8},{10,11... | collective-permute-start | bytes 1622024 | tf_op jit(solution)/shard_map/ppermute | solution.py:597
  166.9 12.9 %collective-permute-start.18 = (bf16[4,272,128]{2,1,0:T(8,128)(2,1)S(1)}, bf16[4,272,128]{2,1,0:T(8,128)(2,1)S(1)}, u32[]{:S(2)}, u32[]{:S(2)}) collective-permute-start(bf16[4,272,128]{2,1,0:T(8,128)(2,1)S(1)} %collective-permute-done.14.refs_1_), channel_id=1, source_target_pairs={{0,1},{1,0},{2,3},{3,2},{4,5},{5,4},{6,7},{7,6},{8,9},{9,8},{10,11... | collective-permute-start | bytes 835592 | tf_op jit(solution)/shard_map/ppermute | solution.py:597
  (41 other events, 684.5 us)

commit v2 on v1

--- a/solution.py
+++ b/solution.py
@@ -27,7 +27,6 @@
 NEVER = -1e30
 F32 = jnp.float32
 BF16 = jnp.bfloat16
-VMEM_LIMIT = 56 * 1024 * 1024
 
 
 def dot(left, right):
@@ -90,15 +89,17 @@
     return ROWS >> level
 
 
-def pool_matrix(levels):
-    matrix = np.zeros((ROWS, ROWS), np.float32)
+def pool_matrix(levels, rows=ROWS):
+    line = lax.broadcasted_iota(jnp.int32, (rows, ROWS), 0)
+    token = lax.broadcasted_iota(jnp.int32, (rows, ROWS), 1)
+    matrix = jnp.zeros((rows, ROWS), F32)
     at = 0
     for level in range(1, levels + 1):
-        size = 1 << level
-        for row in range(level_rows(level)):
-            matrix[at + row, row * size : (row + 1) * size] = 1.0 / size
+        if at < rows:
+            mine = lax.shift_right_arithmetic(token, jnp.int32(level)) == line - at
+            matrix = jnp.where(mine, 1.0 / (1 << level), matrix)
         at += level_rows(level)
-    return matrix
+    return matrix.astype(BF16)
 
 
 POOL_AT = {1: 0, 2: 128, 3: 192}
@@ -192,6 +193,10 @@
     return low, low + count * UNIT
 
 
+def extra_rows(holders):
+    return GATHER if direct(holders) else 0
+
+
 def far_blocks(place, levels):
     out = []
     for level in range(LOCAL + 1, levels + 1):
@@ -201,6 +206,10 @@
         third = jnp.where(odd == 1, 2 * parent - 1, 2 * parent + 2)
         out.append((level, (2 * parent - 2, third, 2 * parent + 3)))
     return out
+
+
+def direct(holders):
+    return holders == 8
 
 
 def pick_matrix(place, levels, holders):
@@ -214,6 +223,8 @@
         shift = 8 - level
         owner = lax.shift_right_arithmetic(row, jnp.int32(shift))
         inside = row - owner * (1 << shift)
+        if direct(holders):
+            owner = jnp.where(owner < 0, -1, jnp.bitwise_xor(owner, place))
         wanted = owner * GATHER + gather_at(level) + inside
         rows.append(jnp.where(column == wanted, 1.0, 0.0))
     return jnp.concatenate(rows, axis=0).astype(BF16)
@@ -246,34 +257,50 @@
     )
 
 
-def first_kernel(tokens, gain, shift, pool, normed_out, next_out, prev_out, gather_out):
+def first_kernel(levels, tokens, inner, outer):
     normed, _ = normalize(tokens[0].astype(F32))
-    normed_out[...] = (normed * gain[...] + shift[...]).astype(BF16)
     high, low = two_parts(normed)
-    pooled = (dot(pool[...], high) + dot(pool[...], low)).astype(BF16)
-    next_out[0:16] = high[ROWS - 16 :]
-    prev_out[0:16] = high[:16]
+    pool = pool_matrix(levels)
+    pooled = (dot(pool, high) + dot(pool, low)).astype(BF16)
+    even = lax.axis_index("seq") % 2 == 0
+
+    def put(at, first, last):
+        rows = first.shape[0]
+        inner[at : at + rows] = jnp.where(even, last, first)
+        outer[at : at + rows] = jnp.where(even, first, last)
+
+    put(0, high[:16], high[ROWS - 16 :])
     for level in range(1, LOCAL + 1):
         at, width = HALO_AT[level]
-        base = POOL_AT[level]
-        next_out[at : at + width] = pooled[base + level_rows(level) - width : base + level_rows(level)]
-        prev_out[at : at + width] = pooled[base : base + width]
-    gather_out[...] = pooled[POOLED:]
+        base, own = POOL_AT[level], level_rows(level)
+        put(at, pooled[base : base + width], pooled[base + own - width : base + own])
+    inner[HALO:] = pooled[POOLED:]
 
 
 def project_kernel(
-    normed, query_w, query_b, key_w, value_w, value_b, pool,
-    query_out, key_out, value_out, key_pool, value_pool,
+    levels,
+    tokens, gain, shift, query_w, query_b, key_w, value_w, value_b, out_w, up_w, down_w, cotangent,
+    normed_out, query_out, key_out, value_out, key_pool, value_pool, out_copy, up_copy, down_copy,
+    cot_copy, sem,
 ):
-    rows = normed[...]
+    pairs = ((out_w, out_copy), (up_w, up_copy), (down_w, down_copy), (cotangent, cot_copy))
+    copies = [pltpu.make_async_copy(*pair, sem.at[n]) for n, pair in enumerate(pairs)]
+    for copy in copies:
+        copy.start()
+    normed, _ = normalize(tokens[0].astype(F32))
+    rows = (normed * gain[...] + shift[...]).astype(BF16)
+    normed_out[...] = rows
+    pool = pool_matrix(levels, POOLED)
     query = (dot(rows, query_w[...]) + query_b[...]).astype(BF16)
     query_out[...] = query * jnp.asarray(0.125, BF16)
     key = dot(rows, key_w[...]).astype(BF16)
+    key_out[...] = key
+    key_pool[...] = dot(pool, key).astype(BF16)
     value = (dot(rows, value_w[...]) + value_b[...]).astype(BF16)
-    key_out[...] = key
     value_out[...] = value
-    key_pool[...] = dot(pool[:POOLED], key).astype(BF16)
-    value_pool[...] = dot(pool[:POOLED], value).astype(BF16)
+    value_pool[...] = dot(pool, value).astype(BF16)
+    for copy in copies:
+        copy.wait()
 
 
 def fill_keys(sub, levels, target, own, pool, halo):
@@ -287,21 +314,27 @@
 
 
 def middle_kernel(
-    levels, holders,
-    starts, tokens, cotangent, query, key, value, key_pool, value_pool, from_prev, from_next,
-    window, gain, shift, key_w, value_w, value_b, out_w, out_b, gain2, shift2, up_w, up_b,
-    down_w, down_b, bias_table, codes,
-    output, attended_out, weights_out, halo_out, key_halo, value_halo, grad_mid_out, sums_out,
-    key_cat, value_cat, attended, sums, small,
+    levels, holders, parts,
+    starts, tokens, cotangent, query, key, value, key_pool, value_pool, inner, outer,
+    gain, shift, key_w, value_w, value_b, out_w, out_b, gain2, shift2, up_w, up_b,
+    down_w, down_b, bias_table, codes, *refs,
 ):
+    windows, refs = refs[:parts], refs[parts:]
+    (
+    output, attended_out, weights_out, halo_out, key_halo, value_halo, mid_out, grad_second_out,
+    late_out, keep, send,
+    key_cat, value_cat, attended, sums, small, sem,
+    ) = refs
     width = tokens.shape[2]
     place = lax.axis_index("seq")
     low, high = item_bounds(starts, place)
     far = 48 * (levels - LOCAL)
 
-    halo_out[0:HALO] = from_prev[...]
-    halo_out[HALO : 2 * HALO] = from_next[...]
-    halo_out[2 * HALO :] = dot(pick_matrix(place, levels, holders), window[...]).astype(BF16)
+    even = place % 2 == 0
+    halo_out[0:HALO] = jnp.where(even, outer[...], inner[0:HALO])
+    halo_out[HALO : 2 * HALO] = jnp.where(even, inner[0:HALO], outer[...])
+    window = jnp.concatenate([ref[...] for ref in windows], axis=0)
+    halo_out[2 * HALO :] = dot(pick_matrix(place, levels, holders), window).astype(BF16)
     scaled = (halo_out[...].astype(F32) * gain[...]).astype(BF16)
     shift_high, shift_low = two_parts(jnp.broadcast_to(shift[...], (16, width)))
     key_shift = (dot(shift_high, key_w[...]) + dot(shift_low, key_w[...]))[0:1]
@@ -366,7 +399,7 @@
         for piece in range(at // 64, (at + step) // 64):
             row = 64 * piece - at
             for part in range(width // 128):
-                sums[piece, 64 * part : 64 * (part + 1)] = grad_down[
+                sums[slot_of(piece), 64 * part : 64 * (part + 1)] = grad_down[
                     row : row + 64, 128 * part : 128 * (part + 1)
                 ]
         grad_active = dot_cols(cot, down_w[cols])
@@ -374,48 +407,92 @@
         low_upper = grad_upper.astype(BF16)
         put(4 + at // 128, jnp.sum(low_upper.astype(F32), axis=0, keepdims=True))
         grad_up = dot_rows(low_second, low_upper).astype(BF16)
-        for piece in range(PIECES):
-            for part in range(step // 128):
-                row = 256 + 16 * (at // 128 + part)
-                sums[piece, row : row + 16] = grad_up[
-                    16 * piece : 16 * (piece + 1), 128 * part : 128 * (part + 1)
-                ]
+        if at >= EARLY_UP:
+            late_out[:, at - EARLY_UP : at - EARLY_UP + step] = grad_up
+        else:
+            put_lines(sums, 256 + 16 * (at // 128), grad_up)
         grad_second = grad_second + dot_cols(low_upper, up_w[:, cols])
 
     output[0] = result.astype(BF16)
-    cot = cot.astype(F32)
-    put(0, jnp.sum(cot, axis=0, keepdims=True))
-    put(20, jnp.sum(grad_second * normed, axis=0, keepdims=True))
-    put(24, jnp.sum(grad_second, axis=0, keepdims=True))
-    grad_mid_out[...] = cot + norm_back(grad_second * gain2[...], normed, scale)
-    spread_small(sums, 512, small)
-    me = my_piece()
+    put(0, jnp.sum(cot.astype(F32), axis=0, keepdims=True))
+    mid_out[...] = mid
+    grad_second_out[...] = grad_second
+    put_small(sums, FIRST_ROWS - SMALL, small)
+    hand_out(sums, keep, send, sem)
+
+
+def branch_kernel(
+    cotangent, mid, grad_second, gain2, attended, out_w,
+    grad_mid_out, grad_attended, grad_out, vectors,
+):
+    normed, scale = normalize(mid[...])
+    grad = grad_second[...]
+    grad_mid = cotangent[0].astype(F32) + norm_back(grad * gain2[...], normed, scale)
+    grad_mid_out[...] = grad_mid
+    branch = grad_mid.astype(BF16)
+    grad_attended[...] = dot_cols(branch, out_w[...]).astype(BF16)
+    grad_out[...] = dot_rows(attended[...], branch).astype(BF16)
+    vectors[0:1] = jnp.sum(branch.astype(F32), axis=0, keepdims=True)
+    vectors[1:2] = jnp.sum(grad * normed, axis=0, keepdims=True)
+    vectors[2:3] = jnp.sum(grad, axis=0, keepdims=True)
+
+
+EARLY_UP = 1536
+FIRST_ROWS = 256 + 192 + SMALL
+SECOND_ROWS = 5 * 64 + SMALL
+FIRST_CUT, SECOND_CUT = 256, 176
+
+
+def slot_of(piece):
+    return (piece // 16) * 16 + jnp.bitwise_xor(my_piece() % 16, piece % 16)
+
+
+def put_lines(sums, base, grad):
     for piece in range(PIECES):
-        sums_out[jnp.bitwise_xor(me, piece)] = sums[piece]
-
-
-def spread_small(sums, row, small):
+        slot = slot_of(piece)
+        for part in range(grad.shape[1] // 128):
+            row = base + 16 * part
+            sums[slot, row : row + 16] = grad[
+                16 * piece : 16 * (piece + 1), 128 * part : 128 * (part + 1)
+            ]
+
+
+def put_small(sums, row, small):
     for piece in range(PIECES):
         if piece < 2:
             part = small[SMALL * piece : SMALL * (piece + 1)].astype(BF16)
         else:
             part = jnp.zeros((SMALL, 128), BF16)
-        sums[piece, row : row + SMALL] = part
+        sums[slot_of(piece), row : row + SMALL] = part
+
+
+def hand_out(sums, keep, send, sem):
+    mine = my_piece() // 16
+    half = PIECES // 2
+    copies = [
+        pltpu.make_async_copy(sums.at[pl.ds(mine * half, half)], keep, sem.at[0]),
+        pltpu.make_async_copy(sums.at[pl.ds((1 - mine) * half, half)], send, sem.at[1]),
+    ]
+    for copy in copies:
+        copy.start()
+    for copy in copies:
+        copy.wait()
 
 
 def back_kernel(
     levels, holders,
     tokens, normed_low, query, key, value, key_pool, value_pool, halo, key_halo, value_halo,
-    weights, attended, grad_mid, gain, shift, query_w, key_w, value_w, out_w, pool,
-    grad_normed_out, to_prev, to_next, to_owners, sums_out,
+    weights, grad_attended, grad_out, late, vectors, gain, shift, query_w, key_w, value_w,
+    grad_normed_out, inner, outer, keep, send, *refs,
+):
+    owners, refs = refs[:-12], refs[-12:]
+    (
     key_cat, value_cat, grad_query, key_own, key_pooled, key_lent, value_own, value_pooled,
-    value_lent, sums, small,
-):
+    value_lent, sums, small, sem,
+    ) = refs
     width = tokens.shape[2]
     place = lax.axis_index("seq")
     far = 48 * (levels - LOCAL)
-    branch = grad_mid[...].astype(BF16)
-    grad_attended = dot_cols(branch, out_w[...]).astype(BF16)
     for ref in (key_own, key_pooled, key_lent, value_own, value_pooled, value_lent):
         ref[...] = jnp.zeros_like(ref)
     key_sums = {"own": key_own, "pool": key_pooled, "halo": key_lent}
@@ -447,29 +524,22 @@
                 ]
 
     low_query = grad_query[...]
-    low_key = (key_own[...] + dot_rows(pool[:POOLED], key_pooled[...].astype(BF16))).astype(BF16)
-    low_value = (value_own[...] + dot_rows(pool[:POOLED], value_pooled[...].astype(BF16))).astype(
-        BF16
-    )
+    pool = pool_matrix(levels, POOLED)
+    low_key = (key_own[...] + dot_rows(pool, key_pooled[...].astype(BF16))).astype(BF16)
+    low_value = (value_own[...] + dot_rows(pool, value_pooled[...].astype(BF16))).astype(BF16)
     lent_key = key_lent[...].astype(BF16)
     lent_value = value_lent[...].astype(BF16)
     lent_normed = halo[...].astype(F32)
     lent_low = (lent_normed * gain[...] + shift[...]).astype(BF16)
     rows = normed_low[...]
 
-    def pieces(base, grad):
-        grad = grad.astype(BF16)
-        for piece in range(PIECES):
-            for part in range(width // 128):
-                row = base + 16 * part
-                sums[piece, row : row + 16] = grad[
-                    16 * piece : 16 * (piece + 1), 128 * part : 128 * (part + 1)
-                ]
-
-    pieces(0, dot_rows(attended[...], branch))
-    pieces(64, dot_rows(rows, low_query))
-    pieces(128, dot_rows(rows, low_key) + dot_rows(lent_low, lent_key))
-    pieces(192, dot_rows(rows, low_value) + dot_rows(lent_low, lent_value))
+    put_lines(sums, 0, late[...])
+    put_lines(sums, 64, grad_out[...])
+    put_lines(sums, 128, dot_rows(rows, low_query).astype(BF16))
+    grad_key = dot_rows(rows, low_key) + dot_rows(lent_low, lent_key)
+    put_lines(sums, 192, grad_key.astype(BF16))
+    grad_value = dot_rows(rows, low_value) + dot_rows(lent_low, lent_value)
+    put_lines(sums, 256, grad_value.astype(BF16))
 
     small[...] = jnp.zeros_like(small)
 
@@ -490,104 +560,162 @@
     grad_normed_out[...] = grad_normed
     put(0, total(low_query))
     put(4, total(low_value) + total(lent_value))
-    put(8, total(branch))
+    put(8, vectors[0:1])
+    put(20, vectors[1:2])
+    put(24, vectors[2:3])
     put(12, total(grad_normed * normed) + total(lent_grad * lent_normed))
     put(16, total(grad_normed) + total(lent_grad))
     lent_grad = lent_grad.astype(BF16)
-    to_prev[...] = lent_grad[:HALO]
-    to_next[...] = lent_grad[HALO : 2 * HALO]
-    to_owners[...] = dot_rows(pick_matrix(place, levels, holders), lent_grad[2 * HALO :]).astype(
-        BF16
-    )
-    spread_small(sums, 256, small)
-    me = my_piece()
-    for piece in range(PIECES):
-        sums_out[jnp.bitwise_xor(me, piece)] = sums[piece]
-
-
-def last_kernel(
-    tokens, gain, grad_mid, grad_normed, from_prev, from_next, from_users, pool, grad_tokens, pooled
-):
+    even = place % 2 == 0
+    inner[...] = jnp.where(even, lent_grad[HALO : 2 * HALO], lent_grad[:HALO])
+    outer[...] = jnp.where(even, lent_grad[:HALO], lent_grad[HALO : 2 * HALO])
+    pick = pick_matrix(place, levels, holders)
+    returned = dot_rows(pick, lent_grad[2 * HALO :]).astype(BF16)
+    if owners:
+        owners[0][...] = returned
+    else:
+        for plane in range(4):
+            for other in range(2):
+                core = (place + other) % 2
+                rows = returned[GATHER * (2 * plane + other) :][:GATHER]
+                for part in range(4):
+                    slot = core * 16 + plane * 4 + part
+                    sums[slot, SECOND_ROWS:] = rows[:, 128 * part : 128 * (part + 1)]
+    put_small(sums, SECOND_ROWS - SMALL, small)
+    hand_out(sums, keep, send, sem)
+
+
+def last_kernel(levels, tokens, gain, grad_mid, grad_normed, inner, outer, *refs):
+    from_users, (grad_tokens, pooled) = refs[:-2], refs[-2:]
+    even = lax.axis_index("seq") % 2 == 0
+    first = jnp.where(even, outer[...], inner[0:HALO]).astype(F32)
+    last = jnp.where(even, inner[0:HALO], outer[...]).astype(F32)
     for level in range(1, LOCAL + 1):
         at, width = HALO_AT[level]
         base, own = POOL_AT[level], level_rows(level)
         pooled[base : base + own] = jnp.zeros((own, pooled.shape[1]), F32)
-        pooled[base : base + width] += from_prev[at : at + width].astype(F32)
-        pooled[base + own - width : base + own] += from_next[at : at + width].astype(F32)
-    users = from_users[0].astype(F32)
-    for other in range(1, from_users.shape[0]):
-        users = users + from_users[other].astype(F32)
-    pooled[POOLED:] = users
+        pooled[base : base + width] += first[at : at + width]
+        pooled[base + own - width : base + own] += last[at : at + width]
+    if len(from_users) > 1:
+        pooled[POOLED:] = functools.reduce(jnp.add, [ref[...].astype(F32) for ref in from_users])
+    else:
+        for part in range(4):
+            pooled[POOLED:, 128 * part : 128 * (part + 1)] = from_users[0][part].astype(F32)
     high, low = two_parts(pooled[...])
-    grad = grad_normed[...] + dot_rows(pool[...], high) + dot_rows(pool[...], low)
-    first = from_prev[:16].astype(F32)
-    last = from_next[:16].astype(F32)
+    pool = pool_matrix(levels)
     gap = jnp.zeros((ROWS - 32, first.shape[1]), F32)
-    grad = grad + jnp.concatenate([first, gap, last], axis=0)
+    grad = grad_normed[...] + dot_rows(pool, high) + dot_rows(pool, low)
+    grad = grad + jnp.concatenate([first[:16], gap, last[:16]], axis=0)
     normed, scale = normalize(tokens[0].astype(F32))
     grad_tokens[0] = grad_mid[...] + norm_back(grad * gain[...], normed, scale)
 
 
 def collect_kernel(kind, *refs):
     blocks, refs = refs[:8], refs[8:]
+    small = refs[-1]
     me = my_piece()
     if kind == 1:
-        down, up, down_b, up_b, gain, shift, small = refs
-        small_row = 512
+        down, up, *order = refs[:-1]
+        lined = [(up, 256, 12)]
+        small_row = FIRST_ROWS - SMALL
     else:
-        out, query, key, value, query_b, value_b, out_b, gain, shift, small = refs
-        small_row = 256
-    small[...] = jnp.zeros_like(small)
+        whole_up, out, query, key, value, *order, up, sem = refs[1:-1]
+        lined = [(up, 0, 4), (out, 64, 4), (query, 128, 4), (key, 192, 4), (value, 256, 4)]
+        small_row = SECOND_ROWS - SMALL
     for core in range(2):
-        for quad in range(4):
+        for plane in range(4):
             for depth in range(4):
-                piece = jnp.bitwise_xor(me, core * 16 + quad * 4 + depth)
-                block = blocks[core * 4 + quad]
-                lines = pl.ds(pl.multiple_of(piece * 16, 16), 16)
+                piece = jnp.bitwise_xor(me, core * 16 + plane * 4 + depth)
+                block = blocks[core * 4 + plane]
                 if kind == 1:
                     rows = pl.ds(pl.multiple_of(piece * 64, 64), 64)
                     for part in range(down.shape[1] // 128):
                         down[rows, 128 * part : 128 * (part + 1)] = block[
                             depth, 64 * part : 64 * (part + 1)
                         ].astype(F32)
-                    for part in range(up.shape[1] // 128):
-                        row = 256 + 16 * part
-                        up[lines, 128 * part : 128 * (part + 1)] = block[
+                lines = pl.ds(pl.multiple_of(piece * 16, 16), 16)
+                for grad, base, parts in lined:
+                    for part in range(parts):
+                        row = base + 16 * part
+                        grad[lines, 128 * part : 128 * (part + 1)] = block[
                             depth, row : row + 16
                         ].astype(F32)
-                else:
-                    for number, grad in enumerate((out, query, key, value)):
-                        for part in range(grad.shape[1] // 128):
-                            row = 64 * number + 16 * part
-                            grad[lines, 128 * part : 128 * (part + 1)] = block[
-                                depth, row : row + 16
-                            ].astype(F32)
 
                 @pl.when(piece < 2)
                 def _(block=block, depth=depth, lines=lines):
                     small[lines] = block[depth, small_row : small_row + SMALL].astype(F32)
 
-    if kind == 1:
-        order = (down_b, up_b, gain, shift)
-    else:
-        order = (query_b, value_b, out_b, gain, shift)
+    if kind == 2:
+        late = whole_up.shape[1] - up.shape[1]
+        copy = pltpu.make_async_copy(up, whole_up.at[:, pl.ds(late, up.shape[1])], sem)
+        copy.start()
     at = 0
     for ref in order:
         ref[...] = small[at : at + ref.shape[0]]
         at += ref.shape[0]
-
-
-def call(kernel, inputs, outputs, scratch=(), smem=0, flops=0):
-    space = [pltpu.SMEM] * smem + [pltpu.VMEM] * (len(inputs) - smem)
+    if kind == 2:
+        copy.wait()
+
+
+class Fetched:
+    def __init__(self, ref, copy):
+        self.ref = ref
+        self.copy = copy
+        self.shape = ref.shape
+
+    def wait(self):
+        if self.copy is not None:
+            self.copy.wait()
+            self.copy = None
+
+    def __getitem__(self, at):
+        self.wait()
+        return self.ref[at]
+
+
+def call(
+    kernel, inputs, outputs, scratch=(), smem=0, flops=0, room=16, fetch=(), far_in=(), far_out=(),
+    alias=None, pinned=(),
+):
+    count_in, count_out = len(inputs), len(outputs)
+    inputs = list(inputs)
+    for at in (*fetch, *pinned):
+        inputs[at] = pltpu.with_memory_space_constraint(inputs[at], pltpu.HBM)
+    in_space = [pltpu.SMEM] * smem + [pltpu.VMEM] * (count_in - smem)
+    out_space = [pltpu.VMEM] * count_out
+    for at in fetch:
+        in_space[at] = pltpu.HBM
+    for at in far_in:
+        in_space[at] = pl.ANY
+    for at in far_out:
+        out_space[at] = pl.ANY
     size = sum(math.prod(s) * jnp.dtype(d).itemsize for s, d in outputs)
     size += sum(math.prod(a.shape) * a.dtype.itemsize for a in inputs)
+    buffers = [pltpu.VMEM(inputs[at].shape, inputs[at].dtype) for at in fetch]
+    if fetch:
+        buffers.append(pltpu.SemaphoreType.DMA((len(fetch),)))
+
+    def with_copies(*refs):
+        refs = list(refs)
+        if fetch:
+            held, sem = refs[-len(fetch) - 1 : -1], refs[-1]
+            refs = refs[: -len(fetch) - 1]
+            for number, at in enumerate(fetch):
+                copy = pltpu.make_async_copy(refs[at], held[number], sem.at[number])
+                copy.start()
+                refs[at] = Fetched(held[number], copy)
+        kernel(*refs)
+        for at in fetch:
+            refs[at].wait()
+
     return pl.pallas_call(
-        kernel,
+        with_copies,
         out_shape=[jax.ShapeDtypeStruct(s, d) for s, d in outputs],
-        in_specs=[pl.BlockSpec(memory_space=s) for s in space],
-        out_specs=[pl.BlockSpec(memory_space=pltpu.VMEM) for _ in outputs],
-        scratch_shapes=[pltpu.VMEM(s, d) for s, d in scratch],
-        compiler_params=pltpu.CompilerParams(vmem_limit_bytes=VMEM_LIMIT),
+        in_specs=[pl.BlockSpec(memory_space=s) for s in in_space],
+        out_specs=[pl.BlockSpec(memory_space=s) for s in out_space],
+        scratch_shapes=[pltpu.VMEM(*s) if isinstance(s, tuple) else s for s in scratch] + buffers,
+        input_output_aliases=alias or {},
+        compiler_params=pltpu.CompilerParams(vmem_limit_bytes=room * 1024 * 1024),
         cost_estimate=pl.CostEstimate(flops=flops, bytes_accessed=size, transcendentals=0),
     )(*inputs)
 
@@ -597,34 +725,144 @@
     return lax.ppermute(array, axis, [(i, i ^ distance) for i in range(count)])
 
 
-def shifted(array, axis, by):
+def swap_outer(array, axis):
     count = lax.axis_size(axis)
-    return lax.ppermute(array, axis, [(i, i + by) for i in range(count) if 0 <= i + by < count])
-
-
-def add(*arrays):
-    total = arrays[0].astype(F32)
-    for array in arrays[1:]:
-        total = total + array.astype(F32)
+    pairs = [(i, i + 1) for i in range(1, count - 1, 2)]
+    return lax.ppermute(array, axis, pairs + [(j, i) for i, j in pairs])
+
+
+def after(value, *others):
+    return lax.optimization_barrier((value, others))[0]
+
+
+def planes(parts):
+    if not isinstance(parts, (list, tuple)):
+        parts = [parts] * 4
+    return [swap(parts[plane], "seq", 2 * plane) for plane in (3, 1, 2)]
+
+
+def sum_of(*values):
+    total = values[0].astype(F32)
+    for value in values[1:]:
+        total = total + value.astype(F32)
     return total.astype(BF16)
 
 
-def sum_pieces(slots):
-    rows = slots.shape[1]
-    slots = slots.reshape(2, 4, 4, rows, 128)
-    other = swap(slots[1], "seq", 1)
-    parts = [add(slots[0, quad], other[quad]) for quad in range(4)]
-    came = [swap(parts[quad], "seq", 2 * quad) for quad in range(1, 4)]
-    depths = [add(*[part[depth] for part in [parts[0]] + came]) for depth in range(4)]
-    came = [swap(depths[depth], "batch", depth) for depth in range(1, 4)]
-    whole = add(depths[0], *came)
+def cores_kernel(cut, keep, other, *outs):
+    ways = ((slice(cut), ((1, 3), (0, 2))), (slice(cut, None), ((2, 3), (0, 1))))
+    for way, (rows, groups) in enumerate(ways):
+        for number, group in enumerate(groups):
+            for at, plane in enumerate(group):
+                for depth in range(4):
+                    slot = 4 * plane + depth
+                    outs[2 * way + number][at, depth] = sum_of(keep[slot, rows], other[slot, rows])
+
+
+def add_cores(keep, other, cut):
+    rows = keep.shape[1]
+    shapes = [(2, 4, cut, 128)] * 2 + [(2, 4, rows - cut, 128)] * 2
+    kernel = functools.partial(cores_kernel, cut)
+    return call(kernel, (keep, other), [(s, BF16) for s in shapes], room=12)
+
+
+def step_one(parts):
+    return [swap(parts[0], "seq", 2), swap(parts[2], "seq", 4)]
+
+
+def step_two(parts):
+    return [swap(parts[0], "seq", 4), swap(parts[2], "seq", 2)]
+
+
+def step_one_kernel(first, first_came, last, last_came, *outs):
+    for way, (kept, came) in enumerate(((first, first_came), (last, last_came))):
+        for number, plane in enumerate((1, 0)):
+            for depth in range(4):
+                outs[2 * way + number][depth] = sum_of(kept[plane, depth], came[plane, depth])
+
+
+def add_step_one(parts, came):
+    inputs = (parts[1], came[0], parts[3], came[1])
+    shapes = [(parts[0].shape[1:], BF16)] * 2 + [(parts[2].shape[1:], BF16)] * 2
+    return call(step_one_kernel, inputs, shapes, room=8)
+
+
+def step_two_kernel(first, first_came, last, last_came, *outs):
+    cut, rows = first.shape[1], outs[0].shape[1]
+    for depth in range(4):
+        out = outs[1 - depth % 2]
+        out[depth // 2, 0:cut] = sum_of(first[depth], first_came[depth])
+        out[depth // 2, cut:] = sum_of(last[depth, : rows - cut], last_came[depth, : rows - cut])
+        if len(outs) > 2:
+            outs[2][depth] = sum_of(last[depth, rows - cut :], last_came[depth, rows - cut :])
+
+
+def add_step_two(parts, came, extra=0):
+    rows = parts[0].shape[1] + parts[2].shape[1] - extra
+    inputs = (parts[1], came[0], parts[3], came[1])
+    outputs = [((2, rows, 128), BF16)] * 2
+    if extra:
+        outputs.append(((4, extra, 128), BF16))
+    return call(step_two_kernel, inputs, outputs, room=8)
+
+
+def near_kernel(kept, came, sent, mine):
+    mine[...] = sum_of(kept[0], came[0])
+    sent[...] = sum_of(kept[1], came[1])
+
+
+def add_near(kept, came):
+    return call(near_kernel, (kept, came), [(kept.shape[1:], BF16)] * 2, room=8)
+
+
+def far_kernel(mine, came, whole):
+    whole[...] = sum_of(mine[...], came[...])
+
+
+def add_far(mine, came):
+    (whole,) = call(far_kernel, (mine, came), [(mine.shape, BF16)], room=8)
     distance = 8
     while distance < lax.axis_size("seq"):
-        whole = add(whole, swap(whole, "seq", distance))
+        other = swap(whole, "seq", distance)
+        (whole,) = call(far_kernel, (whole, other), [(mine.shape, BF16)], room=8)
         distance *= 2
-    column = jnp.stack([whole] + [swap(whole, "batch", depth) for depth in range(1, 4)])
-    plane = [column] + [swap(column, "seq", 2 * quad) for quad in range(1, 4)]
-    return plane + [swap(block, "seq", 1) for block in plane]
+    return whole
+
+
+def pair_kernel(one, two, out):
+    out[0] = one[...]
+    out[1] = two[...]
+
+
+def pair_of(one, two):
+    (pair,) = call(pair_kernel, (one, two), [((2, *one.shape), BF16)], room=8)
+    return pair
+
+
+def column_kernel(pair, came, out):
+    for far in range(2):
+        out[2 * far] = pair[far]
+        out[2 * far + 1] = came[far]
+
+
+def column_of(pair, came):
+    (column,) = call(column_kernel, (pair, came), [((4, *pair.shape[1:]), BF16)], room=8)
+    return column
+
+
+def plane_of(column, came):
+    return [column, came[1], came[2], came[0]]
+
+
+def chip_kernel(inner, came, chip):
+    chip[0:GATHER] = inner[HALO:]
+    chip[GATHER:] = came[HALO:]
+
+
+def share(inner, came):
+    if not direct(lax.axis_size("seq")):
+        return [lax.all_gather(inner[HALO:], "seq", axis=0, tiled=True)]
+    (chip,) = call(chip_kernel, (inner, came), [((2 * GATHER, inner.shape[1]), BF16)], room=8)
+    return plane_of(chip, planes(chip))
 
 
 def on_device(
@@ -640,7 +878,6 @@
     lent = 2 * HALO + far
     cols = columns_of(levels)
     groups = (ROWS // SUB) * (HEADS // QUAD)
-    pool = jnp.asarray(pool_matrix(levels), BF16)
     bias_table = jnp.asarray(score_bias(levels))
     codes = jnp.asarray(column_codes(levels))
 
@@ -648,31 +885,48 @@
         return vector.reshape(1, -1)
 
     gain, shift = row(first_gain), row(first_shift)
-    normed_low, for_next, for_prev, for_all = call(
-        first_kernel,
-        (tokens, gain, shift, pool),
-        [((ROWS, width), BF16), ((HALO, width), BF16), ((HALO, width), BF16)]
-        + [((GATHER, width), BF16)],
+    inner, outer = call(
+        functools.partial(first_kernel, levels),
+        (tokens,),
+        [((HALO + GATHER, width), BF16), ((HALO, width), BF16)],
         flops=4 * ROWS * ROWS * width,
-    )
-    from_prev = shifted(for_next, "seq", 1)
-    from_next = shifted(for_prev, "seq", -1)
-    window = lax.all_gather(for_all, "seq", axis=0, tiled=True)
-    query, key, value, key_pool, value_pool = call(
-        project_kernel,
-        (normed_low, query_weight, row(query_bias), key_weight, value_weight, row(value_bias), pool),
-        [((ROWS, width), BF16)] * 3 + [((POOLED, width), BF16)] * 2,
+        room=8,
+    )
+    inner_came = swap(inner, "seq", 1)
+    outer_came = swap_outer(outer, "seq")
+    windows = share(inner, inner_came)
+    (
+        normed_low, query, key, value, key_pool, value_pool, out_weight, up_weight, down_weight,
+        cotangent,
+    ) = call(
+        functools.partial(project_kernel, levels),
+        (
+            tokens, gain, shift, query_weight, row(query_bias), key_weight, value_weight,
+            row(value_bias), out_weight, up_weight, down_weight, cotangent,
+        ),
+        [((ROWS, width), BF16)] * 4
+        + [((POOLED, width), BF16)] * 2
+        + [(a.shape, a.dtype) for a in (out_weight, up_weight, down_weight, cotangent)],
+        scratch=[pltpu.SemaphoreType.DMA((4,))],
+        fetch=(0, 1, 2, 3, 4, 5, 6, 7),
+        far_in=(8, 9, 10, 11),
+        pinned=(8, 9, 10, 11),
         flops=8 * ROWS * width * width,
-    )
+        room=24,
+    )
+    extra = extra_rows(holders)
+    owner_shapes = [] if extra else [((holders * GATHER, width), BF16)]
+    half = PIECES // 2
+    dma_pair = pltpu.SemaphoreType.DMA((2,))
     (
-        output, attended, weights, halo, key_halo, value_halo, grad_mid, sums,
+        output, attended, weights, halo, key_halo, value_halo, mid, grad_second, late, keep, send,
     ) = call(
-        functools.partial(middle_kernel, levels, holders),
+        functools.partial(middle_kernel, levels, holders, len(windows)),
         (
-            item_start, tokens, cotangent, query, key, value, key_pool, value_pool, from_prev,
-            from_next, window, gain, shift, key_weight, value_weight, row(value_bias), out_weight,
+            item_start, tokens, cotangent, query, key, value, key_pool, value_pool, inner_came,
+            outer_came, gain, shift, key_weight, value_weight, row(value_bias), out_weight,
             row(out_bias), row(second_gain), row(second_shift), up_weight, row(up_bias),
-            down_weight, row(down_bias), bias_table, codes,
+            down_weight, row(down_bias), bias_table, codes, *windows,
         ),
         [
             ((1, ROWS, width), BF16),
@@ -682,33 +936,52 @@
             ((lent, width), BF16),
             ((lent, width), BF16),
             ((ROWS, width), F32),
-            ((PIECES, 512 + SMALL, 128), BF16),
+            ((ROWS, width), F32),
+            ((width, hidden - EARLY_UP), BF16),
+            ((half, FIRST_ROWS, 128), BF16),
+            ((half, FIRST_ROWS, 128), BF16),
         ],
         scratch=[
             ((cols, width), BF16),
             ((cols, width), BF16),
             ((ROWS, width), BF16),
-            ((PIECES, 512 + SMALL, 128), BF16),
+            ((PIECES, FIRST_ROWS, 128), BF16),
             ((2 * SMALL, 128), F32),
+            dma_pair,
         ],
         smem=1,
+        fetch=(12, 13, 10, 11, 14, 23, 24, 16, 1, 17, 18, 20, 22),
+        far_out=(9, 10),
         flops=12 * ROWS * width * hidden,
-    )
-    first_sums = sum_pieces(sums)
-    grad_normed, to_prev, to_next, to_owners, sums = call(
+        room=32,
+    )
+    other = swap(send, "seq", 1)
+    grad_mid, grad_attended, grad_out, vectors = call(
+        branch_kernel,
+        (cotangent, mid, grad_second, row(second_gain), attended, out_weight),
+        [((ROWS, width), F32), ((ROWS, width), BF16), ((width, width), BF16), ((8, width), F32)],
+        fetch=(3,),
+        flops=4 * ROWS * width * width,
+        room=8,
+    )
+    first = add_cores(keep, after(other, grad_attended), FIRST_CUT)
+    first_came = step_one(first)
+    grad_attended, grad_out, vectors = after((grad_attended, grad_out, vectors), first)
+    grad_normed, inner, outer, keep, send, *owners = call(
         functools.partial(back_kernel, levels, holders),
         (
             tokens, normed_low, query, key, value, key_pool, value_pool, halo, key_halo,
-            value_halo, weights, attended, grad_mid, gain, shift, query_weight, key_weight,
-            value_weight, out_weight, pool,
+            value_halo, weights, grad_attended, grad_out, late, vectors, gain, shift, query_weight,
+            key_weight, value_weight,
         ),
         [
             ((ROWS, width), F32),
             ((HALO, width), BF16),
             ((HALO, width), BF16),
-            ((holders * GATHER, width), BF16),
-            ((PIECES, 256 + SMALL, 128), BF16),
-        ],
+            ((half, SECOND_ROWS + extra, 128), BF16),
+            ((half, SECOND_ROWS + extra, 128), BF16),
+        ]
+        + owner_shapes,
         scratch=[
             ((cols, width), BF16),
             ((cols, width), BF16),
@@ -719,40 +992,73 @@
             ((ROWS, width), F32),
             ((POOLED, width), F32),
             ((lent, width), F32),
-            ((PIECES, 256 + SMALL, 128), BF16),
+            ((PIECES, SECOND_ROWS + extra, 128), BF16),
             ((2 * SMALL, 128), F32),
+            dma_pair,
         ],
+        fetch=(15, 16, 0, 17, 18, 19),
+        far_out=(3, 4),
         flops=20 * ROWS * width * width,
-    )
-    second_sums = sum_pieces(sums)
-    back_next = shifted(to_prev, "seq", -1)
-    back_prev = shifted(to_next, "seq", 1)
-    users = lax.all_to_all(
-        to_owners.reshape(holders, GATHER, width), "seq", split_axis=0, concat_axis=0, tiled=True
-    )
+        room=28,
+    )
+    other = swap(after(send, first_came), "seq", 1)
+    inner_came = swap(inner, "seq", 1)
+    outer_came = swap_outer(outer, "seq")
+    first = add_step_one(first, first_came)
+    first_came = step_two(first)
+    second = add_cores(keep, other, SECOND_CUT)
+    second_came = step_one(second)
+    sent, kept = add_step_two(first, after(first_came, second))
+    sent, kept = add_near(kept, swap(sent, "batch", 1))
+    second = add_step_one(second, after(second_came, kept))
+    second_came = step_two(second)
+    first = add_far(kept, after(swap(sent, "batch", 2), second))
+    pair = pair_of(first, swap(first, "batch", 2))
+    sent, kept, *users = add_step_two(second, after(second_came, pair), extra)
+    column = column_of(pair, after(swap(pair, "batch", 1), kept))
+    first_came = planes(column)
+    sent, kept = add_near(kept, after(swap(sent, "batch", 1), column))
+    second = add_far(kept, swap(sent, "batch", 2))
+    pair = pair_of(second, swap(second, "batch", 2))
+    second_column = column_of(pair, swap(pair, "batch", 1))
+    second_came = planes(second_column)
+    if not users:
+        rows = owners[0].reshape(holders, GATHER, width)
+        users = list(lax.all_to_all(rows, "seq", split_axis=0, concat_axis=0, tiled=True))
+    users, inner_came, outer_came = after((users, inner_came, outer_came), second_column)
     (grad_tokens,) = call(
-        last_kernel,
-        (tokens, gain, grad_mid, grad_normed, back_prev, back_next, users, pool),
+        functools.partial(last_kernel, levels),
+        (tokens, gain, grad_mid, grad_normed, inner_came, outer_came, *users),
         [((1, ROWS, width), F32)],
         scratch=[((ROWS, width), F32)],
+        fetch=(0, 1),
         flops=4 * ROWS * ROWS * width,
-    )
+        room=8,
+    )
+    first_sums = plane_of(column, after(first_came, grad_tokens))
+    first_sums += [swap(block, "seq", 1) for block in first_sums]
     lines = width // 128
     small = ((lines, 128), F32)
-    scratch = [((PIECES * SMALL, 128), F32)]
-    down, up, down_b, up_b, gain2, shift2 = call(
+    square = ((width, width), F32)
+    small_rows = ((PIECES * SMALL, 128), F32)
+    down, up, down_b, up_b = call(
         functools.partial(collect_kernel, 1),
         first_sums,
-        [((hidden, width), F32), ((width, hidden), F32), small, ((hidden // 128, 128), F32)]
-        + [small] * 2,
-        scratch=scratch,
-    )
-    square = ((width, width), F32)
-    out_w, query_w, key_w, value_w, query_b, value_b, out_b, gain1, shift1 = call(
+        [((hidden, width), F32), ((width, hidden), F32), small, ((hidden // 128, 128), F32)],
+        scratch=[small_rows],
+        room=24,
+    )
+    second_sums = plane_of(second_column, after(second_came, down_b))
+    second_sums += [swap(block, "seq", 1) for block in second_sums]
+    up, out_w, query_w, key_w, value_w, query_b, value_b, out_b, gain1, shift1, gain2, shift2 = call(
         functools.partial(collect_kernel, 2),
-        second_sums,
-        [square] * 4 + [small] * 5,
-        scratch=scratch,
+        [*second_sums, up],
+        [((width, hidden), F32)] + [square] * 4 + [small] * 7,
+        scratch=[((width, hidden - EARLY_UP), F32), pltpu.SemaphoreType.DMA, small_rows],
+        far_in=(8,),
+        far_out=(0,),
+        alias={8: 0},
+        room=20,
     )
     vectors = [query_b, value_b, out_b, up_b, down_b, gain1, shift1, gain2, shift2]
     return (output, grad_tokens, query_w, key_w, value_w, out_w, up, down) + tuple(

time: 193 us -> 140 us (0.73)
  waiting for transfers between devices: 72.2 us -> 45.7 us
  blocking collectives: 24.5 us -> 0 us
  starting transfers between devices: 41.1 us -> 54.4 us
  local copies, waits for them, and re-layouts: 7.95 us -> 0.95 us
  Pallas kernels: 44.4 us -> 38 us
    ppermute x34 -> x37, waiting for transfers between devices: 72.2 us -> 45.7 us  [swap(): return lax.ppermute(array, axis, [(i, i ^ distance) for i in range(count)])]
    ppermute x34 -> x37, starting transfers between devices: 34.8 us -> 53 us  [swap(): return lax.ppermute(array, axis, [(i, i ^ distance) for i in range(count)])]
    all_gather x1 -> x0, blocking collectives: 14.5 us -> none  [on_device(): window = lax.all_gather(for_all, 'seq', axis=0, tiled=True)]
    all_to_all x1 -> x0, blocking collectives: 9.99 us -> none  [on_device(): lax.all_to_all(to_owners.reshape(holders, GATHER, width), 'seq', split_ax...]
    pallas_call x7 -> x23, Pallas kernels: 44.4 us -> 38 us  [call(): pl.pallas_call(with_copies, out_shape=[jax.ShapeDtypeStruct(s, d) for s,...]
    ppermute x4 -> x2, starting transfers between devices: 6.34 us -> 1.31 us  [swap_outer(): return lax.ppermute(array, axis, pairs + [(j, i) for i, j in pairs])]
    slice x2 -> x0, local copies, waits for them, and re-layouts: 4.56 us -> none  [sum_pieces(): other = swap(slots[1], 'seq', 1)]
    unnamed x54 -> x4, local copies, waits for them, and re-layouts: 3.39 us -> 0.95 us
  transfers between devices with their start and end apart: 38 -> 39, of which waited for: 17 -> 21; matrix products, arithmetic and copies ran while one was open for 2% -> 0% of each run, Pallas kernels for 11% -> 14%
where the time goes in v2:
time: 140 us
  starting transfers between devices  54.4 us (39%)
  waiting for transfers between devices  45.7 us (33%)
  Pallas kernels  38 us (27%)
    ppermute x37, starting transfers between devices, swap(): return lax.ppermute(array, axis, [(i, i ^ distance) for i in range(count)])  53 us
    ppermute x37, waiting for transfers between devices, swap(): return lax.ppermute(array, axis, [(i, i ^ distance) for i in range(count)])  45.7 us
    pallas_call x23, Pallas kernels, call(): pl.pallas_call(with_copies, out_shape=[jax.ShapeDtypeStruct(s, d) for s,...  38 us
  transfers between devices with their start and end apart: 39, of which 21 were waited for; matrix products, arithmetic and copies ran while one was open for 0% of the time, Pallas kernels for 14%

profile of v2, /device:TPU:0, one launch (start us, length us, event | category | flops | bytes accessed | tf_op | source)
XLA Modules:
  0.0 140.1 jit_solution(6623155363193009419)
XLA Ops:
  3.7 5.1 %collective-permute-start.4 = (bf16[64,512]{1,0:T(8,128)(2,1)S(1)}, bf16[64,512]{1,0:T(8,128)(2,1)S(1)}, u32[]{:S(2)}, u32[]{:S(2)}) collective-permute-start(bf16[64,512]{1,0:T(8,128)(2,1)S(1)} %shard_map.325.refs_25_), channel_id=1, source_target_pairs={{0,6},{1,7},{2,4},{3,5},{4,2},{5,3},{6,0},{7,1},{8,14},{9,15},{10,... | collective-permute-start | bytes 196616 | tf_op jit(solution)/shard_map/ppermute | solution.py:725
  10.2 3.3 %shard_map.323 = (bf16[256,512]{1,0:T(8,128)(2,1)S(1)}, bf16[256,512]{1,0:T(8,128)(2,1)S(1)}, bf16[256,512]{1,0:T(8,128)(2,1)S(1)}, bf16[256,512]{1,0:T(8,128)(2...) custom-call(bf16[1,256,512]{2,1,0:T(8,128)(2,1)} %refs_0_.9, ...), custom_call_target="tpu_custom_call" | custom-call | flops 536870912 | bytes 13312000 | tf_op jit(solution)/shard_map/pallas_call | solution.py:711
  13.9 13.6 %shard_map.326 = (bf16[1,256,512]{2,1,0:T(8,128)(2,1)}, bf16[256,512]{1,0:T(8,128)(2,1)S(1)}, bf16[8,256,384]{2,1,0:T(8,128)(2,1)S(1)}, bf16[320,512]{1,0:T(8,12...) custom-call(s32[1,2]{1,0:T(1,128)S(1)} %copy-done.1, ...), custom_call_target="tpu_custom_call" | custom-call | flops 3221225472 | bytes 16648200 | tf_op jit(solution)/shard_map/pallas_call | solution.py:711
  29.0 2.5 %collective-permute-done.5.refs_1_ = bf16[16,464,128]{2,1,0:T(8,128)(2,1)S(1)} collective-permute-done((bf16[16,464,128]{2,1,0:T(8,128)(2,1)S(1)}, bf16[16,464,128]{2,1,0:T(8,128)(2,1)S(1)}, u32[]{:S(2)}, u32[]{:S(2)}) %collective-permute-start.5) | collective-permute-done | bytes 1900576 | tf_op jit(solution)/shard_map/ppermute | solution.py:725
  31.9 2.3 %collective-permute-start.6 = (bf16[2,4,256,128]{3,2,1,0:T(8,128)(2,1)S(1)}, bf16[2,4,256,128]{3,2,1,0:T(8,128)(2,1)S(1)}, u32[]{:S(2)}, u32[]{:S(2)}) collective-permute-start(bf16[2,4,256,128]{3,2,1,0:T(8,128)(2,1)S(1)} %get-tuple-element.140), channel_id=1, source_target_pairs={{0,2},{1,3},{2,0},{3,1},{4,6},{5,7},{6,4},{7,5},{8,10},{9,11},{10,... | collective-permute-start | bytes 1572872 | tf_op jit(solution)/shard_map/ppermute | solution.py:725
  35.0 7.8 %shard_map.329 = (f32[256,512]{1,0:T(8,128)S(1)}, bf16[112,512]{1,0:T(8,128)(2,1)S(1)}, bf16[112,512]{1,0:T(8,128)(2,1)S(1)}, bf16[16,368,128]{2,1,0:T(8,128)(2,1)S(1)}, bf16[16,368,128]{2,1,0:T(8,128)(2,1)S(1)}) custom-call(bf16[1,256,512]{2,1,0:T(8,128)(2,1)} %refs_0_.9, bf16[256,512]{1,0:T(8,128)(2,1)S(1)} %get-tuple-element.129.refs_1_, ...), custom_call_target="tpu_custom_call" | custom-call | flops 1342177280 | bytes 10997760 | tf_op jit(solution)/shard_map/pallas_call | solution.py:711
  42.8 3.0 %collective-permute-done.7.refs_3_ = bf16[2,4,208,128]{3,2,1,0:T(8,128)(2,1)S(1)} collective-permute-done((bf16[2,4,208,128]{3,2,1,0:T(8,128)(2,1)S(1)}, bf16[2,4,208,128]{3,2,1,0:T(8,128)(2,1)S(1)}, u32[]{:S(2)}, u32[]{:S(2)}) %collective-permute-start.7) | collective-permute-done | bytes 426016 | tf_op jit(solution)/shard_map/ppermute | solution.py:725
  52.7 3.4 %collective-permute-done.12.refs_3_ = bf16[4,208,128]{2,1,0:T(8,128)(2,1)S(1)} collective-permute-done((bf16[4,208,128]{2,1,0:T(8,128)(2,1)S(1)}, bf16[4,208,128]{2,1,0:T(8,128)(2,1)S(1)}, u32[]{:S(2)}, u32[]{:S(2)}) %collective-permute-start.12) | collective-permute-done | bytes 213024 | tf_op jit(solution)/shard_map/ppermute | solution.py:725
  58.0 5.0 %collective-permute-done.13.refs_1_ = bf16[2,464,128]{2,1,0:T(8,128)(2,1)S(1)} collective-permute-done((bf16[2,464,128]{2,1,0:T(8,128)(2,1)S(1)}, bf16[2,464,128]{2,1,0:T(8,128)(2,1)S(1)}, u32[]{:S(2)}, u32[]{:S(2)}) %collective-permute-start.13) | collective-permute-done | bytes 237600 | tf_op jit(solution)/shard_map/ppermute | solution.py:725
  63.1 2.8 %collective-permute-start.16 = (bf16[464,128]{1,0:T(8,128)(2,1)S(1)}, bf16[464,128]{1,0:T(8,128)(2,1)S(1)}, u32[]{:S(2)}, u32[]{:S(2)}) collective-permute-start(bf16[464,128]{1,0:T(8,128)(2,1)S(1)} %get-tuple-element.170), channel_id=1, source_target_pairs={{0,16},{8,24},{16,0},{24,8},{1,17},{9,25},{17,1},{25,9},{2,18},{10... | collective-permute-start | bytes 356360 | tf_op jit(solution)/shard_map/ppermute | solution.py:725
  69.0 2.9 %collective-permute-start.17 = (bf16[464,128]{1,0:T(8,128)(2,1)S(1)}, bf16[464,128]{1,0:T(8,128)(2,1)S(1)}, u32[]{:S(2)}, u32[]{:S(2)}) collective-permute-start(bf16[464,128]{1,0:T(8,128)(2,1)S(1)} %shard_map.335.refs_0_), channel_id=1, source_target_pairs={{0,16},{8,24},{16,0},{24,8},{1,17},{9,25},{17,1},{25,9},{2,18},{10... | collective-permute-start | bytes 356360 | tf_op jit(solution)/shard_map/ppermute | solution.py:725
  74.8 5.6 %collective-permute-start.21 = (bf16[2,464,128]{2,1,0:T(8,128)(2,1)S(1)}, bf16[2,464,128]{2,1,0:T(8,128)(2,1)S(1)}, u32[]{:S(2)}, u32[]{:S(2)}) collective-permute-start(bf16[2,464,128]{2,1,0:T(8,128)(2,1)S(1)} %shard_map.336.refs_0_), channel_id=1, source_target_pairs={{0,8},{8,0},{16,24},{24,16},{1,9},{9,1},{17,25},{25,17},{2,10},{10... | collective-permute-start | bytes 712712 | tf_op jit(solution)/shard_map/ppermute | solution.py:725
  81.8 2.6 %collective-permute-done.21.refs_1_ = bf16[2,464,128]{2,1,0:T(8,128)(2,1)S(1)} collective-permute-done((bf16[2,464,128]{2,1,0:T(8,128)(2,1)S(1)}, bf16[2,464,128]{2,1,0:T(8,128)(2,1)S(1)}, u32[]{:S(2)}, u32[]{:S(2)}) %collective-permute-start.21) | collective-permute-done | bytes 237600 | tf_op jit(solution)/shard_map/ppermute | solution.py:725
  89.9 3.6 %collective-permute-done.22.refs_1_ = bf16[336,128]{1,0:T(8,128)(2,1)S(1)} collective-permute-done((bf16[336,128]{1,0:T(8,128)(2,1)S(1)}, bf16[336,128]{1,0:T(8,128)(2,1)S(1)}, u32[]{:S(2)}, u32[]{:S(2)}) %collective-permute-start.22) | collective-permute-done | bytes 86048 | tf_op jit(solution)/shard_map/ppermute | solution.py:725
  95.4 3.6 %collective-permute-done.23.refs_1_ = bf16[336,128]{1,0:T(8,128)(2,1)S(1)} collective-permute-done((bf16[336,128]{1,0:T(8,128)(2,1)S(1)}, bf16[336,128]{1,0:T(8,128)(2,1)S(1)}, u32[]{:S(2)}, u32[]{:S(2)}) %collective-permute-start.23) | collective-permute-done | bytes 86048 | tf_op jit(solution)/shard_map/ppermute | solution.py:725
  99.0 2.5 %collective-permute-start.24 = (bf16[2,336,128]{2,1,0:T(8,128)(2,1)S(1)}, bf16[2,336,128]{2,1,0:T(8,128)(2,1)S(1)}, u32[]{:S(2)}, u32[]{:S(2)}) collective-permute-start(bf16[2,336,128]{2,1,0:T(8,128)(2,1)S(1)} %shard_map.341.refs_0_), channel_id=1, source_target_pairs={{0,8},{8,0},{16,24},{24,16},{1,9},{9,1},{17,25},{25,17},{2,10},{10... | collective-permute-start | bytes 516104 | tf_op jit(solution)/shard_map/ppermute | solution.py:725
  101.6 3.4 %collective-permute-done.24.refs_1_ = bf16[2,336,128]{2,1,0:T(8,128)(2,1)S(1)} collective-permute-done((bf16[2,336,128]{2,1,0:T(8,128)(2,1)S(1)}, bf16[2,336,128]{2,1,0:T(8,128)(2,1)S(1)}, u32[]{:S(2)}, u32[]{:S(2)}) %collective-permute-start.24) | collective-permute-done | bytes 172064 | tf_op jit(solution)/shard_map/ppermute | solution.py:725
  105.7 2.8 %collective-permute-start.31 = (bf16[4,464,128]{2,1,0:T(8,128)(2,1)S(1)}, bf16[4,464,128]{2,1,0:T(8,128)(2,1)S(1)}, u32[]{:S(2)}, u32[]{:S(2)}) collective-permute-start(bf16[4,464,128]{2,1,0:T(8,128)(2,1)S(1)} %shard_map.338.refs_0_), channel_id=1, source_target_pairs={{0,1},{1,0},{2,3},{3,2},{4,5},{5,4},{6,7},{7,6},{8,9},{9,8},{10,11... | collective-permute-start | bytes 1425416 | tf_op jit(solution)/shard_map/ppermute | solution.py:725
  110.7 3.1 %collective-permute-start.32 = (bf16[4,464,128]{2,1,0:T(8,128)(2,1)S(1)}, bf16[4,464,128]{2,1,0:T(8,128)(2,1)S(1)}, u32[]{:S(2)}, u32[]{:S(2)}) collective-permute-start(bf16[4,464,128]{2,1,0:T(8,128)(2,1)S(1)} %collective-permute-done.29.refs_1_), channel_id=1, source_target_pairs={{0,1},{1,0},{2,3},{3,2},{4,5},{5,4},{6,7},{7,6},{8,9},{9,8},{10,11... | collective-permute-start | bytes 1425416 | tf_op jit(solution)/shard_map/ppermute | solution.py:725
  118.1 4.0 %shard_map.344 = (f32[2048,512]{1,0:T(8,128)}, f32[512,2048]{1,0:T(8,128)}, f32[4,128]{1,0:T(4,128)}, f32[16,128]{1,0:T(8,128)}) custom-call(bf16[4,464,128]{2,1,0:T(8,128)(2,1)S(1)} %shard_map.338.refs_0_, bf16[4,464,128]{2,1,0:T(8,128)(2,1)S(1)} %collective-permute-done.29.refs_1_, bf16[4,464,128]{2,1,0:T(8,128)(2,1)S(1)} %collective-permute-done.30.refs_2_, ...), custom_call_target="tpu_custom_call" | custom-call | bytes 12199936 | tf_op jit(solution)/shard_map/pallas_call | solution.py:711
  122.1 3.2 %collective-permute-done.27.refs_2_ = bf16[4,336,128]{2,1,0:T(8,128)(2,1)S(1)} collective-permute-done((bf16[4,336,128]{2,1,0:T(8,128)(2,1)S(1)}, bf16[4,336,128]{2,1,0:T(8,128)(2,1)S(1)}, u32[]{:S(2)}, u32[]{:S(2)}) %collective-permute-start.27) | collective-permute-done | bytes 344096 | tf_op jit(solution)/shard_map/ppermute | solution.py:725
  125.2 2.3 %collective-permute-done.26.refs_1_ = bf16[4,336,128]{2,1,0:T(8,128)(2,1)S(1)} collective-permute-done((bf16[4,336,128]{2,1,0:T(8,128)(2,1)S(1)}, bf16[4,336,128]{2,1,0:T(8,128)(2,1)S(1)}, u32[]{:S(2)}, u32[]{:S(2)}) %collective-permute-start.26) | collective-permute-done | bytes 344096 | tf_op jit(solution)/shard_map/ppermute | solution.py:725
  127.5 6.3 %collective-permute-done.25.refs_3_ = bf16[4,336,128]{2,1,0:T(8,128)(2,1)S(1)} collective-permute-done((bf16[4,336,128]{2,1,0:T(8,128)(2,1)S(1)}, bf16[4,336,128]{2,1,0:T(8,128)(2,1)S(1)}, u32[]{:S(2)}, u32[]{:S(2)}) %collective-permute-start.25) | collective-permute-done | bytes 344096 | tf_op jit(solution)/shard_map/ppermute | solution.py:725
  136.4 3.5 %shard_map.345 = (f32[512,2048]{1,0:T(8,128)}, f32[512,512]{1,0:T(8,128)}, f32[512,512]{1,0:T(8,128)}, f32[512,512]{1,0:T(8,128)}, f32[512,512]{1,0:T(8,128)}, /...) custom-call(bf16[4,336,128]{2,1,0:T(8,128)(2,1)S(1)} %shard_map.342., ...), custom_call_target="tpu_custom_call", output_to_operand_aliasing={{0}: (8, {})} | custom-call | bytes 15349760 | tf_op jit(solution)/shard_map/pallas_call | solution.py:711
  (81 shorter events, 40.9 us)
Async XLA Ops:
  2.7 10.8 %collective-permute-start.1 = (bf16[112,512]{1,0:T(8,128)(2,1)S(1)}, bf16[112,512]{1,0:T(8,128)(2,1)S(1)}, u32[]{:S(2)}, u32[]{:S(2)}) collective-permute-start(bf16[112,512]{1,0:T(8,128)(2,1)S(1)} %get-tuple-element.120), channel_id=1, source_target_pairs={{1,2},{3,4},{5,6},{2,1},{4,3},{6,5},{9,10},{11,12},{13,14},{10,9},... | collective-permute-start | bytes 344072 | tf_op jit(solution)/shard_map/ppermute | solution.py:731
  3.7 9.8 %collective-permute-start.4 = (bf16[64,512]{1,0:T(8,128)(2,1)S(1)}, bf16[64,512]{1,0:T(8,128)(2,1)S(1)}, u32[]{:S(2)}, u32[]{:S(2)}) collective-permute-start(bf16[64,512]{1,0:T(8,128)(2,1)S(1)} %shard_map.325.refs_25_), channel_id=1, source_target_pairs={{0,6},{1,7},{2,4},{3,5},{4,2},{5,3},{6,0},{7,1},{8,14},{9,15},{10,... | collective-permute-start | bytes 196616 | tf_op jit(solution)/shard_map/ppermute | solution.py:725
  31.9 14.5 %collective-permute-start.6 = (bf16[2,4,256,128]{3,2,1,0:T(8,128)(2,1)S(1)}, bf16[2,4,256,128]{3,2,1,0:T(8,128)(2,1)S(1)}, u32[]{:S(2)}, u32[]{:S(2)}) collective-permute-start(bf16[2,4,256,128]{3,2,1,0:T(8,128)(2,1)S(1)} %get-tuple-element.140), channel_id=1, source_target_pairs={{0,2},{1,3},{2,0},{3,1},{4,6},{5,7},{6,4},{7,5},{8,10},{9,11},{10,... | collective-permute-start | bytes 1572872 | tf_op jit(solution)/shard_map/ppermute | solution.py:725
  34.2 11.6 %collective-permute-start.7 = (bf16[2,4,208,128]{3,2,1,0:T(8,128)(2,1)S(1)}, bf16[2,4,208,128]{3,2,1,0:T(8,128)(2,1)S(1)}, u32[]{:S(2)}, u32[]{:S(2)}) collective-permute-start(bf16[2,4,208,128]{3,2,1,0:T(8,128)(2,1)S(1)} %get-tuple-element.142), channel_id=1, source_target_pairs={{0,4},{1,5},{2,6},{3,7},{4,0},{5,1},{6,2},{7,3},{8,12},{9,13},{10,... | collective-permute-start | bytes 1277960 | tf_op jit(solution)/shard_map/ppermute | solution.py:725
  46.7 9.4 %collective-permute-start.11 = (bf16[4,256,128]{2,1,0:T(8,128)(2,1)S(1)}, bf16[4,256,128]{2,1,0:T(8,128)(2,1)S(1)}, u32[]{:S(2)}, u32[]{:S(2)}) collective-permute-start(bf16[4,256,128]{2,1,0:T(8,128)(2,1)S(1)} %get-tuple-element.156), channel_id=1, source_target_pairs={{0,4},{1,5},{2,6},{3,7},{4,0},{5,1},{6,2},{7,3},{8,12},{9,13},{10,... | collective-permute-start | bytes 786440 | tf_op jit(solution)/shard_map/ppermute | solution.py:725
  48.0 8.1 %collective-permute-start.12 = (bf16[4,208,128]{2,1,0:T(8,128)(2,1)S(1)}, bf16[4,208,128]{2,1,0:T(8,128)(2,1)S(1)}, u32[]{:S(2)}, u32[]{:S(2)}) collective-permute-start(bf16[4,208,128]{2,1,0:T(8,128)(2,1)S(1)} %get-tuple-element.157), channel_id=1, source_target_pairs={{0,2},{1,3},{2,0},{3,1},{4,6},{5,7},{6,4},{7,5},{8,10},{9,11},{10,... | collective-permute-start | bytes 638984 | tf_op jit(solution)/shard_map/ppermute | solution.py:725
  50.1 15.8 %collective-permute-start.10 = (bf16[2,4,192,128]{3,2,1,0:T(8,128)(2,1)S(1)}, bf16[2,4,192,128]{3,2,1,0:T(8,128)(2,1)S(1)}, u32[]{:S(2)}, u32[]{:S(2)}) collective-permute-start(bf16[2,4,192,128]{3,2,1,0:T(8,128)(2,1)S(1)} %get-tuple-element.154), channel_id=1, source_target_pairs={{0,4},{1,5},{2,6},{3,7},{4,0},{5,1},{6,2},{7,3},{8,12},{9,13},{10,... | collective-permute-start | bytes 1179656 | tf_op jit(solution)/shard_map/ppermute | solution.py:725
  51.5 14.5 %collective-permute-start.9 = (bf16[2,4,176,128]{3,2,1,0:T(8,128)(2,1)S(1)}, bf16[2,4,176,128]{3,2,1,0:T(8,128)(2,1)S(1)}, u32[]{:S(2)}, u32[]{:S(2)}) collective-permute-start(bf16[2,4,176,128]{3,2,1,0:T(8,128)(2,1)S(1)} %get-tuple-element.153), channel_id=1, source_target_pairs={{0,2},{1,3},{2,0},{3,1},{4,6},{5,7},{6,4},{7,5},{8,10},{9,11},{10,... | collective-permute-start | bytes 1081352 | tf_op jit(solution)/shard_map/ppermute | solution.py:725
  56.2 6.8 %collective-permute-start.13 = (bf16[2,464,128]{2,1,0:T(8,128)(2,1)S(1)}, bf16[2,464,128]{2,1,0:T(8,128)(2,1)S(1)}, u32[]{:S(2)}, u32[]{:S(2)}) collective-permute-start(bf16[2,464,128]{2,1,0:T(8,128)(2,1)S(1)} %get-tuple-element.163), channel_id=1, source_target_pairs={{0,8},{8,0},{16,24},{24,16},{1,9},{9,1},{17,25},{25,17},{2,10},{10... | collective-permute-start | bytes 712712 | tf_op jit(solution)/shard_map/ppermute | solution.py:725
  63.1 5.8 %collective-permute-start.16 = (bf16[464,128]{1,0:T(8,128)(2,1)S(1)}, bf16[464,128]{1,0:T(8,128)(2,1)S(1)}, u32[]{:S(2)}, u32[]{:S(2)}) collective-permute-start(bf16[464,128]{1,0:T(8,128)(2,1)S(1)} %get-tuple-element.170), channel_id=1, source_target_pairs={{0,16},{8,24},{16,0},{24,8},{1,17},{9,25},{17,1},{25,9},{2,18},{10... | collective-permute-start | bytes 356360 | tf_op jit(solution)/shard_map/ppermute | solution.py:725
  66.1 14.2 %collective-permute-start.15 = (bf16[4,192,128]{2,1,0:T(8,128)(2,1)S(1)}, bf16[4,192,128]{2,1,0:T(8,128)(2,1)S(1)}, u32[]{:S(2)}, u32[]{:S(2)}) collective-permute-start(bf16[4,192,128]{2,1,0:T(8,128)(2,1)S(1)} %get-tuple-element.169), channel_id=1, source_target_pairs={{0,2},{1,3},{2,0},{3,1},{4,6},{5,7},{6,4},{7,5},{8,10},{9,11},{10,... | collective-permute-start | bytes 589832 | tf_op jit(solution)/shard_map/ppermute | solution.py:725
  71.9 8.5 %collective-permute-start.14 = (bf16[4,176,128]{2,1,0:T(8,128)(2,1)S(1)}, bf16[4,176,128]{2,1,0:T(8,128)(2,1)S(1)}, u32[]{:S(2)}, u32[]{:S(2)}) collective-permute-start(bf16[4,176,128]{2,1,0:T(8,128)(2,1)S(1)} %get-tuple-element.168), channel_id=1, source_target_pairs={{0,4},{1,5},{2,6},{3,7},{4,0},{5,1},{6,2},{7,3},{8,12},{9,13},{10,... | collective-permute-start | bytes 540680 | tf_op jit(solution)/shard_map/ppermute | solution.py:725
  74.8 9.7 %collective-permute-start.21 = (bf16[2,464,128]{2,1,0:T(8,128)(2,1)S(1)}, bf16[2,464,128]{2,1,0:T(8,128)(2,1)S(1)}, u32[]{:S(2)}, u32[]{:S(2)}) collective-permute-start(bf16[2,464,128]{2,1,0:T(8,128)(2,1)S(1)} %shard_map.336.refs_0_), channel_id=1, source_target_pairs={{0,8},{8,0},{16,24},{24,16},{1,9},{9,1},{17,25},{25,17},{2,10},{10... | collective-permute-start | bytes 712712 | tf_op jit(solution)/shard_map/ppermute | solution.py:725
  80.5 7.6 %collective-permute-start.20 = (bf16[2,336,128]{2,1,0:T(8,128)(2,1)S(1)}, bf16[2,336,128]{2,1,0:T(8,128)(2,1)S(1)}, u32[]{:S(2)}, u32[]{:S(2)}) collective-permute-start(bf16[2,336,128]{2,1,0:T(8,128)(2,1)S(1)} %get-tuple-element.179), channel_id=1, source_target_pairs={{0,8},{8,0},{16,24},{24,16},{1,9},{9,1},{17,25},{25,17},{2,10},{10... | collective-permute-start | bytes 516104 | tf_op jit(solution)/shard_map/ppermute | solution.py:725
  84.5 26.2 %collective-permute-start.30 = (bf16[4,464,128]{2,1,0:T(8,128)(2,1)S(1)}, bf16[4,464,128]{2,1,0:T(8,128)(2,1)S(1)}, u32[]{:S(2)}, u32[]{:S(2)}) collective-permute-start(bf16[4,464,128]{2,1,0:T(8,128)(2,1)S(1)} %shard_map.338.refs_0_), channel_id=1, source_target_pairs={{0,4},{1,5},{2,6},{3,7},{4,0},{5,1},{6,2},{7,3},{8,12},{9,13},{10,... | collective-permute-start | bytes 1425416 | tf_op jit(solution)/shard_map/ppermute | solution.py:725
  85.3 25.4 %collective-permute-start.29 = (bf16[4,464,128]{2,1,0:T(8,128)(2,1)S(1)}, bf16[4,464,128]{2,1,0:T(8,128)(2,1)S(1)}, u32[]{:S(2)}, u32[]{:S(2)}) collective-permute-start(bf16[4,464,128]{2,1,0:T(8,128)(2,1)S(1)} %shard_map.338.refs_0_), channel_id=1, source_target_pairs={{0,2},{1,3},{2,0},{3,1},{4,6},{5,7},{6,4},{7,5},{8,10},{9,11},{10,... | collective-permute-start | bytes 1425416 | tf_op jit(solution)/shard_map/ppermute | solution.py:725
  86.9 23.8 %collective-permute-start.28 = (bf16[4,464,128]{2,1,0:T(8,128)(2,1)S(1)}, bf16[4,464,128]{2,1,0:T(8,128)(2,1)S(1)}, u32[]{:S(2)}, u32[]{:S(2)}) collective-permute-start(bf16[4,464,128]{2,1,0:T(8,128)(2,1)S(1)} %shard_map.338.refs_0_), channel_id=1, source_target_pairs={{0,6},{1,7},{2,4},{3,5},{4,2},{5,3},{6,0},{7,1},{8,14},{9,15},{10,... | collective-permute-start | bytes 1425416 | tf_op jit(solution)/shard_map/ppermute | solution.py:725
  99.0 5.9 %collective-permute-start.24 = (bf16[2,336,128]{2,1,0:T(8,128)(2,1)S(1)}, bf16[2,336,128]{2,1,0:T(8,128)(2,1)S(1)}, u32[]{:S(2)}, u32[]{:S(2)}) collective-permute-start(bf16[2,336,128]{2,1,0:T(8,128)(2,1)S(1)} %shard_map.341.refs_0_), channel_id=1, source_target_pairs={{0,8},{8,0},{16,24},{24,16},{1,9},{9,1},{17,25},{25,17},{2,10},{10... | collective-permute-start | bytes 516104 | tf_op jit(solution)/shard_map/ppermute | solution.py:725
  105.7 10.9 %collective-permute-start.31 = (bf16[4,464,128]{2,1,0:T(8,128)(2,1)S(1)}, bf16[4,464,128]{2,1,0:T(8,128)(2,1)S(1)}, u32[]{:S(2)}, u32[]{:S(2)}) collective-permute-start(bf16[4,464,128]{2,1,0:T(8,128)(2,1)S(1)} %shard_map.338.refs_0_), channel_id=1, source_target_pairs={{0,1},{1,0},{2,3},{3,2},{4,5},{5,4},{6,7},{7,6},{8,9},{9,8},{10,11... | collective-permute-start | bytes 1425416 | tf_op jit(solution)/shard_map/ppermute | solution.py:725
  110.7 6.1 %collective-permute-start.32 = (bf16[4,464,128]{2,1,0:T(8,128)(2,1)S(1)}, bf16[4,464,128]{2,1,0:T(8,128)(2,1)S(1)}, u32[]{:S(2)}, u32[]{:S(2)}) collective-permute-start(bf16[4,464,128]{2,1,0:T(8,128)(2,1)S(1)} %collective-permute-done.29.refs_1_), channel_id=1, source_target_pairs={{0,1},{1,0},{2,3},{3,2},{4,5},{5,4},{6,7},{7,6},{8,9},{9,8},{10,11... | collective-permute-start | bytes 1425416 | tf_op jit(solution)/shard_map/ppermute | solution.py:725
  114.3 10.9 %collective-permute-start.27 = (bf16[4,336,128]{2,1,0:T(8,128)(2,1)S(1)}, bf16[4,336,128]{2,1,0:T(8,128)(2,1)S(1)}, u32[]{:S(2)}, u32[]{:S(2)}) collective-permute-start(bf16[4,336,128]{2,1,0:T(8,128)(2,1)S(1)} %shard_map.342.refs_0_), channel_id=1, source_target_pairs={{0,4},{1,5},{2,6},{3,7},{4,0},{5,1},{6,2},{7,3},{8,12},{9,13},{10,... | collective-permute-start | bytes 1032200 | tf_op jit(solution)/shard_map/ppermute | solution.py:725
  116.6 10.9 %collective-permute-start.26 = (bf16[4,336,128]{2,1,0:T(8,128)(2,1)S(1)}, bf16[4,336,128]{2,1,0:T(8,128)(2,1)S(1)}, u32[]{:S(2)}, u32[]{:S(2)}) collective-permute-start(bf16[4,336,128]{2,1,0:T(8,128)(2,1)S(1)} %shard_map.342.refs_0_), channel_id=1, source_target_pairs={{0,2},{1,3},{2,0},{3,1},{4,6},{5,7},{6,4},{7,5},{8,10},{9,11},{10,... | collective-permute-start | bytes 1032200 | tf_op jit(solution)/shard_map/ppermute | solution.py:725
  116.9 17.0 %collective-permute-start.25 = (bf16[4,336,128]{2,1,0:T(8,128)(2,1)S(1)}, bf16[4,336,128]{2,1,0:T(8,128)(2,1)S(1)}, u32[]{:S(2)}, u32[]{:S(2)}) collective-permute-start(bf16[4,336,128]{2,1,0:T(8,128)(2,1)S(1)} %shard_map.342.refs_0_), channel_id=1, source_target_pairs={{0,6},{1,7},{2,4},{3,5},{4,2},{5,3},{6,0},{7,1},{8,14},{9,15},{10,... | collective-permute-start | bytes 1032200 | tf_op jit(solution)/shard_map/ppermute | solution.py:725
  118.1 16.3 %collective-permute-start.35 = (bf16[4,336,128]{2,1,0:T(8,128)(2,1)S(1)}, bf16[4,336,128]{2,1,0:T(8,128)(2,1)S(1)}, u32[]{:S(2)}, u32[]{:S(2)}) collective-permute-start(bf16[4,336,128]{2,1,0:T(8,128)(2,1)S(1)} %shard_map.342.refs_0_), channel_id=1, source_target_pairs={{0,1},{1,0},{2,3},{3,2},{4,5},{5,4},{6,7},{7,6},{8,9},{9,8},{10,11... | collective-permute-start | bytes 1032200 | tf_op jit(solution)/shard_map/ppermute | solution.py:725
  (17 other events, 61.9 us)

commit v3 on v2

--- a/solution.py
+++ b/solution.py
@@ -277,16 +277,18 @@
     inner[HALO:] = pooled[POOLED:]
 
 
-def project_kernel(
-    levels,
-    tokens, gain, shift, query_w, query_b, key_w, value_w, value_b, out_w, up_w, down_w, cotangent,
-    normed_out, query_out, key_out, value_out, key_pool, value_pool, out_copy, up_copy, down_copy,
-    cot_copy, sem,
-):
-    pairs = ((out_w, out_copy), (up_w, up_copy), (down_w, down_copy), (cotangent, cot_copy))
-    copies = [pltpu.make_async_copy(*pair, sem.at[n]) for n, pair in enumerate(pairs)]
+def project_kernel(levels, count, *refs):
+    sources, refs = refs[:count], refs[count:]
+    held, (normed_out, query_out, key_out, value_out, key_pool, value_pool, sem) = (
+        refs[:count],
+        refs[count:],
+    )
+    copies = [pltpu.make_async_copy(*pair, sem.at[n]) for n, pair in enumerate(zip(sources, held))]
     for copy in copies:
         copy.start()
+    tokens, gain, shift, query_w, query_b, key_w, value_w, value_b = [
+        Fetched(ref, copy) for ref, copy in zip(held[:8], copies[:8])
+    ]
     normed, _ = normalize(tokens[0].astype(F32))
     rows = (normed * gain[...] + shift[...]).astype(BF16)
     normed_out[...] = rows
@@ -299,7 +301,7 @@
     value = (dot(rows, value_w[...]) + value_b[...]).astype(BF16)
     value_out[...] = value
     value_pool[...] = dot(pool, value).astype(BF16)
-    for copy in copies:
+    for copy in copies[8:]:
         copy.wait()
 
 
@@ -315,16 +317,26 @@
 
 def middle_kernel(
     levels, holders, parts,
-    starts, tokens, cotangent, query, key, value, key_pool, value_pool, inner, outer,
-    gain, shift, key_w, value_w, value_b, out_w, out_b, gain2, shift2, up_w, up_b,
-    down_w, down_b, bias_table, codes, *refs,
+    starts, tokens, query, key, value, key_pool, value_pool, inner, outer,
+    gain, shift, key_w, value_w, value_b, out_b, gain2, shift2, up_b, bias_table, codes,
+    out_source, up_source, cot_source, down_source, *refs,
 ):
     windows, refs = refs[:parts], refs[parts:]
     (
-    output, attended_out, weights_out, halo_out, key_halo, value_halo, mid_out, grad_second_out,
-    late_out, keep, send,
-    key_cat, value_cat, attended, sums, small, sem,
+    attended_out, weights_out, halo_out, key_halo, value_halo, mid_out, second_out, active_out,
+    slope_out, keep, send, out_held, up_held, cot_held, down_held,
+    key_cat, value_cat, attended, sums, small, sem, sources_sem,
     ) = refs
+    pairs = (
+        (out_source, out_held), (up_source, up_held), (cot_source, cot_held),
+        (down_source, down_held),
+    )
+    brought = []
+    for number, pair in enumerate(pairs):
+        copy = pltpu.make_async_copy(*pair, sources_sem.at[number])
+        copy.start()
+        brought.append(Fetched(pair[1], copy))
+    out_w, up_w, cotangent, down_w = brought
     width = tokens.shape[2]
     place = lax.axis_index("seq")
     low, high = item_bounds(starts, place)
@@ -380,71 +392,81 @@
     low_second = (normed * gain2[...] + shift2[...]).astype(BF16)
     cot = cotangent[0]
     hidden = up_w.shape[1]
-    small[...] = jnp.zeros_like(small)
-
-    def put(row, vector):
-        for part in range(vector.shape[1] // 128):
-            small[row + part : row + part + 1] = vector[:, 128 * part : 128 * (part + 1)]
-
-    result = mid + down_b[...]
-    grad_second = jnp.zeros((ROWS, width), F32)
-    step = width
-    for at in range(0, hidden, step):
-        cols = slice(at, at + step)
+    mid_out[...] = mid
+    second_out[...] = low_second
+    for at in range(0, hidden, width):
+        cols = slice(at, at + width)
         upper = dot(low_second, up_w[:, cols]) + up_b[:, cols]
         below, phi = normal_parts(upper)
+        slope_out[:, cols] = below + upper * phi
         active = (upper * below).astype(BF16)
-        result = result + dot(active, down_w[cols])
+        active_out[:, cols] = active
         grad_down = dot_rows(active, cot).astype(BF16)
-        for piece in range(at // 64, (at + step) // 64):
+        for piece in range(at // 64, (at + width) // 64):
             row = 64 * piece - at
             for part in range(width // 128):
                 sums[slot_of(piece), 64 * part : 64 * (part + 1)] = grad_down[
                     row : row + 64, 128 * part : 128 * (part + 1)
                 ]
-        grad_active = dot_cols(cot, down_w[cols])
-        grad_upper = grad_active * (below + upper * phi)
-        low_upper = grad_upper.astype(BF16)
-        put(4 + at // 128, jnp.sum(low_upper.astype(F32), axis=0, keepdims=True))
-        grad_up = dot_rows(low_second, low_upper).astype(BF16)
-        if at >= EARLY_UP:
-            late_out[:, at - EARLY_UP : at - EARLY_UP + step] = grad_up
-        else:
-            put_lines(sums, 256 + 16 * (at // 128), grad_up)
-        grad_second = grad_second + dot_cols(low_upper, up_w[:, cols])
-
+    small[...] = jnp.zeros_like(small)
+    put_vector(small, 0, jnp.sum(cot.astype(F32), axis=0, keepdims=True))
+    put_small(sums, 256, small)
+    down_w.wait()
+    hand_out(sums, keep, [send], sem)
+
+
+def feed_kernel(
+    cotangent, mid, low_second, active, slope, gain2, up_w, down_w, down_b, out_w, attended,
+    output, grad_mid_out, grad_attended, grad_out, out_b_sum, keep, *refs,
+):
+    sends, (sums, small, sem) = refs[:-3], refs[-3:]
+    cot = cotangent[0]
+    hidden, width = down_w.shape
+    result = mid[...] + down_b[...]
+    grad_second = jnp.zeros((ROWS, width), F32)
+    small[...] = jnp.zeros_like(small)
+    for at in range(0, hidden, width):
+        cols = slice(at, at + width)
+        result = result + dot(active[:, cols], down_w[cols])
+        grad_upper = (dot_cols(cot, down_w[cols]) * slope[:, cols]).astype(BF16)
+        put_vector(small, at // 128, jnp.sum(grad_upper.astype(F32), axis=0, keepdims=True))
+        put_lines(sums, at // 8, dot_rows(low_second[...], grad_upper).astype(BF16))
+        grad_second = grad_second + dot_cols(grad_upper, up_w[:, cols])
     output[0] = result.astype(BF16)
-    put(0, jnp.sum(cot.astype(F32), axis=0, keepdims=True))
-    mid_out[...] = mid
-    grad_second_out[...] = grad_second
-    put_small(sums, FIRST_ROWS - SMALL, small)
-    hand_out(sums, keep, send, sem)
-
-
-def branch_kernel(
-    cotangent, mid, grad_second, gain2, attended, out_w,
-    grad_mid_out, grad_attended, grad_out, vectors,
-):
     normed, scale = normalize(mid[...])
-    grad = grad_second[...]
-    grad_mid = cotangent[0].astype(F32) + norm_back(grad * gain2[...], normed, scale)
+    put_vector(small, 16, jnp.sum(grad_second * normed, axis=0, keepdims=True))
+    put_vector(small, 20, jnp.sum(grad_second, axis=0, keepdims=True))
+    put_small(sums, 256, small)
+    grad_mid = cot.astype(F32) + norm_back(grad_second * gain2[...], normed, scale)
     grad_mid_out[...] = grad_mid
     branch = grad_mid.astype(BF16)
     grad_attended[...] = dot_cols(branch, out_w[...]).astype(BF16)
     grad_out[...] = dot_rows(attended[...], branch).astype(BF16)
-    vectors[0:1] = jnp.sum(branch.astype(F32), axis=0, keepdims=True)
-    vectors[1:2] = jnp.sum(grad * normed, axis=0, keepdims=True)
-    vectors[2:3] = jnp.sum(grad, axis=0, keepdims=True)
-
-
-EARLY_UP = 1536
-FIRST_ROWS = 256 + 192 + SMALL
-SECOND_ROWS = 5 * 64 + SMALL
-FIRST_CUT, SECOND_CUT = 256, 176
+    out_b_sum[...] = jnp.sum(branch.astype(F32), axis=0, keepdims=True)
+    hand_out(sums, keep, sends, sem)
+
+
+FEED, BACK, BORROWED, LAST = "feed", "back", "borrowed", "last"
+ORDER = (FEED, 1, 2, BACK, 1, 2, 3, 1, BORROWED, 2, 1, 3, 2, 1, 3, 2, 1, 3, 2, 1, 3, 2, 3, LAST, 2, 1, 3, 3)
+Z_DIRECT = True
+GROUP_ROWS = 256 + SMALL
+MID_PARTS, LATE_PARTS = 2, 4
+
+
+def put_vector(small, row, vector):
+    for part in range(vector.shape[1] // 128):
+        small[row + part : row + part + 1] = vector[:, 128 * part : 128 * (part + 1)]
+
+
+def turned(place):
+    return (place & 4) * 2 + (place // 2 & 4) + (place & 3)
 
 
 def slot_of(piece):
-    return (piece // 16) * 16 + jnp.bitwise_xor(my_piece() % 16, piece % 16)
+    mine, place = my_piece() % 16, piece % 16
+    if piece // 16 == 1:
+        mine, place = turned(mine), turned(place)
+    return (piece // 16) * 16 + jnp.bitwise_xor(mine, place)
 
 
 def put_lines(sums, base, grad):
@@ -466,13 +488,14 @@
         sums[slot_of(piece), row : row + SMALL] = part
 
 
-def hand_out(sums, keep, send, sem):
+def hand_out(sums, keep, sends, sem):
     mine = my_piece() // 16
     half = PIECES // 2
-    copies = [
-        pltpu.make_async_copy(sums.at[pl.ds(mine * half, half)], keep, sem.at[0]),
-        pltpu.make_async_copy(sums.at[pl.ds((1 - mine) * half, half)], send, sem.at[1]),
-    ]
+    count = half // len(sends)
+    copies = [pltpu.make_async_copy(sums.at[pl.ds(mine * half, half)], keep, sem.at[0])]
+    for number, send in enumerate(sends):
+        rows = pl.ds((1 - mine) * half + number * count, count)
+        copies.append(pltpu.make_async_copy(sums.at[rows], send, sem.at[1 + number]))
     for copy in copies:
         copy.start()
     for copy in copies:
@@ -482,10 +505,10 @@
 def back_kernel(
     levels, holders,
     tokens, normed_low, query, key, value, key_pool, value_pool, halo, key_halo, value_halo,
-    weights, grad_attended, grad_out, late, vectors, gain, shift, query_w, key_w, value_w,
-    grad_normed_out, inner, outer, keep, send, *refs,
+    weights, grad_attended, grad_out, out_b_sum, gain, shift, query_w, key_w, value_w,
+    grad_normed_out, inner, outer, keep, *refs,
 ):
-    owners, refs = refs[:-12], refs[-12:]
+    sends, owners, refs = refs[:LATE_PARTS], refs[LATE_PARTS:-12], refs[-12:]
     (
     key_cat, value_cat, grad_query, key_own, key_pooled, key_lent, value_own, value_pooled,
     value_lent, sums, small, sem,
@@ -533,19 +556,13 @@
     lent_low = (lent_normed * gain[...] + shift[...]).astype(BF16)
     rows = normed_low[...]
 
-    put_lines(sums, 0, late[...])
-    put_lines(sums, 64, grad_out[...])
-    put_lines(sums, 128, dot_rows(rows, low_query).astype(BF16))
+    put_lines(sums, 0, grad_out[...])
+    put_lines(sums, 64, dot_rows(rows, low_query).astype(BF16))
     grad_key = dot_rows(rows, low_key) + dot_rows(lent_low, lent_key)
-    put_lines(sums, 192, grad_key.astype(BF16))
+    put_lines(sums, 128, grad_key.astype(BF16))
     grad_value = dot_rows(rows, low_value) + dot_rows(lent_low, lent_value)
-    put_lines(sums, 256, grad_value.astype(BF16))
-
+    put_lines(sums, 192, grad_value.astype(BF16))
     small[...] = jnp.zeros_like(small)
-
-    def put(row, vector):
-        for part in range(vector.shape[1] // 128):
-            small[row + part : row + part + 1] = vector[:, 128 * part : 128 * (part + 1)]
 
     def total(values):
         return jnp.sum(values.astype(F32), axis=0, keepdims=True)
@@ -558,13 +575,11 @@
     )
     lent_grad = dot_cols(lent_key, key_w[...]) + dot_cols(lent_value, value_w[...])
     grad_normed_out[...] = grad_normed
-    put(0, total(low_query))
-    put(4, total(low_value) + total(lent_value))
-    put(8, vectors[0:1])
-    put(20, vectors[1:2])
-    put(24, vectors[2:3])
-    put(12, total(grad_normed * normed) + total(lent_grad * lent_normed))
-    put(16, total(grad_normed) + total(lent_grad))
+    put_vector(small, 0, total(low_query))
+    put_vector(small, 4, total(low_value) + total(lent_value))
+    put_vector(small, 8, out_b_sum[...])
+    put_vector(small, 12, total(grad_normed * normed) + total(lent_grad * lent_normed))
+    put_vector(small, 16, total(grad_normed) + total(lent_grad))
     lent_grad = lent_grad.astype(BF16)
     even = place % 2 == 0
     inner[...] = jnp.where(even, lent_grad[HALO : 2 * HALO], lent_grad[:HALO])
@@ -577,12 +592,13 @@
         for plane in range(4):
             for other in range(2):
                 core = (place + other) % 2
+                at = jnp.where(core == 1, turned(4 * plane), 4 * plane)
                 rows = returned[GATHER * (2 * plane + other) :][:GATHER]
                 for part in range(4):
-                    slot = core * 16 + plane * 4 + part
-                    sums[slot, SECOND_ROWS:] = rows[:, 128 * part : 128 * (part + 1)]
-    put_small(sums, SECOND_ROWS - SMALL, small)
-    hand_out(sums, keep, send, sem)
+                    slot = core * 16 + at + part
+                    sums[slot, GROUP_ROWS:] = rows[:, 128 * part : 128 * (part + 1)]
+    put_small(sums, 256, small)
+    hand_out(sums, keep, sends, sem)
 
 
 def last_kernel(levels, tokens, gain, grad_mid, grad_normed, inner, outer, *refs):
@@ -611,50 +627,44 @@
 
 
 def collect_kernel(kind, *refs):
-    blocks, refs = refs[:8], refs[8:]
-    small = refs[-1]
+    blocks, refs, small = refs[:4], refs[4:-1], refs[-1]
     me = my_piece()
-    if kind == 1:
-        down, up, *order = refs[:-1]
-        lined = [(up, 256, 12)]
-        small_row = FIRST_ROWS - SMALL
-    else:
-        whole_up, out, query, key, value, *order, up, sem = refs[1:-1]
-        lined = [(up, 0, 4), (out, 64, 4), (query, 128, 4), (key, 192, 4), (value, 256, 4)]
-        small_row = SECOND_ROWS - SMALL
+    squares = 4 if kind == 2 else 1
+    grads, order = refs[:squares], refs[squares:]
+
     for core in range(2):
+        odd = (me // 16 + core) % 2 == 1
         for plane in range(4):
             for depth in range(4):
-                piece = jnp.bitwise_xor(me, core * 16 + plane * 4 + depth)
-                block = blocks[core * 4 + plane]
-                if kind == 1:
+                place = 4 * plane + depth
+                place = jnp.where(odd, turned(place), place)
+                piece = jnp.bitwise_xor(me, core * 16 + place)
+                block = blocks[2 * core + plane % 2]
+
+                def held(row, rows, block=block, plane=plane, depth=depth):
+                    return block[plane // 2, depth, row : row + rows].astype(F32)
+
+                lines = pl.ds(pl.multiple_of(piece * 16, 16), 16)
+                if kind == 0:
+                    (down,) = grads
                     rows = pl.ds(pl.multiple_of(piece * 64, 64), 64)
                     for part in range(down.shape[1] // 128):
-                        down[rows, 128 * part : 128 * (part + 1)] = block[
-                            depth, 64 * part : 64 * (part + 1)
-                        ].astype(F32)
-                lines = pl.ds(pl.multiple_of(piece * 16, 16), 16)
-                for grad, base, parts in lined:
-                    for part in range(parts):
-                        row = base + 16 * part
-                        grad[lines, 128 * part : 128 * (part + 1)] = block[
-                            depth, row : row + 16
-                        ].astype(F32)
+                        down[rows, 128 * part : 128 * (part + 1)] = held(64 * part, 64)
+                else:
+                    base = 0
+                    for grad in grads:
+                        for part in range(grad.shape[1] // 128):
+                            grad[lines, 128 * part : 128 * (part + 1)] = held(base, 16)
+                            base += 16
 
                 @pl.when(piece < 2)
-                def _(block=block, depth=depth, lines=lines):
-                    small[lines] = block[depth, small_row : small_row + SMALL].astype(F32)
-
-    if kind == 2:
-        late = whole_up.shape[1] - up.shape[1]
-        copy = pltpu.make_async_copy(up, whole_up.at[:, pl.ds(late, up.shape[1])], sem)
-        copy.start()
+                def _(held=held, lines=lines):
+                    small[lines] = held(256, SMALL)
+
     at = 0
     for ref in order:
         ref[...] = small[at : at + ref.shape[0]]
         at += ref.shape[0]
-    if kind == 2:
-        copy.wait()
 
 
 class Fetched:
@@ -674,49 +684,27 @@
 
 
 def call(
-    kernel, inputs, outputs, scratch=(), smem=0, flops=0, room=16, fetch=(), far_in=(), far_out=(),
-    alias=None, pinned=(),
+    kernel, inputs, outputs, scratch=(), smem=0, room=16, far_in=(), far_out=(), alias=None, pinned=()
 ):
-    count_in, count_out = len(inputs), len(outputs)
     inputs = list(inputs)
-    for at in (*fetch, *pinned):
-        inputs[at] = pltpu.with_memory_space_constraint(inputs[at], pltpu.HBM)
-    in_space = [pltpu.SMEM] * smem + [pltpu.VMEM] * (count_in - smem)
-    out_space = [pltpu.VMEM] * count_out
-    for at in fetch:
-        in_space[at] = pltpu.HBM
+    in_space = [pltpu.SMEM] * smem + [pltpu.VMEM] * (len(inputs) - smem)
+    out_space = [pltpu.VMEM] * len(outputs)
     for at in far_in:
         in_space[at] = pl.ANY
+    for at in pinned:
+        inputs[at] = pltpu.with_memory_space_constraint(inputs[at], pltpu.HBM)
+        in_space[at] = pltpu.HBM
     for at in far_out:
         out_space[at] = pl.ANY
-    size = sum(math.prod(s) * jnp.dtype(d).itemsize for s, d in outputs)
-    size += sum(math.prod(a.shape) * a.dtype.itemsize for a in inputs)
-    buffers = [pltpu.VMEM(inputs[at].shape, inputs[at].dtype) for at in fetch]
-    if fetch:
-        buffers.append(pltpu.SemaphoreType.DMA((len(fetch),)))
-
-    def with_copies(*refs):
-        refs = list(refs)
-        if fetch:
-            held, sem = refs[-len(fetch) - 1 : -1], refs[-1]
-            refs = refs[: -len(fetch) - 1]
-            for number, at in enumerate(fetch):
-                copy = pltpu.make_async_copy(refs[at], held[number], sem.at[number])
-                copy.start()
-                refs[at] = Fetched(held[number], copy)
-        kernel(*refs)
-        for at in fetch:
-            refs[at].wait()
-
     return pl.pallas_call(
-        with_copies,
+        kernel,
         out_shape=[jax.ShapeDtypeStruct(s, d) for s, d in outputs],
         in_specs=[pl.BlockSpec(memory_space=s) for s in in_space],
         out_specs=[pl.BlockSpec(memory_space=s) for s in out_space],
-        scratch_shapes=[pltpu.VMEM(*s) if isinstance(s, tuple) else s for s in scratch] + buffers,
+        scratch_shapes=[pltpu.VMEM(*s) if isinstance(s, tuple) else s for s in scratch],
         input_output_aliases=alias or {},
         compiler_params=pltpu.CompilerParams(vmem_limit_bytes=room * 1024 * 1024),
-        cost_estimate=pl.CostEstimate(flops=flops, bytes_accessed=size, transcendentals=0),
+        cost_estimate=pl.CostEstimate(flops=0, bytes_accessed=0, transcendentals=0),
     )(*inputs)
 
 
@@ -735,10 +723,16 @@
     return lax.optimization_barrier((value, others))[0]
 
 
-def planes(parts):
-    if not isinstance(parts, (list, tuple)):
-        parts = [parts] * 4
-    return [swap(parts[plane], "seq", 2 * plane) for plane in (3, 1, 2)]
+def planes(array):
+    return [swap(array, "seq", 2 * plane) for plane in (3, 1, 2)]
+
+
+def hop(array, step):
+    pairs = []
+    for place in range(lax.axis_size("seq")):
+        bit = 2 << (step if place % 2 == 0 else 1 - step)
+        pairs.append((place, place ^ bit))
+    return lax.ppermute(array, "seq", pairs)
 
 
 def sum_of(*values):
@@ -748,105 +742,146 @@
     return total.astype(BF16)
 
 
-def cores_kernel(cut, keep, other, *outs):
-    ways = ((slice(cut), ((1, 3), (0, 2))), (slice(cut, None), ((2, 3), (0, 1))))
-    for way, (rows, groups) in enumerate(ways):
-        for number, group in enumerate(groups):
-            for at, plane in enumerate(group):
-                for depth in range(4):
-                    slot = 4 * plane + depth
-                    outs[2 * way + number][at, depth] = sum_of(keep[slot, rows], other[slot, rows])
-
-
-def add_cores(keep, other, cut):
-    rows = keep.shape[1]
-    shapes = [(2, 4, cut, 128)] * 2 + [(2, 4, rows - cut, 128)] * 2
-    kernel = functools.partial(cores_kernel, cut)
-    return call(kernel, (keep, other), [(s, BF16) for s in shapes], room=12)
-
-
-def step_one(parts):
-    return [swap(parts[0], "seq", 2), swap(parts[2], "seq", 4)]
-
-
-def step_two(parts):
-    return [swap(parts[0], "seq", 4), swap(parts[2], "seq", 2)]
-
-
-def step_one_kernel(first, first_came, last, last_came, *outs):
-    for way, (kept, came) in enumerate(((first, first_came), (last, last_came))):
-        for number, plane in enumerate((1, 0)):
-            for depth in range(4):
-                outs[2 * way + number][depth] = sum_of(kept[plane, depth], came[plane, depth])
-
-
-def add_step_one(parts, came):
-    inputs = (parts[1], came[0], parts[3], came[1])
-    shapes = [(parts[0].shape[1:], BF16)] * 2 + [(parts[2].shape[1:], BF16)] * 2
-    return call(step_one_kernel, inputs, shapes, room=8)
-
-
-def step_two_kernel(first, first_came, last, last_came, *outs):
-    cut, rows = first.shape[1], outs[0].shape[1]
+def halves_kernel(kept, *refs):
+    came, (sent_out, kept_out) = refs[:-2], refs[-2:]
+    each = kept.shape[0] // len(came)
+    for slot in range(kept.shape[0]):
+        out = (kept_out, sent_out)[slot % 2]
+        out[slot // 2] = sum_of(kept[slot], came[slot // each][slot % each])
+
+
+def add_halves(kept, *came):
+    shape = (kept.shape[0] // 2, *kept.shape[1:])
+    return call(halves_kernel, (kept, *came), [(shape, BF16)] * 2, room=12)
+
+
+def plane_kernel(extra, kept, came, sent_out, kept_out, *complete):
+    rows = kept.shape[1] - extra
     for depth in range(4):
-        out = outs[1 - depth % 2]
-        out[depth // 2, 0:cut] = sum_of(first[depth], first_came[depth])
-        out[depth // 2, cut:] = sum_of(last[depth, : rows - cut], last_came[depth, : rows - cut])
-        if len(outs) > 2:
-            outs[2][depth] = sum_of(last[depth, rows - cut :], last_came[depth, rows - cut :])
-
-
-def add_step_two(parts, came, extra=0):
-    rows = parts[0].shape[1] + parts[2].shape[1] - extra
-    inputs = (parts[1], came[0], parts[3], came[1])
+        total = sum_of(kept[depth], came[depth])
+        (kept_out, sent_out)[depth % 2][depth // 2] = total[:rows]
+        if extra:
+            complete[0][depth] = total[rows:]
+
+
+def add_plane(kept, came, extra):
+    rows = kept.shape[1] - extra
     outputs = [((2, rows, 128), BF16)] * 2
     if extra:
         outputs.append(((4, extra, 128), BF16))
-    return call(step_two_kernel, inputs, outputs, room=8)
-
-
-def near_kernel(kept, came, sent, mine):
-    mine[...] = sum_of(kept[0], came[0])
-    sent[...] = sum_of(kept[1], came[1])
-
-
-def add_near(kept, came):
-    return call(near_kernel, (kept, came), [(kept.shape[1:], BF16)] * 2, room=8)
-
-
-def far_kernel(mine, came, whole):
-    whole[...] = sum_of(mine[...], came[...])
-
-
-def add_far(mine, came):
-    (whole,) = call(far_kernel, (mine, came), [(mine.shape, BF16)], room=8)
+    return call(functools.partial(plane_kernel, extra), (kept, came), outputs, room=8)
+
+
+def plane_direct_kernel(extra, kept, came, *outs):
+    rows = kept.shape[1] - extra
+    for depth in range(4):
+        total = sum_of(kept[depth], came[depth])
+        outs[depth][...] = total[:rows]
+        if extra:
+            outs[4][depth] = total[rows:]
+
+
+def add_plane_direct(kept, came, extra):
+    rows = kept.shape[1] - extra
+    outputs = [((rows, 128), BF16)] * 4
+    if extra:
+        outputs.append(((4, extra, 128), BF16))
+    outs = call(functools.partial(plane_direct_kernel, extra), (kept, came), outputs, room=8)
+    return [*outs[:4], list(outs[4:])]
+
+
+def column_kernel(whole, two, three, one, out):
+    for depth, ref in enumerate((whole, one, two, three)):
+        out[0, depth] = ref[...]
+
+
+def column_of(whole, came):
+    (column,) = call(column_kernel, (whole, *came), [((1, 4, *whole.shape), BF16)], room=8)
+    return column
+
+
+def whole_kernel(*refs):
+    refs[-1][...] = sum_of(*[ref[...] for ref in refs[:-1]])
+
+
+def add_whole(mine, *came):
+    (whole,) = call(whole_kernel, (mine, *came), [(mine.shape, BF16)], room=8)
     distance = 8
     while distance < lax.axis_size("seq"):
         other = swap(whole, "seq", distance)
-        (whole,) = call(far_kernel, (whole, other), [(mine.shape, BF16)], room=8)
+        (whole,) = call(whole_kernel, (whole, other), [(mine.shape, BF16)], room=8)
         distance *= 2
     return whole
 
 
-def pair_kernel(one, two, out):
-    out[0] = one[...]
-    out[1] = two[...]
-
-
-def pair_of(one, two):
-    (pair,) = call(pair_kernel, (one, two), [((2, *one.shape), BF16)], room=8)
-    return pair
-
-
-def column_kernel(pair, came, out):
-    for far in range(2):
-        out[2 * far] = pair[far]
-        out[2 * far + 1] = came[far]
-
-
-def column_of(pair, came):
-    (column,) = call(column_kernel, (pair, came), [((4, *pair.shape[1:]), BF16)], room=8)
-    return column
+def joined_kernel(mine, came, out):
+    for slot in range(mine.shape[0]):
+        out[2 * slot] = mine[slot]
+        out[2 * slot + 1] = came[slot]
+
+
+def join(mine, came):
+    (out,) = call(joined_kernel, (mine, came), [((2 * mine.shape[0], *mine.shape[1:]), BF16)], room=8)
+    return out
+
+
+class Group:
+    def __init__(self, keep, sends):
+        self.kept = slots(keep)
+        self.came = [slots(swap(send, "seq", 1)) for send in sends]
+        self.stage = 0
+        self.users = []
+
+    def step(self, last, extra):
+        stage, kept = self.stage, self.kept
+        came = after(self.came, last)
+        self.stage += 1
+        if stage == 0:
+            sent, self.kept = add_halves(kept, *came)
+            self.came = hop(sent, 0)
+        elif stage == 1:
+            sent, kept = add_halves(kept, came)
+            self.kept = kept[0]
+            self.came = hop(sent[0], 1)
+        elif stage == 2 and Z_DIRECT:
+            *self.kept, self.users = add_plane_direct(kept, came, extra)
+            self.came = [swap(self.kept[depth], "batch", depth) for depth in (2, 3, 1)]
+            self.stage = 4
+        elif stage == 4 and Z_DIRECT:
+            self.kept = add_whole(kept[0], *came)
+            self.came = [swap(self.kept, "batch", depth) for depth in (2, 3, 1)]
+            self.stage = 6
+        elif stage == 6 and Z_DIRECT:
+            self.kept = column_of(kept, came)
+            self.came = hop(self.kept, 1)
+        elif stage == 2:
+            sent, self.kept, *self.users = add_plane(kept, came, extra)
+            self.came = swap(sent, "batch", 1)
+        elif stage == 3:
+            sent, kept = add_halves(kept, came)
+            self.kept = kept[0]
+            self.came = swap(sent[0], "batch", 2)
+        elif stage == 4:
+            self.kept = add_whole(kept, came)[None]
+            self.came = swap(self.kept, "batch", 2)
+        elif stage == 5:
+            self.kept = join(kept, came)
+            self.came = swap(self.kept, "batch", 1)
+        elif stage == 6:
+            self.kept = join(kept, came)[None]
+            self.came = hop(self.kept, 1)
+        elif stage == 7:
+            self.kept = join(kept, came)
+            self.came = hop(self.kept, 0)
+        else:
+            self.sums = [kept, came]
+            self.sums += [swap(block, "seq", 1) for block in self.sums]
+            return came
+        return self.kept[0] if isinstance(self.kept, list) else self.kept
+
+
+def slots(array):
+    return array.reshape(-1, 4, *array.shape[1:])
 
 
 def plane_of(column, came):
@@ -876,6 +911,7 @@
     levels = (ROWS * holders // (4 * BLOCK)).bit_length() - 1
     far = 48 * (levels - LOCAL)
     lent = 2 * HALO + far
+
     cols = columns_of(levels)
     groups = (ROWS // SUB) * (HEADS // QUAD)
     bias_table = jnp.asarray(score_bias(levels))
@@ -889,177 +925,180 @@
         functools.partial(first_kernel, levels),
         (tokens,),
         [((HALO + GATHER, width), BF16), ((HALO, width), BF16)],
-        flops=4 * ROWS * ROWS * width,
         room=8,
     )
     inner_came = swap(inner, "seq", 1)
     outer_came = swap_outer(outer, "seq")
     windows = share(inner, inner_came)
-    (
-        normed_low, query, key, value, key_pool, value_pool, out_weight, up_weight, down_weight,
-        cotangent,
-    ) = call(
-        functools.partial(project_kernel, levels),
-        (
-            tokens, gain, shift, query_weight, row(query_bias), key_weight, value_weight,
-            row(value_bias), out_weight, up_weight, down_weight, cotangent,
-        ),
-        [((ROWS, width), BF16)] * 4
-        + [((POOLED, width), BF16)] * 2
-        + [(a.shape, a.dtype) for a in (out_weight, up_weight, down_weight, cotangent)],
-        scratch=[pltpu.SemaphoreType.DMA((4,))],
-        fetch=(0, 1, 2, 3, 4, 5, 6, 7),
-        far_in=(8, 9, 10, 11),
-        pinned=(8, 9, 10, 11),
-        flops=8 * ROWS * width * width,
+    carried = (
+        tokens, gain, shift, query_weight, row(query_bias), key_weight, value_weight,
+        row(value_bias), row(out_bias), row(second_gain), row(second_shift), row(up_bias),
+        row(down_bias), bias_table, codes,
+    )
+    count = len(carried)
+    *carried, normed_low, query, key, value, key_pool, value_pool = call(
+        functools.partial(project_kernel, levels, count),
+        carried,
+        [(a.shape, a.dtype) for a in carried]
+        + [((ROWS, width), BF16)] * 4
+        + [((POOLED, width), BF16)] * 2,
+        scratch=[pltpu.SemaphoreType.DMA((count,))],
+        pinned=range(count),
         room=24,
     )
+    (
+        tokens, gain, shift, query_weight, _, key_weight, value_weight, value_bias, out_bias,
+        second_gain, second_shift, up_bias, down_bias, bias_table, codes,
+    ) = carried
     extra = extra_rows(holders)
     owner_shapes = [] if extra else [((holders * GATHER, width), BF16)]
     half = PIECES // 2
-    dma_pair = pltpu.SemaphoreType.DMA((2,))
+    copies = pltpu.SemaphoreType.DMA((1 + max(MID_PARTS, LATE_PARTS),))
+
+    def piece_sums(parts, rows=GROUP_ROWS):
+        sends = [((half // parts, rows, 128), BF16)] * parts
+        return [((half, rows, 128), BF16)] + sends
+
+    sums_scratch = ((PIECES, GROUP_ROWS, 128), BF16)
+    small_scratch = ((2 * SMALL, 128), F32)
     (
-        output, attended, weights, halo, key_halo, value_halo, mid, grad_second, late, keep, send,
+        attended, weights, halo, key_halo, value_halo, mid, low_second, active, slope, keep, send,
+        out_weight, up_weight, cotangent, down_weight,
     ) = call(
         functools.partial(middle_kernel, levels, holders, len(windows)),
         (
-            item_start, tokens, cotangent, query, key, value, key_pool, value_pool, inner_came,
-            outer_came, gain, shift, key_weight, value_weight, row(value_bias), out_weight,
-            row(out_bias), row(second_gain), row(second_shift), up_weight, row(up_bias),
-            down_weight, row(down_bias), bias_table, codes, *windows,
+            item_start, tokens, query, key, value, key_pool, value_pool, inner_came, outer_came,
+            gain, shift, key_weight, value_weight, value_bias, out_bias, second_gain, second_shift,
+            up_bias, bias_table, codes, out_weight, up_weight, cotangent, down_weight, *windows,
         ),
         [
-            ((1, ROWS, width), BF16),
             ((ROWS, width), BF16),
             ((groups, QUAD * SUB, cols), BF16),
             ((lent, width), BF16),
             ((lent, width), BF16),
             ((lent, width), BF16),
             ((ROWS, width), F32),
-            ((ROWS, width), F32),
-            ((width, hidden - EARLY_UP), BF16),
-            ((half, FIRST_ROWS, 128), BF16),
-            ((half, FIRST_ROWS, 128), BF16),
-        ],
+            ((ROWS, width), BF16),
+            ((ROWS, hidden), BF16),
+            ((ROWS, hidden), F32),
+        ]
+        + piece_sums(1)
+        + [(a.shape, a.dtype) for a in (out_weight, up_weight, cotangent, down_weight)],
         scratch=[
             ((cols, width), BF16),
             ((cols, width), BF16),
             ((ROWS, width), BF16),
-            ((PIECES, FIRST_ROWS, 128), BF16),
-            ((2 * SMALL, 128), F32),
-            dma_pair,
+            sums_scratch,
+            small_scratch,
+            copies,
+            pltpu.SemaphoreType.DMA((4,)),
         ],
         smem=1,
-        fetch=(12, 13, 10, 11, 14, 23, 24, 16, 1, 17, 18, 20, 22),
+        far_in=(20, 21, 22, 23),
+        pinned=(20, 21, 22, 23),
         far_out=(9, 10),
-        flops=12 * ROWS * width * hidden,
-        room=32,
+        room=24,
     )
-    other = swap(send, "seq", 1)
-    grad_mid, grad_attended, grad_out, vectors = call(
-        branch_kernel,
-        (cotangent, mid, grad_second, row(second_gain), attended, out_weight),
-        [((ROWS, width), F32), ((ROWS, width), BF16), ((width, width), BF16), ((8, width), F32)],
-        fetch=(3,),
-        flops=4 * ROWS * width * width,
-        room=8,
-    )
-    first = add_cores(keep, after(other, grad_attended), FIRST_CUT)
-    first_came = step_one(first)
-    grad_attended, grad_out, vectors = after((grad_attended, grad_out, vectors), first)
-    grad_normed, inner, outer, keep, send, *owners = call(
-        functools.partial(back_kernel, levels, holders),
-        (
-            tokens, normed_low, query, key, value, key_pool, value_pool, halo, key_halo,
-            value_halo, weights, grad_attended, grad_out, late, vectors, gain, shift, query_weight,
-            key_weight, value_weight,
-        ),
-        [
-            ((ROWS, width), F32),
-            ((HALO, width), BF16),
-            ((HALO, width), BF16),
-            ((half, SECOND_ROWS + extra, 128), BF16),
-            ((half, SECOND_ROWS + extra, 128), BF16),
-        ]
-        + owner_shapes,
-        scratch=[
-            ((cols, width), BF16),
-            ((cols, width), BF16),
-            ((ROWS, width), BF16),
-            ((ROWS, width), F32),
-            ((POOLED, width), F32),
-            ((lent, width), F32),
-            ((ROWS, width), F32),
-            ((POOLED, width), F32),
-            ((lent, width), F32),
-            ((PIECES, SECOND_ROWS + extra, 128), BF16),
-            ((2 * SMALL, 128), F32),
-            dma_pair,
-        ],
-        fetch=(15, 16, 0, 17, 18, 19),
-        far_out=(3, 4),
-        flops=20 * ROWS * width * width,
-        room=28,
-    )
-    other = swap(after(send, first_came), "seq", 1)
-    inner_came = swap(inner, "seq", 1)
-    outer_came = swap_outer(outer, "seq")
-    first = add_step_one(first, first_came)
-    first_came = step_two(first)
-    second = add_cores(keep, other, SECOND_CUT)
-    second_came = step_one(second)
-    sent, kept = add_step_two(first, after(first_came, second))
-    sent, kept = add_near(kept, swap(sent, "batch", 1))
-    second = add_step_one(second, after(second_came, kept))
-    second_came = step_two(second)
-    first = add_far(kept, after(swap(sent, "batch", 2), second))
-    pair = pair_of(first, swap(first, "batch", 2))
-    sent, kept, *users = add_step_two(second, after(second_came, pair), extra)
-    column = column_of(pair, after(swap(pair, "batch", 1), kept))
-    first_came = planes(column)
-    sent, kept = add_near(kept, after(swap(sent, "batch", 1), column))
-    second = add_far(kept, swap(sent, "batch", 2))
-    pair = pair_of(second, swap(second, "batch", 2))
-    second_column = column_of(pair, swap(pair, "batch", 1))
-    second_came = planes(second_column)
-    if not users:
-        rows = owners[0].reshape(holders, GATHER, width)
-        users = list(lax.all_to_all(rows, "seq", split_axis=0, concat_axis=0, tiled=True))
-    users, inner_came, outer_came = after((users, inner_came, outer_came), second_column)
-    (grad_tokens,) = call(
-        functools.partial(last_kernel, levels),
-        (tokens, gain, grad_mid, grad_normed, inner_came, outer_came, *users),
-        [((1, ROWS, width), F32)],
-        scratch=[((ROWS, width), F32)],
-        fetch=(0, 1),
-        flops=4 * ROWS * ROWS * width,
-        room=8,
-    )
-    first_sums = plane_of(column, after(first_came, grad_tokens))
-    first_sums += [swap(block, "seq", 1) for block in first_sums]
     lines = width // 128
     small = ((lines, 128), F32)
     square = ((width, width), F32)
-    small_rows = ((PIECES * SMALL, 128), F32)
-    down, up, down_b, up_b = call(
-        functools.partial(collect_kernel, 1),
-        first_sums,
-        [((hidden, width), F32), ((width, hidden), F32), small, ((hidden // 128, 128), F32)],
-        scratch=[small_rows],
-        room=24,
-    )
-    second_sums = plane_of(second_column, after(second_came, down_b))
-    second_sums += [swap(block, "seq", 1) for block in second_sums]
-    up, out_w, query_w, key_w, value_w, query_b, value_b, out_b, gain1, shift1, gain2, shift2 = call(
-        functools.partial(collect_kernel, 2),
-        [*second_sums, up],
-        [((width, hidden), F32)] + [square] * 4 + [small] * 7,
-        scratch=[((width, hidden - EARLY_UP), F32), pltpu.SemaphoreType.DMA, small_rows],
-        far_in=(8,),
-        far_out=(0,),
-        alias={8: 0},
-        room=20,
-    )
+    collected = {
+        1: [((hidden, width), F32), small],
+        2: [((width, hidden), F32), ((hidden // 128, 128), F32), small, small],
+        3: [square] * 4 + [small] * 5,
+    }
+    sums = {1: Group(keep, [send])}
+    done = {}
+    last = ()
+    for what in ORDER:
+        if what == FEED:
+            output, grad_mid, grad_attended, grad_out, out_b_sum, keep, *sends = call(
+                feed_kernel,
+                (
+                    cotangent, after(mid, last), low_second, active, slope, second_gain, up_weight, down_weight,
+                    down_bias, out_weight, attended,
+                ),
+                [
+                    ((1, ROWS, width), BF16),
+                    ((ROWS, width), F32),
+                    ((ROWS, width), BF16),
+                    ((width, width), BF16),
+                    ((1, width), F32),
+                ]
+                + piece_sums(MID_PARTS),
+                scratch=[sums_scratch, small_scratch, copies],
+                far_out=range(5, 6 + MID_PARTS),
+                room=24,
+            )
+            sums[2] = Group(keep, sends)
+            last = grad_attended
+        elif what == BACK:
+            grad_normed, inner, outer, keep, *sends = call(
+                functools.partial(back_kernel, levels, holders),
+                (
+                    tokens, normed_low, after(query, last), key, value, key_pool, value_pool, halo, key_halo,
+                    value_halo, weights, grad_attended, grad_out, out_b_sum, gain, shift, query_weight,
+                    key_weight, value_weight,
+                ),
+                [
+                    ((ROWS, width), F32),
+                    ((HALO, width), BF16),
+                    ((HALO, width), BF16),
+                ]
+                + piece_sums(LATE_PARTS, GROUP_ROWS + extra)
+                + owner_shapes,
+                scratch=[
+                    ((cols, width), BF16),
+                    ((cols, width), BF16),
+                    ((ROWS, width), BF16),
+                    ((ROWS, width), F32),
+                    ((POOLED, width), F32),
+                    ((lent, width), F32),
+                    ((ROWS, width), F32),
+                    ((POOLED, width), F32),
+                    ((lent, width), F32),
+                    ((PIECES, GROUP_ROWS + extra, 128), BF16),
+                    small_scratch,
+                    copies,
+                ],
+                far_out=range(3, 4 + LATE_PARTS),
+                room=28,
+            )
+            sends, owners = sends[:LATE_PARTS], sends[LATE_PARTS:]
+            sums[3] = Group(keep, sends)
+            inner_came = swap(inner, "seq", 1)
+            outer_came = swap_outer(outer, "seq")
+            last = grad_normed
+        elif what == LAST:
+            users = sums[3].users
+            if not extra:
+                rows = owners[0].reshape(holders, GATHER, width)
+                users = list(lax.all_to_all(rows, "seq", split_axis=0, concat_axis=0, tiled=True))
+            (grad_tokens,) = call(
+                functools.partial(last_kernel, levels),
+                (tokens, gain, grad_mid, after(grad_normed, last), inner_came, outer_came, *users),
+                [((1, ROWS, width), F32)],
+                scratch=[((ROWS, width), F32)],
+                room=8,
+            )
+            last = grad_tokens
+        elif what == BORROWED:
+            inner_came, outer_came = after((inner_came, outer_came), last)
+            last = (inner_came, outer_came)
+        elif sums[what].stage < 9:
+            last = sums[what].step(last, extra if what == 3 else 0)
+        else:
+            done[what] = call(
+                functools.partial(collect_kernel, what - 1),
+                after(sums[what].sums, last),
+                collected[what],
+                scratch=[((PIECES * SMALL, 128), F32)],
+                room=16,
+            )
+            last = done[what][-1]
+    down, down_b = done[1]
+    up, up_b, gain2, shift2 = done[2]
+    out_w, query_w, key_w, value_w, query_b, value_b, out_b, gain1, shift1 = done[3]
     vectors = [query_b, value_b, out_b, up_b, down_b, gain1, shift1, gain2, shift2]
     return (output, grad_tokens, query_w, key_w, value_w, out_w, up, down) + tuple(
         vector.reshape(-1) for vector in vectors

time: 140 us -> 132 us (0.943)
  waiting for transfers between devices: 45.7 us -> 40.6 us
  Pallas kernels: 38 us -> 34.2 us
    ppermute x37 -> x36, waiting for transfers between devices: 45.7 us -> 23.5 us  [swap(): return lax.ppermute(array, axis, [(i, i ^ distance) for i in range(count)])]
    ppermute x0 -> x12, starting transfers between devices: none -> 19.5 us  [hop(): return lax.ppermute(array, 'seq', pairs)]
    ppermute x37 -> x36, starting transfers between devices: 53 us -> 34.1 us  [swap(): return lax.ppermute(array, axis, [(i, i ^ distance) for i in range(count)])]
    ppermute x0 -> x12, waiting for transfers between devices: none -> 17.1 us  [hop(): return lax.ppermute(array, 'seq', pairs)]
    pallas_call x23 -> x28, Pallas kernels: 38 us -> 34.2 us  [call(): pl.pallas_call(kernel, out_shape=[jax.ShapeDtypeStruct(s, d) for s, d in...]
  transfers between devices with their start and end apart: 39 -> 50, of which waited for: 21 -> 19; matrix products, arithmetic and copies ran while one was open for 0% -> 0% of each run, Pallas kernels for 14% -> 17%
where the time goes in v3:
time: 132 us
  starting transfers between devices  55.1 us (42%)
  waiting for transfers between devices  40.6 us (31%)
  Pallas kernels  34.2 us (26%)
    pallas_call x28, Pallas kernels, call(): pl.pallas_call(kernel, out_shape=[jax.ShapeDtypeStruct(s, d) for s, d in...  34.2 us
    ppermute x36, starting transfers between devices, swap(): return lax.ppermute(array, axis, [(i, i ^ distance) for i in range(count)])  34.1 us
    ppermute x36, waiting for transfers between devices, swap(): return lax.ppermute(array, axis, [(i, i ^ distance) for i in range(count)])  23.5 us
    ppermute x12, starting transfers between devices, hop(): return lax.ppermute(array, 'seq', pairs)  19.5 us
    ppermute x12, waiting for transfers between devices, hop(): return lax.ppermute(array, 'seq', pairs)  17.1 us
  transfers between devices with their start and end apart: 50, of which 19 were waited for; matrix products, arithmetic and copies ran while one was open for 0% of the time, Pallas kernels for 17%

profile of v3, /device:TPU:0, one launch (start us, length us, event | category | flops | bytes accessed | tf_op | source)
XLA Modules:
  0.0 131.8 jit_solution(17751427064269080471)
XLA Ops:
  3.7 5.1 %collective-permute-start.4 = (bf16[64,512]{1,0:T(8,128)(2,1)S(1)}, bf16[64,512]{1,0:T(8,128)(2,1)S(1)}, u32[]{:S(2)}, u32[]{:S(2)}) collective-permute-start(bf16[64,512]{1,0:T(8,128)(2,1)S(1)} %shard_map.325.refs_0_), channel_id=1, source_target_pairs={{0,6},{1,7},{2,4},{3,5},{4,2},{5,3},{6,0},{7,1},{8,14},{9,15},{10,... | collective-permute-start | bytes 196616 | tf_op jit(solution)/shard_map/ppermute | solution.py:713
  10.2 3.4 %shard_map.323 = (bf16[1,256,512]{2,1,0:T(8,128)(2,1)S(1)}, f32[1,512]{1,0:T(1,128)S(1)}, f32[1,512]{1,0:T(1,128)S(1)}, bf16[512,512]{1,0:T(8,128)(2,1)S(1)}, f3...) custom-call(bf16[1,256,512]{2,1,0:T(8,128)(2,1)} %tokens.1, ...), custom_call_target="tpu_custom_call" | custom-call | tf_op jit(solution)/shard_map/pallas_call | solution.py:699
  13.9 8.9 %shard_map.326 = (bf16[256,512]{1,0:T(8,128)(2,1)S(1)}, bf16[8,256,384]{2,1,0:T(8,128)(2,1)S(1)}, bf16[320,512]{1,0:T(8,128)(2,1)S(1)}, bf16[320,512]{1,0:T(8,12...) custom-call(s32[1,2]{1,0:T(1,128)S(1)} %copy-done.1, ...), custom_call_target="tpu_custom_call" | custom-call | tf_op jit(solution)/shard_map/pallas_call | solution.py:699
  22.9 4.6 %shard_map.327 = (bf16[1,256,512]{2,1,0:T(8,128)(2,1)}, f32[256,512]{1,0:T(8,128)S(1)}, bf16[256,512]{1,0:T(8,128)(2,1)S(1)}, bf16[512,512]{1,0:T(8,128)(2,1)S(1...) custom-call(bf16[1,256,512]{2,1,0:T(8,128)(2,1)S(1)} %get-tuple-elem, ...), custom_call_target="tpu_custom_call" | custom-call | tf_op jit(solution)/shard_map/pallas_call | solution.py:699
  28.3 2.3 %collective-permute-start.13 = (bf16[2,4,272,128]{3,2,1,0:T(8,128)(2,1)S(1)}, bf16[2,4,272,128]{3,2,1,0:T(8,128)(2,1)S(1)}, u32[]{:S(2)}, u32[]{:S(2)}) collective-permute-start(bf16[2,4,272,128]{3,2,1,0:T(8,128)(2,1)S(1)} %get-tuple-element.221), channel_id=1, source_target_pairs={{0,2},{1,5},{2,0},{3,7},{4,6},{5,1},{6,4},{7,3},{8,10},{9,13},{10,... | collective-permute-start | bytes 1671176 | tf_op jit(solution)/shard_map/ppermute | solution.py:735
  32.9 6.4 %shard_map.330 = (f32[256,512]{1,0:T(8,128)S(1)}, bf16[112,512]{1,0:T(8,128)(2,1)S(1)}, bf16[112,512]{1,0:T(8,128)(2,1)S(1)}, bf16[16,304,128]{2,1,0:T(8,128)(2,...) custom-call(bf16[1,256,512]{2,1,0:T(8,128)(2,1)S(1)} %get-tuple-elem, ...), custom_call_target="tpu_custom_call" | custom-call | tf_op jit(solution)/shard_map/pallas_call | solution.py:699
  40.5 3.6 %collective-permute-done.12.refs_0_ = bf16[2,4,272,128]{3,2,1,0:T(8,128)(2,1)S(1)} collective-permute-done((bf16[2,4,272,128]{3,2,1,0:T(8,128)(2,1)S(1)}, bf16[2,4,272,128]{3,2,1,0:T(8,128)(2,1)S(1)}, u32[]{:S(2)}, u32[]{:S(2)}) %collective-permute-start.12) | collective-permute-done | bytes 557088 | tf_op jit(solution)/shard_map/ppermute | solution.py:735
  44.6 2.1 %collective-permute-start.14 = (bf16[2,4,304,128]{3,2,1,0:T(8,128)(2,1)S(1)}, bf16[2,4,304,128]{3,2,1,0:T(8,128)(2,1)S(1)}, u32[]{:S(2)}, u32[]{:S(2)}) collective-permute-start(bf16[2,4,304,128]{3,2,1,0:T(8,128)(2,1)S(1)} %get-tuple-element.231), channel_id=1, source_target_pairs={{0,2},{1,5},{2,0},{3,7},{4,6},{5,1},{6,4},{7,3},{8,10},{9,13},{10,... | collective-permute-start | bytes 1867784 | tf_op jit(solution)/shard_map/ppermute | solution.py:735
  49.6 6.7 %collective-permute-done.15.came = bf16[4,272,128]{2,1,0:T(8,128)(2,1)S(1)} collective-permute-done((bf16[4,272,128]{2,1,0:T(8,128)(2,1)S(1)}, bf16[4,272,128]{2,1,0:T(8,128)(2,1)S(1)}, u32[]{:S(2)}, u32[]{:S(2)}) %collective-permute-start.15) | collective-permute-done | bytes 278560 | tf_op jit(solution)/shard_map/ppermute | solution.py:735
  56.3 2.6 %collective-permute-start.16 = (bf16[272,128]{1,0:T(8,128)(2,1)S(1)}, bf16[272,128]{1,0:T(8,128)(2,1)S(1)}, u32[]{:S(2)}, u32[]{:S(2)}) collective-permute-start(bf16[272,128]{1,0:T(8,128)(2,1)S(1)} %get-tuple-element.235), channel_id=1, source_target_pairs={{0,16},{8,24},{16,0},{24,8},{1,17},{9,25},{17,1},{25,9},{2,18},{10... | collective-permute-start | bytes 208904 | tf_op jit(solution)/shard_map/ppermute | solution.py:713
  60.7 2.8 %collective-permute-start.26 = (bf16[272,128]{1,0:T(8,128)(2,1)S(1)}, bf16[272,128]{1,0:T(8,128)(2,1)S(1)}, u32[]{:S(2)}, u32[]{:S(2)}) collective-permute-start(bf16[272,128]{1,0:T(8,128)(2,1)S(1)} %get-tuple-element.251), channel_id=1, source_target_pairs={{0,16},{8,24},{16,0},{24,8},{1,17},{9,25},{17,1},{25,9},{2,18},{10... | collective-permute-start | bytes 208904 | tf_op jit(solution)/shard_map/ppermute | solution.py:713
  63.5 3.1 %collective-permute-start.27 = (bf16[272,128]{1,0:T(8,128)(2,1)S(1)}, bf16[272,128]{1,0:T(8,128)(2,1)S(1)}, u32[]{:S(2)}, u32[]{:S(2)}) collective-permute-start(bf16[272,128]{1,0:T(8,128)(2,1)S(1)} %get-tuple-element.252), channel_id=1, source_target_pairs={{0,24},{8,16},{16,8},{24,0},{1,25},{9,17},{17,9},{25,1},{2,26},{10... | collective-permute-start | bytes 208904 | tf_op jit(solution)/shard_map/ppermute | solution.py:713
  70.5 4.4 %collective-permute-start.22 = (bf16[4,304,128]{2,1,0:T(8,128)(2,1)S(1)}, bf16[4,304,128]{2,1,0:T(8,128)(2,1)S(1)}, u32[]{:S(2)}, u32[]{:S(2)}) collective-permute-start(bf16[4,304,128]{2,1,0:T(8,128)(2,1)S(1)} %bitcast.47), channel_id=1, source_target_pairs={{0,4},{1,3},{2,6},{3,1},{4,0},{5,7},{6,2},{7,5},{8,12},{9,11},{10,... | collective-permute-start | bytes 933896 | tf_op jit(solution)/shard_map/ppermute | solution.py:735
  75.1 3.2 %collective-permute-done.23.two = bf16[272,128]{1,0:T(8,128)(2,1)S(1)} collective-permute-done((bf16[272,128]{1,0:T(8,128)(2,1)S(1)}, bf16[272,128]{1,0:T(8,128)(2,1)S(1)}, u32[]{:S(2)}, u32[]{:S(2)}) %collective-permute-start.23) | collective-permute-done | bytes 69664 | tf_op jit(solution)/shard_map/ppermute | solution.py:713
  78.3 2.1 %collective-permute-start.32 = (bf16[1,4,272,128]{3,2,1,0:T(8,128)(2,1)S(1)}, bf16[1,4,272,128]{3,2,1,0:T(8,128)(2,1)S(1)}, u32[]{:S(2)}, u32[]{:S(2)}) collective-permute-start(bf16[1,4,272,128]{3,2,1,0:T(8,128)(2,1)S(1)} %shard_map.339.mine), channel_id=1, source_target_pairs={{0,4},{1,3},{2,6},{3,1},{4,0},{5,7},{6,2},{7,5},{8,12},{9,11},{10,... | collective-permute-start | bytes 835592 | tf_op jit(solution)/shard_map/ppermute | solution.py:735
  87.2 4.1 %collective-permute-done.33.two = bf16[272,128]{1,0:T(8,128)(2,1)S(1)} collective-permute-done((bf16[272,128]{1,0:T(8,128)(2,1)S(1)}, bf16[272,128]{1,0:T(8,128)(2,1)S(1)}, u32[]{:S(2)}, u32[]{:S(2)}) %collective-permute-start.33) | collective-permute-done | bytes 69664 | tf_op jit(solution)/shard_map/ppermute | solution.py:713
  95.4 4.1 %collective-permute-done.29.refs_1_ = bf16[272,128]{1,0:T(8,128)(2,1)S(1)} collective-permute-done((bf16[272,128]{1,0:T(8,128)(2,1)S(1)}, bf16[272,128]{1,0:T(8,128)(2,1)S(1)}, u32[]{:S(2)}, u32[]{:S(2)}) %collective-permute-start.29) | collective-permute-done | bytes 69664 | tf_op jit(solution)/shard_map/ppermute | solution.py:713
  106.7 2.1 %collective-permute-done.37.three = bf16[272,128]{1,0:T(8,128)(2,1)S(1)} collective-permute-done((bf16[272,128]{1,0:T(8,128)(2,1)S(1)}, bf16[272,128]{1,0:T(8,128)(2,1)S(1)}, u32[]{:S(2)}, u32[]{:S(2)}) %collective-permute-start.37) | collective-permute-done | bytes 69664 | tf_op jit(solution)/shard_map/ppermute | solution.py:713
  108.8 2.3 %collective-permute-done.36.two = bf16[272,128]{1,0:T(8,128)(2,1)S(1)} collective-permute-done((bf16[272,128]{1,0:T(8,128)(2,1)S(1)}, bf16[272,128]{1,0:T(8,128)(2,1)S(1)}, u32[]{:S(2)}, u32[]{:S(2)}) %collective-permute-start.36) | collective-permute-done | bytes 69664 | tf_op jit(solution)/shard_map/ppermute | solution.py:713
  113.1 4.6 %collective-permute-done.41.came = bf16[1,4,272,128]{3,2,1,0:T(8,128)(2,1)S(1)} collective-permute-done((bf16[1,4,272,128]{3,2,1,0:T(8,128)(2,1)S(1)}, bf16[1,4,272,128]{3,2,1,0:T(8,128)(2,1)S(1)}, u32[]{:S(2)}, u32[]{:S(2)}) %collective-permute-start.41) | collective-permute-done | bytes 278560 | tf_op jit(solution)/shard_map/ppermute | solution.py:735
  117.7 2.2 %collective-permute-start.43 = (bf16[2,4,272,128]{3,2,1,0:T(8,128)(2,1)S(1)}, bf16[2,4,272,128]{3,2,1,0:T(8,128)(2,1)S(1)}, u32[]{:S(2)}, u32[]{:S(2)}) collective-permute-start(bf16[2,4,272,128]{3,2,1,0:T(8,128)(2,1)S(1)} %shard_map.346.refs_0_), channel_id=1, source_target_pairs={{0,2},{1,5},{2,0},{3,7},{4,6},{5,1},{6,4},{7,3},{8,10},{9,13},{10,... | collective-permute-start | bytes 1671176 | tf_op jit(solution)/shard_map/ppermute | solution.py:735
  121.3 2.4 %shard_map.348 = (f32[512,2048]{1,0:T(8,128)}, f32[16,128]{1,0:T(8,128)}, f32[4,128]{1,0:T(4,128)}, f32[4,128]{1,0:T(4,128)}) custom-call(bf16[2,4,272,128]{3,2,1,0:T(8,128)(2,1)S(1)} %shard_map.344.refs_0_, bf16[2,4,272,128]{3,2,1,0:T(8,128)(2,1)S(1)} %collective-permute-done.42.refs_1_, bf16[2,4,272,128]{3,2,1,0:T(8,128)(2,1)S(1)} %collective-permute-done.46.refs_2_, ...), custom_call_target="tpu_custom_call" | custom-call | tf_op jit(solution)/shard_map/pallas_call | solution.py:699
  123.7 2.4 %shard_map.349 = (f32[2048,512]{1,0:T(8,128)}, f32[4,128]{1,0:T(4,128)}) custom-call(bf16[2,4,272,128]{3,2,1,0:T(8,128)(2,1)S(1)} %shard_map.342.refs_0_, bf16[2,4,272,128]{3,2,1,0:T(8,128)(2,1)S(1)} %collective-permute-done.39.refs_1_, bf16[2,4,272,128]{3,2,1,0:T(8,128)(2,1)S(1)} %collective-permute-done.44.refs_2_, ...), custom_call_target="tpu_custom_call" | custom-call | tf_op jit(solution)/shard_map/pallas_call | solution.py:699
  129.4 2.4 %shard_map.350 = (f32[512,512]{1,0:T(8,128)}, f32[512,512]{1,0:T(8,128)}, f32[512,512]{1,0:T(8,128)}, f32[512,512]{1,0:T(8,128)}, f32[4,128]{1,0:T(4,128)}, /*in...) custom-call(bf16[2,4,272,128]{3,2,1,0:T(8,128)(2,1)S(1)} %shard_map.346.refs_0_, ...), custom_call_target="tpu_custom_call" | custom-call | tf_op jit(solution)/shard_map/pallas_call | solution.py:699
  (108 shorter events, 43.1 us)
Async XLA Ops:
  2.7 11.0 %collective-permute-start.1 = (bf16[112,512]{1,0:T(8,128)(2,1)S(1)}, bf16[112,512]{1,0:T(8,128)(2,1)S(1)}, u32[]{:S(2)}, u32[]{:S(2)}) collective-permute-start(bf16[112,512]{1,0:T(8,128)(2,1)S(1)} %get-tuple-element.170), channel_id=1, source_target_pairs={{1,2},{3,4},{5,6},{2,1},{4,3},{6,5},{9,10},{11,12},{13,14},{10,9},... | collective-permute-start | bytes 344072 | tf_op jit(solution)/shard_map/ppermute | solution.py:719
  3.7 9.9 %collective-permute-start.4 = (bf16[64,512]{1,0:T(8,128)(2,1)S(1)}, bf16[64,512]{1,0:T(8,128)(2,1)S(1)}, u32[]{:S(2)}, u32[]{:S(2)}) collective-permute-start(bf16[64,512]{1,0:T(8,128)(2,1)S(1)} %shard_map.325.refs_0_), channel_id=1, source_target_pairs={{0,6},{1,7},{2,4},{3,5},{4,2},{5,3},{6,0},{7,1},{8,14},{9,15},{10,... | collective-permute-start | bytes 196616 | tf_op jit(solution)/shard_map/ppermute | solution.py:713
  28.3 11.7 %collective-permute-start.13 = (bf16[2,4,272,128]{3,2,1,0:T(8,128)(2,1)S(1)}, bf16[2,4,272,128]{3,2,1,0:T(8,128)(2,1)S(1)}, u32[]{:S(2)}, u32[]{:S(2)}) collective-permute-start(bf16[2,4,272,128]{3,2,1,0:T(8,128)(2,1)S(1)} %get-tuple-element.221), channel_id=1, source_target_pairs={{0,2},{1,5},{2,0},{3,7},{4,6},{5,1},{6,4},{7,3},{8,10},{9,13},{10,... | collective-permute-start | bytes 1671176 | tf_op jit(solution)/shard_map/ppermute | solution.py:735
  30.9 13.2 %collective-permute-start.12 = (bf16[2,4,272,128]{3,2,1,0:T(8,128)(2,1)S(1)}, bf16[2,4,272,128]{3,2,1,0:T(8,128)(2,1)S(1)}, u32[]{:S(2)}, u32[]{:S(2)}) collective-permute-start(bf16[2,4,272,128]{3,2,1,0:T(8,128)(2,1)S(1)} %get-tuple-element.220), channel_id=1, source_target_pairs={{0,2},{1,5},{2,0},{3,7},{4,6},{5,1},{6,4},{7,3},{8,10},{9,13},{10,... | collective-permute-start | bytes 1671176 | tf_op jit(solution)/shard_map/ppermute | solution.py:735
  44.6 24.9 %collective-permute-start.14 = (bf16[2,4,304,128]{3,2,1,0:T(8,128)(2,1)S(1)}, bf16[2,4,304,128]{3,2,1,0:T(8,128)(2,1)S(1)}, u32[]{:S(2)}, u32[]{:S(2)}) collective-permute-start(bf16[2,4,304,128]{3,2,1,0:T(8,128)(2,1)S(1)} %get-tuple-element.231), channel_id=1, source_target_pairs={{0,2},{1,5},{2,0},{3,7},{4,6},{5,1},{6,4},{7,3},{8,10},{9,13},{10,... | collective-permute-start | bytes 1867784 | tf_op jit(solution)/shard_map/ppermute | solution.py:735
  46.7 9.6 %collective-permute-start.15 = (bf16[4,272,128]{2,1,0:T(8,128)(2,1)S(1)}, bf16[4,272,128]{2,1,0:T(8,128)(2,1)S(1)}, u32[]{:S(2)}, u32[]{:S(2)}) collective-permute-start(bf16[4,272,128]{2,1,0:T(8,128)(2,1)S(1)} %bitcast.49), channel_id=1, source_target_pairs={{0,4},{1,3},{2,6},{3,1},{4,0},{5,7},{6,2},{7,5},{8,12},{9,11},{10,... | collective-permute-start | bytes 835592 | tf_op jit(solution)/shard_map/ppermute | solution.py:735
  47.4 13.2 %collective-permute-start.19 = (bf16[4,272,128]{2,1,0:T(8,128)(2,1)S(1)}, bf16[4,272,128]{2,1,0:T(8,128)(2,1)S(1)}, u32[]{:S(2)}, u32[]{:S(2)}) collective-permute-start(bf16[4,272,128]{2,1,0:T(8,128)(2,1)S(1)} %bitcast.48), channel_id=1, source_target_pairs={{0,4},{1,3},{2,6},{3,1},{4,0},{5,7},{6,2},{7,5},{8,12},{9,11},{10,... | collective-permute-start | bytes 835592 | tf_op jit(solution)/shard_map/ppermute | solution.py:735
  48.7 10.3 %collective-permute-start.20 = (bf16[112,512]{1,0:T(8,128)(2,1)S(1)}, bf16[112,512]{1,0:T(8,128)(2,1)S(1)}, u32[]{:S(2)}, u32[]{:S(2)}) collective-permute-start(bf16[112,512]{1,0:T(8,128)(2,1)S(1)} %get-tuple-element.239), channel_id=1, source_target_pairs={{0,1},{1,0},{2,3},{3,2},{4,5},{5,4},{6,7},{7,6},{8,9},{9,8},{10,11... | collective-permute-start | bytes 344072 | tf_op jit(solution)/shard_map/ppermute | solution.py:713
  48.7 11.6 %collective-permute-start.21 = (bf16[112,512]{1,0:T(8,128)(2,1)S(1)}, bf16[112,512]{1,0:T(8,128)(2,1)S(1)}, u32[]{:S(2)}, u32[]{:S(2)}) collective-permute-start(bf16[112,512]{1,0:T(8,128)(2,1)S(1)} %get-tuple-element.240), channel_id=1, source_target_pairs={{1,2},{3,4},{5,6},{2,1},{4,3},{6,5},{9,10},{11,12},{13,14},{10,9},... | collective-permute-start | bytes 344072 | tf_op jit(solution)/shard_map/ppermute | solution.py:719
  60.7 8.0 %collective-permute-start.26 = (bf16[272,128]{1,0:T(8,128)(2,1)S(1)}, bf16[272,128]{1,0:T(8,128)(2,1)S(1)}, u32[]{:S(2)}, u32[]{:S(2)}) collective-permute-start(bf16[272,128]{1,0:T(8,128)(2,1)S(1)} %get-tuple-element.251), channel_id=1, source_target_pairs={{0,16},{8,24},{16,0},{24,8},{1,17},{9,25},{17,1},{25,9},{2,18},{10... | collective-permute-start | bytes 208904 | tf_op jit(solution)/shard_map/ppermute | solution.py:713
  66.6 8.4 %collective-permute-start.28 = (bf16[272,128]{1,0:T(8,128)(2,1)S(1)}, bf16[272,128]{1,0:T(8,128)(2,1)S(1)}, u32[]{:S(2)}, u32[]{:S(2)}) collective-permute-start(bf16[272,128]{1,0:T(8,128)(2,1)S(1)} %get-tuple-element.253), channel_id=1, source_target_pairs={{0,8},{8,0},{16,24},{24,16},{1,9},{9,1},{17,25},{25,17},{2,10},{10... | collective-permute-start | bytes 208904 | tf_op jit(solution)/shard_map/ppermute | solution.py:713
  66.7 8.4 %collective-permute-start.25 = (bf16[272,128]{1,0:T(8,128)(2,1)S(1)}, bf16[272,128]{1,0:T(8,128)(2,1)S(1)}, u32[]{:S(2)}, u32[]{:S(2)}) collective-permute-start(bf16[272,128]{1,0:T(8,128)(2,1)S(1)} %shard_map.336.whole), channel_id=1, source_target_pairs={{0,8},{8,0},{16,24},{24,16},{1,9},{9,1},{17,25},{25,17},{2,10},{10... | collective-permute-start | bytes 208904 | tf_op jit(solution)/shard_map/ppermute | solution.py:713
  69.5 8.8 %collective-permute-start.23 = (bf16[272,128]{1,0:T(8,128)(2,1)S(1)}, bf16[272,128]{1,0:T(8,128)(2,1)S(1)}, u32[]{:S(2)}, u32[]{:S(2)}) collective-permute-start(bf16[272,128]{1,0:T(8,128)(2,1)S(1)} %shard_map.336.whole), channel_id=1, source_target_pairs={{0,16},{8,24},{16,0},{24,8},{1,17},{9,25},{17,1},{25,9},{2,18},{10... | collective-permute-start | bytes 208904 | tf_op jit(solution)/shard_map/ppermute | solution.py:713
  70.5 13.4 %collective-permute-start.22 = (bf16[4,304,128]{2,1,0:T(8,128)(2,1)S(1)}, bf16[4,304,128]{2,1,0:T(8,128)(2,1)S(1)}, u32[]{:S(2)}, u32[]{:S(2)}) collective-permute-start(bf16[4,304,128]{2,1,0:T(8,128)(2,1)S(1)} %bitcast.47), channel_id=1, source_target_pairs={{0,4},{1,3},{2,6},{3,1},{4,0},{5,7},{6,2},{7,5},{8,12},{9,11},{10,... | collective-permute-start | bytes 933896 | tf_op jit(solution)/shard_map/ppermute | solution.py:735
  78.3 13.1 %collective-permute-start.32 = (bf16[1,4,272,128]{3,2,1,0:T(8,128)(2,1)S(1)}, bf16[1,4,272,128]{3,2,1,0:T(8,128)(2,1)S(1)}, u32[]{:S(2)}, u32[]{:S(2)}) collective-permute-start(bf16[1,4,272,128]{3,2,1,0:T(8,128)(2,1)S(1)} %shard_map.339.mine), channel_id=1, source_target_pairs={{0,4},{1,3},{2,6},{3,1},{4,0},{5,7},{6,2},{7,5},{8,12},{9,11},{10,... | collective-permute-start | bytes 835592 | tf_op jit(solution)/shard_map/ppermute | solution.py:735
  82.4 8.8 %collective-permute-start.33 = (bf16[272,128]{1,0:T(8,128)(2,1)S(1)}, bf16[272,128]{1,0:T(8,128)(2,1)S(1)}, u32[]{:S(2)}, u32[]{:S(2)}) collective-permute-start(bf16[272,128]{1,0:T(8,128)(2,1)S(1)} %shard_map.338.whole), channel_id=1, source_target_pairs={{0,16},{8,24},{16,0},{24,8},{1,17},{9,25},{17,1},{25,9},{2,18},{10... | collective-permute-start | bytes 208904 | tf_op jit(solution)/shard_map/ppermute | solution.py:713
  91.3 9.6 %collective-permute-start.40 = (bf16[1,4,272,128]{3,2,1,0:T(8,128)(2,1)S(1)}, bf16[1,4,272,128]{3,2,1,0:T(8,128)(2,1)S(1)}, u32[]{:S(2)}, u32[]{:S(2)}) collective-permute-start(bf16[1,4,272,128]{3,2,1,0:T(8,128)(2,1)S(1)} %shard_map.341.mine), channel_id=1, source_target_pairs={{0,4},{1,3},{2,6},{3,1},{4,0},{5,7},{6,2},{7,5},{8,12},{9,11},{10,... | collective-permute-start | bytes 835592 | tf_op jit(solution)/shard_map/ppermute | solution.py:735
  91.4 13.7 %collective-permute-start.39 = (bf16[2,4,272,128]{3,2,1,0:T(8,128)(2,1)S(1)}, bf16[2,4,272,128]{3,2,1,0:T(8,128)(2,1)S(1)}, u32[]{:S(2)}, u32[]{:S(2)}) collective-permute-start(bf16[2,4,272,128]{3,2,1,0:T(8,128)(2,1)S(1)} %shard_map.342.refs_0_), channel_id=1, source_target_pairs={{0,2},{1,5},{2,0},{3,7},{4,6},{5,1},{6,4},{7,3},{8,10},{9,13},{10,... | collective-permute-start | bytes 1671176 | tf_op jit(solution)/shard_map/ppermute | solution.py:735
  100.9 11.5 %collective-permute-start.42 = (bf16[2,4,272,128]{3,2,1,0:T(8,128)(2,1)S(1)}, bf16[2,4,272,128]{3,2,1,0:T(8,128)(2,1)S(1)}, u32[]{:S(2)}, u32[]{:S(2)}) collective-permute-start(bf16[2,4,272,128]{3,2,1,0:T(8,128)(2,1)S(1)} %shard_map.344.refs_0_), channel_id=1, source_target_pairs={{0,2},{1,5},{2,0},{3,7},{4,6},{5,1},{6,4},{7,3},{8,10},{9,13},{10,... | collective-permute-start | bytes 1671176 | tf_op jit(solution)/shard_map/ppermute | solution.py:735
  112.1 9.2 %collective-permute-start.46 = (bf16[2,4,272,128]{3,2,1,0:T(8,128)(2,1)S(1)}, bf16[2,4,272,128]{3,2,1,0:T(8,128)(2,1)S(1)}, u32[]{:S(2)}, u32[]{:S(2)}) collective-permute-start(bf16[2,4,272,128]{3,2,1,0:T(8,128)(2,1)S(1)} %shard_map.344.refs_0_), channel_id=1, source_target_pairs={{0,1},{1,0},{2,3},{3,2},{4,5},{5,4},{6,7},{7,6},{8,9},{9,8},{10,11... | collective-permute-start | bytes 1671176 | tf_op jit(solution)/shard_map/ppermute | solution.py:713
  112.4 8.9 %collective-permute-start.47 = (bf16[2,4,272,128]{3,2,1,0:T(8,128)(2,1)S(1)}, bf16[2,4,272,128]{3,2,1,0:T(8,128)(2,1)S(1)}, u32[]{:S(2)}, u32[]{:S(2)}) collective-permute-start(bf16[2,4,272,128]{3,2,1,0:T(8,128)(2,1)S(1)} %collective-permute-done.42.refs_1_), channel_id=1, source_target_pairs={{0,1},{1,0},{2,3},{3,2},{4,5},{5,4},{6,7},{7,6},{8,9},{9,8},{10,11... | collective-permute-start | bytes 1671176 | tf_op jit(solution)/shard_map/ppermute | solution.py:713
  112.6 11.2 %collective-permute-start.44 = (bf16[2,4,272,128]{3,2,1,0:T(8,128)(2,1)S(1)}, bf16[2,4,272,128]{3,2,1,0:T(8,128)(2,1)S(1)}, u32[]{:S(2)}, u32[]{:S(2)}) collective-permute-start(bf16[2,4,272,128]{3,2,1,0:T(8,128)(2,1)S(1)} %shard_map.342.refs_0_), channel_id=1, source_target_pairs={{0,1},{1,0},{2,3},{3,2},{4,5},{5,4},{6,7},{7,6},{8,9},{9,8},{10,11... | collective-permute-start | bytes 1671176 | tf_op jit(solution)/shard_map/ppermute | solution.py:713
  112.9 10.8 %collective-permute-start.45 = (bf16[2,4,272,128]{3,2,1,0:T(8,128)(2,1)S(1)}, bf16[2,4,272,128]{3,2,1,0:T(8,128)(2,1)S(1)}, u32[]{:S(2)}, u32[]{:S(2)}) collective-permute-start(bf16[2,4,272,128]{3,2,1,0:T(8,128)(2,1)S(1)} %collective-permute-done.39.refs_1_), channel_id=1, source_target_pairs={{0,1},{1,0},{2,3},{3,2},{4,5},{5,4},{6,7},{7,6},{8,9},{9,8},{10,11... | collective-permute-start | bytes 1671176 | tf_op jit(solution)/shard_map/ppermute | solution.py:713
  117.7 9.7 %collective-permute-start.43 = (bf16[2,4,272,128]{3,2,1,0:T(8,128)(2,1)S(1)}, bf16[2,4,272,128]{3,2,1,0:T(8,128)(2,1)S(1)}, u32[]{:S(2)}, u32[]{:S(2)}) collective-permute-start(bf16[2,4,272,128]{3,2,1,0:T(8,128)(2,1)S(1)} %shard_map.346.refs_0_), channel_id=1, source_target_pairs={{0,2},{1,5},{2,0},{3,7},{4,6},{5,1},{6,4},{7,3},{8,10},{9,13},{10,... | collective-permute-start | bytes 1671176 | tf_op jit(solution)/shard_map/ppermute | solution.py:735
  (28 other events, 152.7 us)

commit v4 on v3

--- a/solution.py
+++ b/solution.py
@@ -62,27 +62,8 @@
 
 
 def normal_parts(upper):
-    far = jnp.abs(upper) * math.sqrt(0.5)
-    t = 1.0 / (1.0 + 0.5 * far)
-    series = (
-        -1.26551223,
-        1.00002368,
-        0.37409196,
-        0.09678418,
-        -0.18628806,
-        0.27886807,
-        -1.13520398,
-        1.48851587,
-        -0.82215223,
-        0.17087277,
-    )
-    power = jnp.full_like(t, series[-1])
-    for term in series[-2::-1]:
-        power = power * t + term
-    square = far * far
-    half_tail = 0.5 * t * jnp.exp(power - square)
-    phi = jnp.exp(-square) * (1.0 / math.sqrt(2.0 * math.pi))
-    return jnp.where(upper < 0.0, half_tail, 1.0 - half_tail), phi
+    below = 0.5 + 0.5 * lax.erf(upper * math.sqrt(0.5))
+    return below, jnp.exp(-0.5 * upper * upper) * (1.0 / math.sqrt(2.0 * math.pi))
 
 
 def level_rows(level):
@@ -411,46 +392,48 @@
     small[...] = jnp.zeros_like(small)
     put_vector(small, 0, jnp.sum(cot.astype(F32), axis=0, keepdims=True))
     put_small(sums, 256, small)
+    copies = hand_out(sums, keep, [send], sem)
     down_w.wait()
-    hand_out(sums, keep, [send], sem)
+    for copy in copies:
+        copy.wait()
 
 
 def feed_kernel(
-    cotangent, mid, low_second, active, slope, gain2, up_w, down_w, down_b, out_w, attended,
-    output, grad_mid_out, grad_attended, grad_out, out_b_sum, keep, *refs,
+    cotangent, mid, low_second, slope, gain2, up_w, down_w, out_w, attended,
+    grad_mid_out, grad_attended, grad_out, out_b_sum, keep, *refs,
 ):
     sends, (sums, small, sem) = refs[:-3], refs[-3:]
     cot = cotangent[0]
     hidden, width = down_w.shape
-    result = mid[...] + down_b[...]
     grad_second = jnp.zeros((ROWS, width), F32)
     small[...] = jnp.zeros_like(small)
     for at in range(0, hidden, width):
         cols = slice(at, at + width)
-        result = result + dot(active[:, cols], down_w[cols])
         grad_upper = (dot_cols(cot, down_w[cols]) * slope[:, cols]).astype(BF16)
         put_vector(small, at // 128, jnp.sum(grad_upper.astype(F32), axis=0, keepdims=True))
         put_lines(sums, at // 8, dot_rows(low_second[...], grad_upper).astype(BF16))
         grad_second = grad_second + dot_cols(grad_upper, up_w[:, cols])
-    output[0] = result.astype(BF16)
     normed, scale = normalize(mid[...])
     put_vector(small, 16, jnp.sum(grad_second * normed, axis=0, keepdims=True))
     put_vector(small, 20, jnp.sum(grad_second, axis=0, keepdims=True))
     put_small(sums, 256, small)
+    copies = hand_out(sums, keep, sends, sem)
     grad_mid = cot.astype(F32) + norm_back(grad_second * gain2[...], normed, scale)
     grad_mid_out[...] = grad_mid
     branch = grad_mid.astype(BF16)
     grad_attended[...] = dot_cols(branch, out_w[...]).astype(BF16)
     grad_out[...] = dot_rows(attended[...], branch).astype(BF16)
     out_b_sum[...] = jnp.sum(branch.astype(F32), axis=0, keepdims=True)
-    hand_out(sums, keep, sends, sem)
+    for copy in copies:
+        copy.wait()
 
 
 FEED, BACK, BORROWED, LAST = "feed", "back", "borrowed", "last"
-ORDER = (FEED, 1, 2, BACK, 1, 2, 3, 1, BORROWED, 2, 1, 3, 2, 1, 3, 2, 1, 3, 2, 1, 3, 2, 3, LAST, 2, 1, 3, 3)
+ORDER = (FEED, 1, 2, BACK, 1, 2, 1, 3, 2, 1, 3, BORROWED, 2, 1, 3, 2, 1, 3, 2, 3, 1, 2, 3, LAST, 2, 1, 3, 3)
+STEP_PARTS = 1
 Z_DIRECT = True
 GROUP_ROWS = 256 + SMALL
-MID_PARTS, LATE_PARTS = 2, 4
+MID_PARTS, LATE_PARTS = 2, 3
 
 
 def put_vector(small, row, vector):
@@ -488,18 +471,31 @@
         sums[slot_of(piece), row : row + SMALL] = part
 
 
-def hand_out(sums, keep, sends, sem):
+def row_bounds(rows, parts):
+    return [16 * (rows // 16 * part // parts) for part in range(parts)] + [rows]
+
+
+def hand_out(sums, keep, sends, sem, first=0, last=None):
     mine = my_piece() // 16
     half = PIECES // 2
-    count = half // len(sends)
-    copies = [pltpu.make_async_copy(sums.at[pl.ds(mine * half, half)], keep, sem.at[0])]
-    for number, send in enumerate(sends):
-        rows = pl.ds((1 - mine) * half + number * count, count)
-        copies.append(pltpu.make_async_copy(sums.at[rows], send, sem.at[1 + number]))
+    last = keep.shape[1] if last is None else last
+    bounds = row_bounds(keep.shape[1], len(sends))
+    copies = []
+    for ref, core, low, high in [(keep, mine, 0, keep.shape[1])] + [
+        (send, 1 - mine, low, high) for send, low, high in zip(sends, bounds, bounds[1:])
+    ]:
+        start, end = max(first, low), min(last, high)
+        if start < end:
+            copies.append(
+                pltpu.make_async_copy(
+                    sums.at[pl.ds(core * half, half), pl.ds(start, end - start)],
+                    ref.at[:, pl.ds(start - low, end - start)],
+                    sem.at[len(copies)],
+                )
+            )
     for copy in copies:
         copy.start()
-    for copy in copies:
-        copy.wait()
+    return copies
 
 
 def back_kernel(
@@ -508,10 +504,10 @@
     weights, grad_attended, grad_out, out_b_sum, gain, shift, query_w, key_w, value_w,
     grad_normed_out, inner, outer, keep, *refs,
 ):
-    sends, owners, refs = refs[:LATE_PARTS], refs[LATE_PARTS:-12], refs[-12:]
+    sends, owners, refs = refs[:LATE_PARTS], refs[LATE_PARTS:-13], refs[-13:]
     (
     key_cat, value_cat, grad_query, key_own, key_pooled, key_lent, value_own, value_pooled,
-    value_lent, sums, small, sem,
+    value_lent, sums, small, sem, rest_sem,
     ) = refs
     width = tokens.shape[2]
     place = lax.axis_index("seq")
@@ -562,6 +558,7 @@
     put_lines(sums, 128, grad_key.astype(BF16))
     grad_value = dot_rows(rows, low_value) + dot_rows(lent_low, lent_value)
     put_lines(sums, 192, grad_value.astype(BF16))
+    copies = hand_out(sums, keep, sends, sem, last=256)
     small[...] = jnp.zeros_like(small)
 
     def total(values):
@@ -598,11 +595,16 @@
                     slot = core * 16 + at + part
                     sums[slot, GROUP_ROWS:] = rows[:, 128 * part : 128 * (part + 1)]
     put_small(sums, 256, small)
-    hand_out(sums, keep, sends, sem)
-
-
-def last_kernel(levels, tokens, gain, grad_mid, grad_normed, inner, outer, *refs):
-    from_users, (grad_tokens, pooled) = refs[:-2], refs[-2:]
+    copies += hand_out(sums, keep, sends, rest_sem, first=256)
+    for copy in copies:
+        copy.wait()
+
+
+def last_kernel(
+    levels, tokens, gain, grad_mid, grad_normed, inner, outer, mid, active, down_w, down_b, *refs
+):
+    from_users, (grad_tokens, output, pooled) = refs[:-3], refs[-3:]
+    output[0] = (mid[...] + dot(active[...], down_w[...]) + down_b[...]).astype(BF16)
     even = lax.axis_index("seq") % 2 == 0
     first = jnp.where(even, outer[...], inner[0:HALO]).astype(F32)
     last = jnp.where(even, inner[0:HALO], outer[...]).astype(F32)
@@ -742,17 +744,35 @@
     return total.astype(BF16)
 
 
-def halves_kernel(kept, *refs):
-    came, (sent_out, kept_out) = refs[:-2], refs[-2:]
-    each = kept.shape[0] // len(came)
+def halves_kernel(count, kept, *refs):
+    came, (kept_out, *sends) = refs[:count], refs[count:]
     for slot in range(kept.shape[0]):
-        out = (kept_out, sent_out)[slot % 2]
-        out[slot // 2] = sum_of(kept[slot], came[slot // each][slot % each])
-
-
-def add_halves(kept, *came):
-    shape = (kept.shape[0] // 2, *kept.shape[1:])
-    return call(halves_kernel, (kept, *came), [(shape, BF16)] * 2, room=12)
+        first = 0
+        for ref in came:
+            last = first + ref.shape[-2]
+            total = sum_of(kept[slot, ..., first:last, :], ref[slot])
+            if slot % 2 == 0:
+                kept_out[slot // 2, ..., first:last, :] = total
+            else:
+                row = 0
+                for send in sends:
+                    end = row + send.shape[-2]
+                    low, high = max(first, row), min(last, end)
+                    if low < high:
+                        send[slot // 2, ..., low - row : high - row, :] = total[
+                            ..., low - first : high - first, :
+                        ]
+                    row = end
+            first = last
+
+
+def add_halves(kept, *came, parts=1):
+    half, rows = (kept.shape[0] // 2, *kept.shape[1:-2]), kept.shape[-2]
+    bounds = row_bounds(rows, parts)
+    sends = [((*half, last - first, 128), BF16) for first, last in zip(bounds, bounds[1:])]
+    kernel = functools.partial(halves_kernel, len(came))
+    kept, *sends = call(kernel, (kept, *came), [((*half, rows, 128), BF16), *sends], room=12)
+    return (sends[0] if parts == 1 else sends), kept
 
 
 def plane_kernel(extra, kept, came, sent_out, kept_out, *complete):
@@ -826,8 +846,9 @@
 
 
 class Group:
-    def __init__(self, keep, sends):
+    def __init__(self, keep, sends, parts=1):
         self.kept = slots(keep)
+        self.parts = parts
         self.came = [slots(swap(send, "seq", 1)) for send in sends]
         self.stage = 0
         self.users = []
@@ -837,10 +858,10 @@
         came = after(self.came, last)
         self.stage += 1
         if stage == 0:
-            sent, self.kept = add_halves(kept, *came)
-            self.came = hop(sent, 0)
+            sent, self.kept = add_halves(kept, *came, parts=self.parts)
+            self.came = hop(sent, 0) if self.parts == 1 else [hop(part, 0) for part in sent]
         elif stage == 1:
-            sent, kept = add_halves(kept, came)
+            sent, kept = add_halves(kept, *(came if self.parts > 1 else [came]))
             self.kept = kept[0]
             self.came = hop(sent[0], 1)
         elif stage == 2 and Z_DIRECT:
@@ -956,7 +977,8 @@
     copies = pltpu.SemaphoreType.DMA((1 + max(MID_PARTS, LATE_PARTS),))
 
     def piece_sums(parts, rows=GROUP_ROWS):
-        sends = [((half // parts, rows, 128), BF16)] * parts
+        bounds = row_bounds(rows, parts)
+        sends = [((half, last - first, 128), BF16) for first, last in zip(bounds, bounds[1:])]
         return [((half, rows, 128), BF16)] + sends
 
     sums_scratch = ((PIECES, GROUP_ROWS, 128), BF16)
@@ -1012,14 +1034,13 @@
     last = ()
     for what in ORDER:
         if what == FEED:
-            output, grad_mid, grad_attended, grad_out, out_b_sum, keep, *sends = call(
+            grad_mid, grad_attended, grad_out, out_b_sum, keep, *sends = call(
                 feed_kernel,
                 (
-                    cotangent, after(mid, last), low_second, active, slope, second_gain, up_weight, down_weight,
-                    down_bias, out_weight, attended,
+                    cotangent, after(mid, last), low_second, slope, second_gain, up_weight, down_weight,
+                    out_weight, attended,
                 ),
                 [
-                    ((1, ROWS, width), BF16),
                     ((ROWS, width), F32),
                     ((ROWS, width), BF16),
                     ((width, width), BF16),
@@ -1027,7 +1048,7 @@
                 ]
                 + piece_sums(MID_PARTS),
                 scratch=[sums_scratch, small_scratch, copies],
-                far_out=range(5, 6 + MID_PARTS),
+                far_out=range(4, 5 + MID_PARTS),
                 room=24,
             )
             sums[2] = Group(keep, sends)
@@ -1060,12 +1081,13 @@
                     ((PIECES, GROUP_ROWS + extra, 128), BF16),
                     small_scratch,
                     copies,
+                    copies,
                 ],
                 far_out=range(3, 4 + LATE_PARTS),
                 room=28,
             )
             sends, owners = sends[:LATE_PARTS], sends[LATE_PARTS:]
-            sums[3] = Group(keep, sends)
+            sums[3] = Group(keep, sends, STEP_PARTS)
             inner_came = swap(inner, "seq", 1)
             outer_came = swap_outer(outer, "seq")
             last = grad_normed
@@ -1074,12 +1096,15 @@
             if not extra:
                 rows = owners[0].reshape(holders, GATHER, width)
                 users = list(lax.all_to_all(rows, "seq", split_axis=0, concat_axis=0, tiled=True))
-            (grad_tokens,) = call(
+            grad_tokens, output = call(
                 functools.partial(last_kernel, levels),
-                (tokens, gain, grad_mid, after(grad_normed, last), inner_came, outer_came, *users),
-                [((1, ROWS, width), F32)],
+                (
+                    tokens, gain, grad_mid, after(grad_normed, last), inner_came, outer_came, mid,
+                    active, down_weight, down_bias, *users,
+                ),
+                [((1, ROWS, width), F32), ((1, ROWS, width), BF16)],
                 scratch=[((ROWS, width), F32)],
-                room=8,
+                room=12,
             )
             last = grad_tokens
         elif what == BORROWED:

time: 132 us -> 126 us (0.955)
  waiting for transfers between devices: 40.6 us -> 33.9 us
  starting transfers between devices: 55.1 us -> 58.9 us
  Pallas kernels: 34.2 us -> 31.5 us
    ppermute x36 -> x35, waiting for transfers between devices: 23.5 us -> 15.8 us  [swap(): return lax.ppermute(array, axis, [(i, i ^ distance) for i in range(count)])]
    pallas_call x28, Pallas kernels: 34.2 us -> 31.5 us  [call(): pl.pallas_call(kernel, out_shape=[jax.ShapeDtypeStruct(s, d) for s, d in...]
    ppermute x36 -> x35, starting transfers between devices: 34.1 us -> 36.6 us  [swap(): return lax.ppermute(array, axis, [(i, i ^ distance) for i in range(count)])]
    ppermute x12, starting transfers between devices: 19.5 us -> 20.8 us  [hop(): return lax.ppermute(array, 'seq', pairs)]
  transfers between devices with their start and end apart: 50 -> 49, of which waited for: 19 -> 15; matrix products, arithmetic and copies ran while one was open for 0% -> 0% of each run, Pallas kernels for 17% -> 17%
where the time goes in v4:
time: 126 us
  starting transfers between devices  58.9 us (47%)
  waiting for transfers between devices  33.9 us (27%)
  Pallas kernels  31.5 us (25%)
    ppermute x35, starting transfers between devices, swap(): return lax.ppermute(array, axis, [(i, i ^ distance) for i in range(count)])  36.6 us
    pallas_call x28, Pallas kernels, call(): pl.pallas_call(kernel, out_shape=[jax.ShapeDtypeStruct(s, d) for s, d in...  31.5 us
    ppermute x12, starting transfers between devices, hop(): return lax.ppermute(array, 'seq', pairs)  20.8 us
    ppermute x12, waiting for transfers between devices, hop(): return lax.ppermute(array, 'seq', pairs)  18.1 us
    ppermute x35, waiting for transfers between devices, swap(): return lax.ppermute(array, axis, [(i, i ^ distance) for i in range(count)])  15.8 us
  transfers between devices with their start and end apart: 49, of which 15 were waited for; matrix products, arithmetic and copies ran while one was open for 0% of the time, Pallas kernels for 17%

profile of v4, /device:TPU:0, one launch (start us, length us, event | category | flops | bytes accessed | tf_op | source)
XLA Modules:
  0.0 126.2 jit_solution(1677043658995663477)
XLA Ops:
  3.7 5.1 %collective-permute-start.4 = (bf16[64,512]{1,0:T(8,128)(2,1)S(1)}, bf16[64,512]{1,0:T(8,128)(2,1)S(1)}, u32[]{:S(2)}, u32[]{:S(2)}) collective-permute-start(bf16[64,512]{1,0:T(8,128)(2,1)S(1)} %shard_map.325.refs_0_), channel_id=1, source_target_pairs={{0,6},{1,7},{2,4},{3,5},{4,2},{5,3},{6,0},{7,1},{8,14},{9,15},{10,... | collective-permute-start | bytes 196616 | tf_op jit(solution)/shard_map/ppermute | solution.py:715
  10.2 3.4 %shard_map.323 = (bf16[1,256,512]{2,1,0:T(8,128)(2,1)S(1)}, f32[1,512]{1,0:T(1,128)S(1)}, f32[1,512]{1,0:T(1,128)S(1)}, bf16[512,512]{1,0:T(8,128)(2,1)S(1)}, f3...) custom-call(bf16[1,256,512]{2,1,0:T(8,128)(2,1)} %tokens.1, ...), custom_call_target="tpu_custom_call" | custom-call | tf_op jit(solution)/shard_map/pallas_call | solution.py:701
  13.9 7.1 %shard_map.326 = (bf16[256,512]{1,0:T(8,128)(2,1)S(1)}, bf16[8,256,384]{2,1,0:T(8,128)(2,1)S(1)}, bf16[320,512]{1,0:T(8,128)(2,1)S(1)}, bf16[320,512]{1,0:T(8,12...) custom-call(s32[1,2]{1,0:T(1,128)S(1)} %copy-done.1, ...), custom_call_target="tpu_custom_call" | custom-call | tf_op jit(solution)/shard_map/pallas_call | solution.py:701
  21.1 3.3 %shard_map.327 = (f32[256,512]{1,0:T(8,128)S(1)}, bf16[256,512]{1,0:T(8,128)(2,1)S(1)}, bf16[512,512]{1,0:T(8,128)(2,1)S(1)}, f32[1,512]{1,0:T(1,128)S(1)}, bf16...) custom-call(bf16[1,256,512]{2,1,0:T(8,128)(2,1)S(1)} %get-tuple-element.181.cotan, ...), custom_call_target="tpu_custom_call" | custom-call | tf_op jit(solution)/shard_map/pallas_call | solution.py:701
  25.3 2.3 %collective-permute-start.11 = (bf16[2,4,272,128]{3,2,1,0:T(8,128)(2,1)S(1)}, bf16[2,4,272,128]{3,2,1,0:T(8,128)(2,1)S(1)}, u32[]{:S(2)}, u32[]{:S(2)}) collective-permute-start(bf16[2,4,272,128]{3,2,1,0:T(8,128)(2,1)S(1)} %get-tuple-element.215), channel_id=1, source_target_pairs={{0,2},{1,5},{2,0},{3,7},{4,6},{5,1},{6,4},{7,3},{8,10},{9,13},{10,... | collective-permute-start | bytes 1671176 | tf_op jit(solution)/shard_map/ppermute | solution.py:737
  27.9 2.0 %collective-permute-start.13 = (bf16[2,4,272,128]{3,2,1,0:T(8,128)(2,1)S(1)}, bf16[2,4,272,128]{3,2,1,0:T(8,128)(2,1)S(1)}, u32[]{:S(2)}, u32[]{:S(2)}) collective-permute-start(bf16[2,4,272,128]{3,2,1,0:T(8,128)(2,1)S(1)} %get-tuple-element.219), channel_id=1, source_target_pairs={{0,2},{1,5},{2,0},{3,7},{4,6},{5,1},{6,4},{7,3},{8,10},{9,13},{10,... | collective-permute-start | bytes 1671176 | tf_op jit(solution)/shard_map/ppermute | solution.py:737
  29.9 6.2 %shard_map.330 = (f32[256,512]{1,0:T(8,128)S(1)}, bf16[112,512]{1,0:T(8,128)(2,1)S(1)}, bf16[112,512]{1,0:T(8,128)(2,1)S(1)}, bf16[16,304,128]{2,1,0:T(8,128)(2,...) custom-call(bf16[1,256,512]{2,1,0:T(8,128)(2,1)S(1)} %get-tuple-elemen, ...), custom_call_target="tpu_custom_call" | custom-call | tf_op jit(solution)/shard_map/pallas_call | solution.py:701
  37.8 5.5 %collective-permute-done.13.refs_0_ = bf16[2,4,272,128]{3,2,1,0:T(8,128)(2,1)S(1)} collective-permute-done((bf16[2,4,272,128]{3,2,1,0:T(8,128)(2,1)S(1)}, bf16[2,4,272,128]{3,2,1,0:T(8,128)(2,1)S(1)}, u32[]{:S(2)}, u32[]{:S(2)}) %collective-permute-start.13) | collective-permute-done | bytes 557088 | tf_op jit(solution)/shard_map/ppermute | solution.py:737
  44.0 2.4 %collective-permute-start.14 = (bf16[2,4,304,128]{3,2,1,0:T(8,128)(2,1)S(1)}, bf16[2,4,304,128]{3,2,1,0:T(8,128)(2,1)S(1)}, u32[]{:S(2)}, u32[]{:S(2)}) collective-permute-start(bf16[2,4,304,128]{3,2,1,0:T(8,128)(2,1)S(1)} %get-tuple-element.228), channel_id=1, source_target_pairs={{0,2},{1,5},{2,0},{3,7},{4,6},{5,1},{6,4},{7,3},{8,10},{9,13},{10,... | collective-permute-start | bytes 1867784 | tf_op jit(solution)/shard_map/ppermute | solution.py:737
  46.8 2.6 %collective-permute-start.15 = (bf16[272,128]{1,0:T(8,128)(2,1)S(1)}, bf16[272,128]{1,0:T(8,128)(2,1)S(1)}, u32[]{:S(2)}, u32[]{:S(2)}) collective-permute-start(bf16[272,128]{1,0:T(8,128)(2,1)S(1)} %get-tuple-element.229), channel_id=1, source_target_pairs={{0,16},{8,24},{16,0},{24,8},{1,17},{9,25},{17,1},{25,9},{2,18},{10... | collective-permute-start | bytes 208904 | tf_op jit(solution)/shard_map/ppermute | solution.py:715
  51.0 5.0 %collective-permute-done.18.came = bf16[4,272,128]{2,1,0:T(8,128)(2,1)S(1)} collective-permute-done((bf16[4,272,128]{2,1,0:T(8,128)(2,1)S(1)}, bf16[4,272,128]{2,1,0:T(8,128)(2,1)S(1)}, u32[]{:S(2)}, u32[]{:S(2)}) %collective-permute-start.18) | collective-permute-done | bytes 278560 | tf_op jit(solution)/shard_map/ppermute | solution.py:737
  59.8 2.8 %collective-permute-start.23 = (bf16[272,128]{1,0:T(8,128)(2,1)S(1)}, bf16[272,128]{1,0:T(8,128)(2,1)S(1)}, u32[]{:S(2)}, u32[]{:S(2)}) collective-permute-start(bf16[272,128]{1,0:T(8,128)(2,1)S(1)} %get-tuple-element.241), channel_id=1, source_target_pairs={{0,16},{8,24},{16,0},{24,8},{1,17},{9,25},{17,1},{25,9},{2,18},{10... | collective-permute-start | bytes 208904 | tf_op jit(solution)/shard_map/ppermute | solution.py:715
  66.0 4.8 %collective-permute-start.21 = (bf16[272,128]{1,0:T(8,128)(2,1)S(1)}, bf16[272,128]{1,0:T(8,128)(2,1)S(1)}, u32[]{:S(2)}, u32[]{:S(2)}) collective-permute-start(bf16[272,128]{1,0:T(8,128)(2,1)S(1)} %shard_map.336.whole), channel_id=1, source_target_pairs={{0,24},{8,16},{16,8},{24,0},{1,25},{9,17},{17,9},{25,1},{2,26},{10... | collective-permute-start | bytes 208904 | tf_op jit(solution)/shard_map/ppermute | solution.py:715
  72.4 2.9 %collective-permute-start.33 = (bf16[272,128]{1,0:T(8,128)(2,1)S(1)}, bf16[272,128]{1,0:T(8,128)(2,1)S(1)}, u32[]{:S(2)}, u32[]{:S(2)}) collective-permute-start(bf16[272,128]{1,0:T(8,128)(2,1)S(1)} %shard_map.338.whole), channel_id=1, source_target_pairs={{0,24},{8,16},{16,8},{24,0},{1,25},{9,17},{17,9},{25,1},{2,26},{10... | collective-permute-start | bytes 208904 | tf_op jit(solution)/shard_map/ppermute | solution.py:715
  75.9 2.2 %collective-permute-done.20.two = bf16[272,128]{1,0:T(8,128)(2,1)S(1)} collective-permute-done((bf16[272,128]{1,0:T(8,128)(2,1)S(1)}, bf16[272,128]{1,0:T(8,128)(2,1)S(1)}, u32[]{:S(2)}, u32[]{:S(2)}) %collective-permute-start.20) | collective-permute-done | bytes 69664 | tf_op jit(solution)/shard_map/ppermute | solution.py:715
  78.0 5.9 %collective-permute-start.31 = (bf16[1,4,272,128]{3,2,1,0:T(8,128)(2,1)S(1)}, bf16[1,4,272,128]{3,2,1,0:T(8,128)(2,1)S(1)}, u32[]{:S(2)}, u32[]{:S(2)}) collective-permute-start(bf16[1,4,272,128]{3,2,1,0:T(8,128)(2,1)S(1)} %shard_map.339.mine), channel_id=1, source_target_pairs={{0,4},{1,3},{2,6},{3,1},{4,0},{5,7},{6,2},{7,5},{8,12},{9,11},{10,... | collective-permute-start | bytes 835592 | tf_op jit(solution)/shard_map/ppermute | solution.py:737
  84.1 2.8 %collective-permute-start.38 = (bf16[1,4,272,128]{3,2,1,0:T(8,128)(2,1)S(1)}, bf16[1,4,272,128]{3,2,1,0:T(8,128)(2,1)S(1)}, u32[]{:S(2)}, u32[]{:S(2)}) collective-permute-start(bf16[1,4,272,128]{3,2,1,0:T(8,128)(2,1)S(1)} %shard_map.341.mine), channel_id=1, source_target_pairs={{0,4},{1,3},{2,6},{3,1},{4,0},{5,7},{6,2},{7,5},{8,12},{9,11},{10,... | collective-permute-start | bytes 835592 | tf_op jit(solution)/shard_map/ppermute | solution.py:737
  90.5 3.6 %collective-permute-done.28.refs_1_ = bf16[272,128]{1,0:T(8,128)(2,1)S(1)} collective-permute-done((bf16[272,128]{1,0:T(8,128)(2,1)S(1)}, bf16[272,128]{1,0:T(8,128)(2,1)S(1)}, u32[]{:S(2)}, u32[]{:S(2)}) %collective-permute-start.28) | collective-permute-done | bytes 69664 | tf_op jit(solution)/shard_map/ppermute | solution.py:715
  99.7 3.3 %collective-permute-done.36.three = bf16[272,128]{1,0:T(8,128)(2,1)S(1)} collective-permute-done((bf16[272,128]{1,0:T(8,128)(2,1)S(1)}, bf16[272,128]{1,0:T(8,128)(2,1)S(1)}, u32[]{:S(2)}, u32[]{:S(2)}) %collective-permute-start.36) | collective-permute-done | bytes 69664 | tf_op jit(solution)/shard_map/ppermute | solution.py:715
  102.9 2.6 %collective-permute-done.35.two = bf16[272,128]{1,0:T(8,128)(2,1)S(1)} collective-permute-done((bf16[272,128]{1,0:T(8,128)(2,1)S(1)}, bf16[272,128]{1,0:T(8,128)(2,1)S(1)}, u32[]{:S(2)}, u32[]{:S(2)}) %collective-permute-start.35) | collective-permute-done | bytes 69664 | tf_op jit(solution)/shard_map/ppermute | solution.py:715
  108.2 4.0 %collective-permute-done.39.came = bf16[1,4,272,128]{3,2,1,0:T(8,128)(2,1)S(1)} collective-permute-done((bf16[1,4,272,128]{3,2,1,0:T(8,128)(2,1)S(1)}, bf16[1,4,272,128]{3,2,1,0:T(8,128)(2,1)S(1)}, u32[]{:S(2)}, u32[]{:S(2)}) %collective-permute-start.39) | collective-permute-done | bytes 278560 | tf_op jit(solution)/shard_map/ppermute | solution.py:737
  115.0 2.4 %shard_map.348 = (f32[512,2048]{1,0:T(8,128)}, f32[16,128]{1,0:T(8,128)}, f32[4,128]{1,0:T(4,128)}, f32[4,128]{1,0:T(4,128)}) custom-call(bf16[2,4,272,128]{3,2,1,0:T(8,128)(2,1)S(1)} %shard_map.344.refs_0_, bf16[2,4,272,128]{3,2,1,0:T(8,128)(2,1)S(1)} %collective-permute-done.40.refs_1_, bf16[2,4,272,128]{3,2,1,0:T(8,128)(2,1)S(1)} %collective-permute-done.45.refs_2_, ...), custom_call_target="tpu_custom_call" | custom-call | tf_op jit(solution)/shard_map/pallas_call | solution.py:701
  117.4 2.4 %shard_map.349 = (f32[2048,512]{1,0:T(8,128)}, f32[4,128]{1,0:T(4,128)}) custom-call(bf16[2,4,272,128]{3,2,1,0:T(8,128)(2,1)S(1)} %shard_map.342.refs_0_, bf16[2,4,272,128]{3,2,1,0:T(8,128)(2,1)S(1)} %collective-permute-done.41.refs_1_, bf16[2,4,272,128]{3,2,1,0:T(8,128)(2,1)S(1)} %collective-permute-done.43.refs_2_, ...), custom_call_target="tpu_custom_call" | custom-call | tf_op jit(solution)/shard_map/pallas_call | solution.py:701
  123.8 2.4 %shard_map.350 = (f32[512,512]{1,0:T(8,128)}, f32[512,512]{1,0:T(8,128)}, f32[512,512]{1,0:T(8,128)}, f32[512,512]{1,0:T(8,128)}, f32[4,128]{1,0:T(4,128)}, /*in...) custom-call(bf16[2,4,272,128]{3,2,1,0:T(8,128)(2,1)S(1)} %shard_map.346.refs_0_, ...), custom_call_target="tpu_custom_call" | custom-call | tf_op jit(solution)/shard_map/pallas_call | solution.py:701
  (106 shorter events, 38.2 us)
Async XLA Ops:
  2.7 11.0 %collective-permute-start.1 = (bf16[112,512]{1,0:T(8,128)(2,1)S(1)}, bf16[112,512]{1,0:T(8,128)(2,1)S(1)}, u32[]{:S(2)}, u32[]{:S(2)}) collective-permute-start(bf16[112,512]{1,0:T(8,128)(2,1)S(1)} %get-tuple-element.170), channel_id=1, source_target_pairs={{1,2},{3,4},{5,6},{2,1},{4,3},{6,5},{9,10},{11,12},{13,14},{10,9},... | collective-permute-start | bytes 344072 | tf_op jit(solution)/shard_map/ppermute | solution.py:721
  3.7 10.0 %collective-permute-start.4 = (bf16[64,512]{1,0:T(8,128)(2,1)S(1)}, bf16[64,512]{1,0:T(8,128)(2,1)S(1)}, u32[]{:S(2)}, u32[]{:S(2)}) collective-permute-start(bf16[64,512]{1,0:T(8,128)(2,1)S(1)} %shard_map.325.refs_0_), channel_id=1, source_target_pairs={{0,6},{1,7},{2,4},{3,5},{4,2},{5,3},{6,0},{7,1},{8,14},{9,15},{10,... | collective-permute-start | bytes 196616 | tf_op jit(solution)/shard_map/ppermute | solution.py:715
  25.3 11.5 %collective-permute-start.11 = (bf16[2,4,272,128]{3,2,1,0:T(8,128)(2,1)S(1)}, bf16[2,4,272,128]{3,2,1,0:T(8,128)(2,1)S(1)}, u32[]{:S(2)}, u32[]{:S(2)}) collective-permute-start(bf16[2,4,272,128]{3,2,1,0:T(8,128)(2,1)S(1)} %get-tuple-element.215), channel_id=1, source_target_pairs={{0,2},{1,5},{2,0},{3,7},{4,6},{5,1},{6,4},{7,3},{8,10},{9,13},{10,... | collective-permute-start | bytes 1671176 | tf_op jit(solution)/shard_map/ppermute | solution.py:737
  27.9 15.3 %collective-permute-start.13 = (bf16[2,4,272,128]{3,2,1,0:T(8,128)(2,1)S(1)}, bf16[2,4,272,128]{3,2,1,0:T(8,128)(2,1)S(1)}, u32[]{:S(2)}, u32[]{:S(2)}) collective-permute-start(bf16[2,4,272,128]{3,2,1,0:T(8,128)(2,1)S(1)} %get-tuple-element.219), channel_id=1, source_target_pairs={{0,2},{1,5},{2,0},{3,7},{4,6},{5,1},{6,4},{7,3},{8,10},{9,13},{10,... | collective-permute-start | bytes 1671176 | tf_op jit(solution)/shard_map/ppermute | solution.py:737
  44.0 13.6 %collective-permute-start.14 = (bf16[2,4,304,128]{3,2,1,0:T(8,128)(2,1)S(1)}, bf16[2,4,304,128]{3,2,1,0:T(8,128)(2,1)S(1)}, u32[]{:S(2)}, u32[]{:S(2)}) collective-permute-start(bf16[2,4,304,128]{3,2,1,0:T(8,128)(2,1)S(1)} %get-tuple-element.228), channel_id=1, source_target_pairs={{0,2},{1,5},{2,0},{3,7},{4,6},{5,1},{6,4},{7,3},{8,10},{9,13},{10,... | collective-permute-start | bytes 1867784 | tf_op jit(solution)/shard_map/ppermute | solution.py:737
  46.4 9.6 %collective-permute-start.18 = (bf16[4,272,128]{2,1,0:T(8,128)(2,1)S(1)}, bf16[4,272,128]{2,1,0:T(8,128)(2,1)S(1)}, u32[]{:S(2)}, u32[]{:S(2)}) collective-permute-start(bf16[4,272,128]{2,1,0:T(8,128)(2,1)S(1)} %bitcast.46), channel_id=1, source_target_pairs={{0,4},{1,3},{2,6},{3,1},{4,0},{5,7},{6,2},{7,5},{8,12},{9,11},{10,... | collective-permute-start | bytes 835592 | tf_op jit(solution)/shard_map/ppermute | solution.py:737
  46.8 9.2 %collective-permute-start.15 = (bf16[272,128]{1,0:T(8,128)(2,1)S(1)}, bf16[272,128]{1,0:T(8,128)(2,1)S(1)}, u32[]{:S(2)}, u32[]{:S(2)}) collective-permute-start(bf16[272,128]{1,0:T(8,128)(2,1)S(1)} %get-tuple-element.229), channel_id=1, source_target_pairs={{0,16},{8,24},{16,0},{24,8},{1,17},{9,25},{17,1},{25,9},{2,18},{10... | collective-permute-start | bytes 208904 | tf_op jit(solution)/shard_map/ppermute | solution.py:715
  57.7 26.2 %collective-permute-start.19 = (bf16[4,304,128]{2,1,0:T(8,128)(2,1)S(1)}, bf16[4,304,128]{2,1,0:T(8,128)(2,1)S(1)}, u32[]{:S(2)}, u32[]{:S(2)}) collective-permute-start(bf16[4,304,128]{2,1,0:T(8,128)(2,1)S(1)} %bitcast.45), channel_id=1, source_target_pairs={{0,4},{1,3},{2,6},{3,1},{4,0},{5,7},{6,2},{7,5},{8,12},{9,11},{10,... | collective-permute-start | bytes 933896 | tf_op jit(solution)/shard_map/ppermute | solution.py:737
  62.6 8.2 %collective-permute-start.24 = (bf16[272,128]{1,0:T(8,128)(2,1)S(1)}, bf16[272,128]{1,0:T(8,128)(2,1)S(1)}, u32[]{:S(2)}, u32[]{:S(2)}) collective-permute-start(bf16[272,128]{1,0:T(8,128)(2,1)S(1)} %get-tuple-element.242), channel_id=1, source_target_pairs={{0,24},{8,16},{16,8},{24,0},{1,25},{9,17},{17,9},{25,1},{2,26},{10... | collective-permute-start | bytes 208904 | tf_op jit(solution)/shard_map/ppermute | solution.py:715
  63.9 8.3 %collective-permute-start.25 = (bf16[272,128]{1,0:T(8,128)(2,1)S(1)}, bf16[272,128]{1,0:T(8,128)(2,1)S(1)}, u32[]{:S(2)}, u32[]{:S(2)}) collective-permute-start(bf16[272,128]{1,0:T(8,128)(2,1)S(1)} %get-tuple-element.243), channel_id=1, source_target_pairs={{0,8},{8,0},{16,24},{24,16},{1,9},{9,1},{17,25},{25,17},{2,10},{10... | collective-permute-start | bytes 208904 | tf_op jit(solution)/shard_map/ppermute | solution.py:715
  64.2 8.2 %collective-permute-start.22 = (bf16[272,128]{1,0:T(8,128)(2,1)S(1)}, bf16[272,128]{1,0:T(8,128)(2,1)S(1)}, u32[]{:S(2)}, u32[]{:S(2)}) collective-permute-start(bf16[272,128]{1,0:T(8,128)(2,1)S(1)} %shard_map.336.whole), channel_id=1, source_target_pairs={{0,8},{8,0},{16,24},{24,16},{1,9},{9,1},{17,25},{25,17},{2,10},{10... | collective-permute-start | bytes 208904 | tf_op jit(solution)/shard_map/ppermute | solution.py:715
  66.0 9.3 %collective-permute-start.21 = (bf16[272,128]{1,0:T(8,128)(2,1)S(1)}, bf16[272,128]{1,0:T(8,128)(2,1)S(1)}, u32[]{:S(2)}, u32[]{:S(2)}) collective-permute-start(bf16[272,128]{1,0:T(8,128)(2,1)S(1)} %shard_map.336.whole), channel_id=1, source_target_pairs={{0,24},{8,16},{16,8},{24,0},{1,25},{9,17},{17,9},{25,1},{2,26},{10... | collective-permute-start | bytes 208904 | tf_op jit(solution)/shard_map/ppermute | solution.py:715
  72.3 11.7 %collective-permute-start.34 = (bf16[272,128]{1,0:T(8,128)(2,1)S(1)}, bf16[272,128]{1,0:T(8,128)(2,1)S(1)}, u32[]{:S(2)}, u32[]{:S(2)}) collective-permute-start(bf16[272,128]{1,0:T(8,128)(2,1)S(1)} %shard_map.338.whole), channel_id=1, source_target_pairs={{0,8},{8,0},{16,24},{24,16},{1,9},{9,1},{17,25},{25,17},{2,10},{10... | collective-permute-start | bytes 208904 | tf_op jit(solution)/shard_map/ppermute | solution.py:715
  72.4 11.6 %collective-permute-start.33 = (bf16[272,128]{1,0:T(8,128)(2,1)S(1)}, bf16[272,128]{1,0:T(8,128)(2,1)S(1)}, u32[]{:S(2)}, u32[]{:S(2)}) collective-permute-start(bf16[272,128]{1,0:T(8,128)(2,1)S(1)} %shard_map.338.whole), channel_id=1, source_target_pairs={{0,24},{8,16},{16,8},{24,0},{1,25},{9,17},{17,9},{25,1},{2,26},{10... | collective-permute-start | bytes 208904 | tf_op jit(solution)/shard_map/ppermute | solution.py:715
  75.3 8.7 %collective-permute-start.32 = (bf16[272,128]{1,0:T(8,128)(2,1)S(1)}, bf16[272,128]{1,0:T(8,128)(2,1)S(1)}, u32[]{:S(2)}, u32[]{:S(2)}) collective-permute-start(bf16[272,128]{1,0:T(8,128)(2,1)S(1)} %shard_map.338.whole), channel_id=1, source_target_pairs={{0,16},{8,24},{16,0},{24,8},{1,17},{9,25},{17,1},{25,9},{2,18},{10... | collective-permute-start | bytes 208904 | tf_op jit(solution)/shard_map/ppermute | solution.py:715
  78.0 12.3 %collective-permute-start.31 = (bf16[1,4,272,128]{3,2,1,0:T(8,128)(2,1)S(1)}, bf16[1,4,272,128]{3,2,1,0:T(8,128)(2,1)S(1)}, u32[]{:S(2)}, u32[]{:S(2)}) collective-permute-start(bf16[1,4,272,128]{3,2,1,0:T(8,128)(2,1)S(1)} %shard_map.339.mine), channel_id=1, source_target_pairs={{0,4},{1,3},{2,6},{3,1},{4,0},{5,7},{6,2},{7,5},{8,12},{9,11},{10,... | collective-permute-start | bytes 835592 | tf_op jit(solution)/shard_map/ppermute | solution.py:737
  84.1 10.8 %collective-permute-start.38 = (bf16[1,4,272,128]{3,2,1,0:T(8,128)(2,1)S(1)}, bf16[1,4,272,128]{3,2,1,0:T(8,128)(2,1)S(1)}, u32[]{:S(2)}, u32[]{:S(2)}) collective-permute-start(bf16[1,4,272,128]{3,2,1,0:T(8,128)(2,1)S(1)} %shard_map.341.mine), channel_id=1, source_target_pairs={{0,4},{1,3},{2,6},{3,1},{4,0},{5,7},{6,2},{7,5},{8,12},{9,11},{10,... | collective-permute-start | bytes 835592 | tf_op jit(solution)/shard_map/ppermute | solution.py:737
  90.4 16.7 %collective-permute-start.41 = (bf16[2,4,272,128]{3,2,1,0:T(8,128)(2,1)S(1)}, bf16[2,4,272,128]{3,2,1,0:T(8,128)(2,1)S(1)}, u32[]{:S(2)}, u32[]{:S(2)}) collective-permute-start(bf16[2,4,272,128]{3,2,1,0:T(8,128)(2,1)S(1)} %shard_map.342.refs_0_), channel_id=1, source_target_pairs={{0,2},{1,5},{2,0},{3,7},{4,6},{5,1},{6,4},{7,3},{8,10},{9,13},{10,... | collective-permute-start | bytes 1671176 | tf_op jit(solution)/shard_map/ppermute | solution.py:737
  94.9 12.2 %collective-permute-start.40 = (bf16[2,4,272,128]{3,2,1,0:T(8,128)(2,1)S(1)}, bf16[2,4,272,128]{3,2,1,0:T(8,128)(2,1)S(1)}, u32[]{:S(2)}, u32[]{:S(2)}) collective-permute-start(bf16[2,4,272,128]{3,2,1,0:T(8,128)(2,1)S(1)} %shard_map.344.refs_0_), channel_id=1, source_target_pairs={{0,2},{1,5},{2,0},{3,7},{4,6},{5,1},{6,4},{7,3},{8,10},{9,13},{10,... | collective-permute-start | bytes 1671176 | tf_op jit(solution)/shard_map/ppermute | solution.py:737
  107.2 7.8 %collective-permute-start.45 = (bf16[2,4,272,128]{3,2,1,0:T(8,128)(2,1)S(1)}, bf16[2,4,272,128]{3,2,1,0:T(8,128)(2,1)S(1)}, u32[]{:S(2)}, u32[]{:S(2)}) collective-permute-start(bf16[2,4,272,128]{3,2,1,0:T(8,128)(2,1)S(1)} %shard_map.344.refs_0_), channel_id=1, source_target_pairs={{0,1},{1,0},{2,3},{3,2},{4,5},{5,4},{6,7},{7,6},{8,9},{9,8},{10,11... | collective-permute-start | bytes 1671176 | tf_op jit(solution)/shard_map/ppermute | solution.py:715
  107.2 7.8 %collective-permute-start.46 = (bf16[2,4,272,128]{3,2,1,0:T(8,128)(2,1)S(1)}, bf16[2,4,272,128]{3,2,1,0:T(8,128)(2,1)S(1)}, u32[]{:S(2)}, u32[]{:S(2)}) collective-permute-start(bf16[2,4,272,128]{3,2,1,0:T(8,128)(2,1)S(1)} %collective-permute-done.40.refs_1_), channel_id=1, source_target_pairs={{0,1},{1,0},{2,3},{3,2},{4,5},{5,4},{6,7},{7,6},{8,9},{9,8},{10,11... | collective-permute-start | bytes 1671176 | tf_op jit(solution)/shard_map/ppermute | solution.py:715
  107.7 9.7 %collective-permute-start.43 = (bf16[2,4,272,128]{3,2,1,0:T(8,128)(2,1)S(1)}, bf16[2,4,272,128]{3,2,1,0:T(8,128)(2,1)S(1)}, u32[]{:S(2)}, u32[]{:S(2)}) collective-permute-start(bf16[2,4,272,128]{3,2,1,0:T(8,128)(2,1)S(1)} %shard_map.342.refs_0_), channel_id=1, source_target_pairs={{0,1},{1,0},{2,3},{3,2},{4,5},{5,4},{6,7},{7,6},{8,9},{9,8},{10,11... | collective-permute-start | bytes 1671176 | tf_op jit(solution)/shard_map/ppermute | solution.py:715
  107.8 9.7 %collective-permute-start.44 = (bf16[2,4,272,128]{3,2,1,0:T(8,128)(2,1)S(1)}, bf16[2,4,272,128]{3,2,1,0:T(8,128)(2,1)S(1)}, u32[]{:S(2)}, u32[]{:S(2)}) collective-permute-start(bf16[2,4,272,128]{3,2,1,0:T(8,128)(2,1)S(1)} %collective-permute-done.41.refs_1_), channel_id=1, source_target_pairs={{0,1},{1,0},{2,3},{3,2},{4,5},{5,4},{6,7},{7,6},{8,9},{9,8},{10,11... | collective-permute-start | bytes 1671176 | tf_op jit(solution)/shard_map/ppermute | solution.py:715
  112.2 9.6 %collective-permute-start.42 = (bf16[2,4,272,128]{3,2,1,0:T(8,128)(2,1)S(1)}, bf16[2,4,272,128]{3,2,1,0:T(8,128)(2,1)S(1)}, u32[]{:S(2)}, u32[]{:S(2)}) collective-permute-start(bf16[2,4,272,128]{3,2,1,0:T(8,128)(2,1)S(1)} %shard_map.346.refs_0_), channel_id=1, source_target_pairs={{0,2},{1,5},{2,0},{3,7},{4,6},{5,1},{6,4},{7,3},{8,10},{9,13},{10,... | collective-permute-start | bytes 1671176 | tf_op jit(solution)/shard_map/ppermute | solution.py:737
  (27 other events, 152.1 us)

commit v5 on v4

--- a/solution.py
+++ b/solution.py
@@ -429,11 +429,11 @@
 
 
 FEED, BACK, BORROWED, LAST = "feed", "back", "borrowed", "last"
-ORDER = (FEED, 1, 2, BACK, 1, 2, 1, 3, 2, 1, 3, BORROWED, 2, 1, 3, 2, 1, 3, 2, 3, 1, 2, 3, LAST, 2, 1, 3, 3)
+ORDER = (FEED, 1, 2, BACK, 1, 2, 1, 3, 2, 1, BORROWED, 3, 2, 1, 3, 2, 1, 3, 2, 3, 1, 2, 3, LAST, 2, 1, 3, 3)
 STEP_PARTS = 1
 Z_DIRECT = True
 GROUP_ROWS = 256 + SMALL
-MID_PARTS, LATE_PARTS = 2, 3
+MID_PARTS, LATE_PARTS = 1, 3
 
 
 def put_vector(small, row, vector):

time: 126 us -> 124 us (0.984)
  starting transfers between devices: 58.9 us -> 50.1 us
  waiting for transfers between devices: 33.9 us -> 40 us
    ppermute x35 -> x34, waiting for transfers between devices: 15.8 us -> 23.3 us  [swap(): return lax.ppermute(array, axis, [(i, i ^ distance) for i in range(count)])]
    ppermute x12, starting transfers between devices: 20.8 us -> 16.1 us  [hop(): return lax.ppermute(array, 'seq', pairs)]
    ppermute x35 -> x34, starting transfers between devices: 36.6 us -> 32.5 us  [swap(): return lax.ppermute(array, axis, [(i, i ^ distance) for i in range(count)])]
    ppermute x12, waiting for transfers between devices: 18.1 us -> 16.8 us  [hop(): return lax.ppermute(array, 'seq', pairs)]
  transfers between devices with their start and end apart: 49 -> 48, of which waited for: 15 -> 22; matrix products, arithmetic and copies ran while one was open for 0% -> 0% of each run, Pallas kernels for 17% -> 17%
where the time goes in v5:
time: 124 us
  starting transfers between devices  50.1 us (40%)
  waiting for transfers between devices  40 us (32%)
  Pallas kernels  31.6 us (25%)
    ppermute x34, starting transfers between devices, swap(): return lax.ppermute(array, axis, [(i, i ^ distance) for i in range(count)])  32.5 us
    pallas_call x28, Pallas kernels, call(): pl.pallas_call(kernel, out_shape=[jax.ShapeDtypeStruct(s, d) for s, d in...  31.6 us
    ppermute x34, waiting for transfers between devices, swap(): return lax.ppermute(array, axis, [(i, i ^ distance) for i in range(count)])  23.3 us
    ppermute x12, waiting for transfers between devices, hop(): return lax.ppermute(array, 'seq', pairs)  16.8 us
    ppermute x12, starting transfers between devices, hop(): return lax.ppermute(array, 'seq', pairs)  16.1 us
  transfers between devices with their start and end apart: 48, of which 22 were waited for; matrix products, arithmetic and copies ran while one was open for 0% of the time, Pallas kernels for 17%

profile of v5, /device:TPU:0, one launch (start us, length us, event | category | flops | bytes accessed | tf_op | source)
XLA Modules:
  0.0 123.6 jit_solution(7376865162138590730)
XLA Ops:
  3.7 5.1 %collective-permute-start.4 = (bf16[64,512]{1,0:T(8,128)(2,1)S(1)}, bf16[64,512]{1,0:T(8,128)(2,1)S(1)}, u32[]{:S(2)}, u32[]{:S(2)}) collective-permute-start(bf16[64,512]{1,0:T(8,128)(2,1)S(1)} %shard_map.325.refs_0_), channel_id=1, source_target_pairs={{0,6},{1,7},{2,4},{3,5},{4,2},{5,3},{6,0},{7,1},{8,14},{9,15},{10,... | collective-permute-start | bytes 196616 | tf_op jit(solution)/shard_map/ppermute | solution.py:715
  10.2 3.4 %shard_map.323 = (bf16[1,256,512]{2,1,0:T(8,128)(2,1)S(1)}, f32[1,512]{1,0:T(1,128)S(1)}, f32[1,512]{1,0:T(1,128)S(1)}, bf16[512,512]{1,0:T(8,128)(2,1)S(1)}, f3...) custom-call(bf16[1,256,512]{2,1,0:T(8,128)(2,1)} %tokens.1, ...), custom_call_target="tpu_custom_call" | custom-call | tf_op jit(solution)/shard_map/pallas_call | solution.py:701
  13.9 7.1 %shard_map.326 = (bf16[256,512]{1,0:T(8,128)(2,1)S(1)}, bf16[8,256,384]{2,1,0:T(8,128)(2,1)S(1)}, bf16[320,512]{1,0:T(8,128)(2,1)S(1)}, bf16[320,512]{1,0:T(8,12...) custom-call(s32[1,2]{1,0:T(1,128)S(1)} %copy-done.1, ...), custom_call_target="tpu_custom_call" | custom-call | tf_op jit(solution)/shard_map/pallas_call | solution.py:701
  21.1 3.4 %shard_map.327 = (f32[256,512]{1,0:T(8,128)S(1)}, bf16[256,512]{1,0:T(8,128)(2,1)S(1)}, bf16[512,512]{1,0:T(8,128)(2,1)S(1)}, f32[1,512]{1,0:T(1,128)S(1)}, bf16...) custom-call(bf16[1,256,512]{2,1,0:T(8,128)(2,1)S(1)} %get-tuple-element.179.cotangent, ...), custom_call_target="tpu_custom_call" | custom-call | tf_op jit(solution)/shard_map/pallas_call | solution.py:701
  25.3 2.3 %collective-permute-start.10 = (bf16[2,4,272,128]{3,2,1,0:T(8,128)(2,1)S(1)}, bf16[2,4,272,128]{3,2,1,0:T(8,128)(2,1)S(1)}, u32[]{:S(2)}, u32[]{:S(2)}) collective-permute-start(bf16[2,4,272,128]{3,2,1,0:T(8,128)(2,1)S(1)} %get-tuple-element.211), channel_id=1, source_target_pairs={{0,2},{1,5},{2,0},{3,7},{4,6},{5,1},{6,4},{7,3},{8,10},{9,13},{10,... | collective-permute-start | bytes 1671176 | tf_op jit(solution)/shard_map/ppermute | solution.py:737
  27.9 2.1 %collective-permute-start.12 = (bf16[2,4,272,128]{3,2,1,0:T(8,128)(2,1)S(1)}, bf16[2,4,272,128]{3,2,1,0:T(8,128)(2,1)S(1)}, u32[]{:S(2)}, u32[]{:S(2)}) collective-permute-start(bf16[2,4,272,128]{3,2,1,0:T(8,128)(2,1)S(1)} %get-tuple-element.215), channel_id=1, source_target_pairs={{0,2},{1,5},{2,0},{3,7},{4,6},{5,1},{6,4},{7,3},{8,10},{9,13},{10,... | collective-permute-start | bytes 1671176 | tf_op jit(solution)/shard_map/ppermute | solution.py:737
  30.0 6.2 %shard_map.330 = (f32[256,512]{1,0:T(8,128)S(1)}, bf16[112,512]{1,0:T(8,128)(2,1)S(1)}, bf16[112,512]{1,0:T(8,128)(2,1)S(1)}, bf16[16,304,128]{2,1,0:T(8,128)(2,...) custom-call(bf16[1,256,512]{2,1,0:T(8,128)(2,1)S(1)} %get-tuple-elemen, ...), custom_call_target="tpu_custom_call" | custom-call | tf_op jit(solution)/shard_map/pallas_call | solution.py:701
  37.8 5.4 %collective-permute-done.12.refs_0_ = bf16[2,4,272,128]{3,2,1,0:T(8,128)(2,1)S(1)} collective-permute-done((bf16[2,4,272,128]{3,2,1,0:T(8,128)(2,1)S(1)}, bf16[2,4,272,128]{3,2,1,0:T(8,128)(2,1)S(1)}, u32[]{:S(2)}, u32[]{:S(2)}) %collective-permute-start.12) | collective-permute-done | bytes 557088 | tf_op jit(solution)/shard_map/ppermute | solution.py:737
  44.0 2.3 %collective-permute-start.13 = (bf16[2,4,304,128]{3,2,1,0:T(8,128)(2,1)S(1)}, bf16[2,4,304,128]{3,2,1,0:T(8,128)(2,1)S(1)}, u32[]{:S(2)}, u32[]{:S(2)}) collective-permute-start(bf16[2,4,304,128]{3,2,1,0:T(8,128)(2,1)S(1)} %get-tuple-element.224), channel_id=1, source_target_pairs={{0,2},{1,5},{2,0},{3,7},{4,6},{5,1},{6,4},{7,3},{8,10},{9,13},{10,... | collective-permute-start | bytes 1867784 | tf_op jit(solution)/shard_map/ppermute | solution.py:737
  46.6 2.5 %collective-permute-start.16 = (bf16[272,128]{1,0:T(8,128)(2,1)S(1)}, bf16[272,128]{1,0:T(8,128)(2,1)S(1)}, u32[]{:S(2)}, u32[]{:S(2)}) collective-permute-start(bf16[272,128]{1,0:T(8,128)(2,1)S(1)} %get-tuple-element.227), channel_id=1, source_target_pairs={{0,16},{8,24},{16,0},{24,8},{1,17},{9,25},{17,1},{25,9},{2,18},{10... | collective-permute-start | bytes 208904 | tf_op jit(solution)/shard_map/ppermute | solution.py:715
  50.0 5.9 %collective-permute-done.19.came = bf16[4,272,128]{2,1,0:T(8,128)(2,1)S(1)} collective-permute-done((bf16[4,272,128]{2,1,0:T(8,128)(2,1)S(1)}, bf16[4,272,128]{2,1,0:T(8,128)(2,1)S(1)}, u32[]{:S(2)}, u32[]{:S(2)}) %collective-permute-start.19) | collective-permute-done | bytes 278560 | tf_op jit(solution)/shard_map/ppermute | solution.py:737
  55.9 3.6 %collective-permute-start.17 = (bf16[272,128]{1,0:T(8,128)(2,1)S(1)}, bf16[272,128]{1,0:T(8,128)(2,1)S(1)}, u32[]{:S(2)}, u32[]{:S(2)}) collective-permute-start(bf16[272,128]{1,0:T(8,128)(2,1)S(1)} %get-tuple-element.228), channel_id=1, source_target_pairs={{0,24},{8,16},{16,8},{24,0},{1,25},{9,17},{17,9},{25,1},{2,26},{10... | collective-permute-start | bytes 208904 | tf_op jit(solution)/shard_map/ppermute | solution.py:715
  59.6 2.4 %collective-permute-done.17.refs_2_ = bf16[272,128]{1,0:T(8,128)(2,1)S(1)} collective-permute-done((bf16[272,128]{1,0:T(8,128)(2,1)S(1)}, bf16[272,128]{1,0:T(8,128)(2,1)S(1)}, u32[]{:S(2)}, u32[]{:S(2)}) %collective-permute-start.17) | collective-permute-done | bytes 69664 | tf_op jit(solution)/shard_map/ppermute | solution.py:715
  64.7 3.1 %collective-permute-start.25 = (bf16[272,128]{1,0:T(8,128)(2,1)S(1)}, bf16[272,128]{1,0:T(8,128)(2,1)S(1)}, u32[]{:S(2)}, u32[]{:S(2)}) collective-permute-start(bf16[272,128]{1,0:T(8,128)(2,1)S(1)} %get-tuple-element.242), channel_id=1, source_target_pairs={{0,24},{8,16},{16,8},{24,0},{1,25},{9,17},{17,9},{25,1},{2,26},{10... | collective-permute-start | bytes 208904 | tf_op jit(solution)/shard_map/ppermute | solution.py:715
  69.9 2.1 %collective-permute-done.24.refs_1_ = bf16[272,128]{1,0:T(8,128)(2,1)S(1)} collective-permute-done((bf16[272,128]{1,0:T(8,128)(2,1)S(1)}, bf16[272,128]{1,0:T(8,128)(2,1)S(1)}, u32[]{:S(2)}, u32[]{:S(2)}) %collective-permute-start.24) | collective-permute-done | bytes 69664 | tf_op jit(solution)/shard_map/ppermute | solution.py:715
  74.3 2.2 %collective-permute-start.33 = (bf16[272,128]{1,0:T(8,128)(2,1)S(1)}, bf16[272,128]{1,0:T(8,128)(2,1)S(1)}, u32[]{:S(2)}, u32[]{:S(2)}) collective-permute-start(bf16[272,128]{1,0:T(8,128)(2,1)S(1)} %shard_map.338.whole), channel_id=1, source_target_pairs={{0,8},{8,0},{16,24},{24,16},{1,9},{9,1},{17,25},{25,17},{2,10},{10... | collective-permute-start | bytes 208904 | tf_op jit(solution)/shard_map/ppermute | solution.py:715
  78.6 2.5 %collective-permute-done.21.two = bf16[272,128]{1,0:T(8,128)(2,1)S(1)} collective-permute-done((bf16[272,128]{1,0:T(8,128)(2,1)S(1)}, bf16[272,128]{1,0:T(8,128)(2,1)S(1)}, u32[]{:S(2)}, u32[]{:S(2)}) %collective-permute-start.21) | collective-permute-done | bytes 69664 | tf_op jit(solution)/shard_map/ppermute | solution.py:715
  84.4 2.5 %collective-permute-start.37 = (bf16[1,4,272,128]{3,2,1,0:T(8,128)(2,1)S(1)}, bf16[1,4,272,128]{3,2,1,0:T(8,128)(2,1)S(1)}, u32[]{:S(2)}, u32[]{:S(2)}) collective-permute-start(bf16[1,4,272,128]{3,2,1,0:T(8,128)(2,1)S(1)} %shard_map.341.mine), channel_id=1, source_target_pairs={{0,4},{1,3},{2,6},{3,1},{4,0},{5,7},{6,2},{7,5},{8,12},{9,11},{10,... | collective-permute-start | bytes 835592 | tf_op jit(solution)/shard_map/ppermute | solution.py:737
  99.2 2.3 %collective-permute-done.35.three = bf16[272,128]{1,0:T(8,128)(2,1)S(1)} collective-permute-done((bf16[272,128]{1,0:T(8,128)(2,1)S(1)}, bf16[272,128]{1,0:T(8,128)(2,1)S(1)}, u32[]{:S(2)}, u32[]{:S(2)}) %collective-permute-start.35) | collective-permute-done | bytes 69664 | tf_op jit(solution)/shard_map/ppermute | solution.py:715
  104.7 4.2 %collective-permute-done.39.refs_1_ = bf16[2,4,272,128]{3,2,1,0:T(8,128)(2,1)S(1)} collective-permute-done((bf16[2,4,272,128]{3,2,1,0:T(8,128)(2,1)S(1)}, bf16[2,4,272,128]{3,2,1,0:T(8,128)(2,1)S(1)}, u32[]{:S(2)}, u32[]{:S(2)}) %collective-permute-start.39) | collective-permute-done | bytes 557088 | tf_op jit(solution)/shard_map/ppermute | solution.py:737
  109.7 2.0 %collective-permute-start.41 = (bf16[2,4,272,128]{3,2,1,0:T(8,128)(2,1)S(1)}, bf16[2,4,272,128]{3,2,1,0:T(8,128)(2,1)S(1)}, u32[]{:S(2)}, u32[]{:S(2)}) collective-permute-start(bf16[2,4,272,128]{3,2,1,0:T(8,128)(2,1)S(1)} %shard_map.346.refs_0_), channel_id=1, source_target_pairs={{0,2},{1,5},{2,0},{3,7},{4,6},{5,1},{6,4},{7,3},{8,10},{9,13},{10,... | collective-permute-start | bytes 1671176 | tf_op jit(solution)/shard_map/ppermute | solution.py:737
  113.6 2.4 %shard_map.348 = (f32[512,2048]{1,0:T(8,128)}, f32[16,128]{1,0:T(8,128)}, f32[4,128]{1,0:T(4,128)}, f32[4,128]{1,0:T(4,128)}) custom-call(bf16[2,4,272,128]{3,2,1,0:T(8,128)(2,1)S(1)} %shard_map.344.refs_0_, bf16[2,4,272,128]{3,2,1,0:T(8,128)(2,1)S(1)} %collective-permute-done.39.refs_1_, bf16[2,4,272,128]{3,2,1,0:T(8,128)(2,1)S(1)} %collective-permute-done.44.refs_2_, ...), custom_call_target="tpu_custom_call" | custom-call | tf_op jit(solution)/shard_map/pallas_call | solution.py:701
  116.0 2.4 %shard_map.349 = (f32[2048,512]{1,0:T(8,128)}, f32[4,128]{1,0:T(4,128)}) custom-call(bf16[2,4,272,128]{3,2,1,0:T(8,128)(2,1)S(1)} %shard_map.342.refs_0_, bf16[2,4,272,128]{3,2,1,0:T(8,128)(2,1)S(1)} %collective-permute-done.40.refs_1_, bf16[2,4,272,128]{3,2,1,0:T(8,128)(2,1)S(1)} %collective-permute-done.42.refs_2_, ...), custom_call_target="tpu_custom_call" | custom-call | tf_op jit(solution)/shard_map/pallas_call | solution.py:701
  121.2 2.4 %shard_map.350 = (f32[512,512]{1,0:T(8,128)}, f32[512,512]{1,0:T(8,128)}, f32[512,512]{1,0:T(8,128)}, f32[512,512]{1,0:T(8,128)}, f32[4,128]{1,0:T(4,128)}, /*in...) custom-call(bf16[2,4,272,128]{3,2,1,0:T(8,128)(2,1)S(1)} %shard_map.346.refs_0_, ...), custom_call_target="tpu_custom_call" | custom-call | tf_op jit(solution)/shard_map/pallas_call | solution.py:701
  (104 shorter events, 42.9 us)
Async XLA Ops:
  2.7 11.0 %collective-permute-start.1 = (bf16[112,512]{1,0:T(8,128)(2,1)S(1)}, bf16[112,512]{1,0:T(8,128)(2,1)S(1)}, u32[]{:S(2)}, u32[]{:S(2)}) collective-permute-start(bf16[112,512]{1,0:T(8,128)(2,1)S(1)} %get-tuple-element.168), channel_id=1, source_target_pairs={{1,2},{3,4},{5,6},{2,1},{4,3},{6,5},{9,10},{11,12},{13,14},{10,9},... | collective-permute-start | bytes 344072 | tf_op jit(solution)/shard_map/ppermute | solution.py:721
  3.7 10.0 %collective-permute-start.4 = (bf16[64,512]{1,0:T(8,128)(2,1)S(1)}, bf16[64,512]{1,0:T(8,128)(2,1)S(1)}, u32[]{:S(2)}, u32[]{:S(2)}) collective-permute-start(bf16[64,512]{1,0:T(8,128)(2,1)S(1)} %shard_map.325.refs_0_), channel_id=1, source_target_pairs={{0,6},{1,7},{2,4},{3,5},{4,2},{5,3},{6,0},{7,1},{8,14},{9,15},{10,... | collective-permute-start | bytes 196616 | tf_op jit(solution)/shard_map/ppermute | solution.py:715
  25.3 11.5 %collective-permute-start.10 = (bf16[2,4,272,128]{3,2,1,0:T(8,128)(2,1)S(1)}, bf16[2,4,272,128]{3,2,1,0:T(8,128)(2,1)S(1)}, u32[]{:S(2)}, u32[]{:S(2)}) collective-permute-start(bf16[2,4,272,128]{3,2,1,0:T(8,128)(2,1)S(1)} %get-tuple-element.211), channel_id=1, source_target_pairs={{0,2},{1,5},{2,0},{3,7},{4,6},{5,1},{6,4},{7,3},{8,10},{9,13},{10,... | collective-permute-start | bytes 1671176 | tf_op jit(solution)/shard_map/ppermute | solution.py:737
  27.9 15.3 %collective-permute-start.12 = (bf16[2,4,272,128]{3,2,1,0:T(8,128)(2,1)S(1)}, bf16[2,4,272,128]{3,2,1,0:T(8,128)(2,1)S(1)}, u32[]{:S(2)}, u32[]{:S(2)}) collective-permute-start(bf16[2,4,272,128]{3,2,1,0:T(8,128)(2,1)S(1)} %get-tuple-element.215), channel_id=1, source_target_pairs={{0,2},{1,5},{2,0},{3,7},{4,6},{5,1},{6,4},{7,3},{8,10},{9,13},{10,... | collective-permute-start | bytes 1671176 | tf_op jit(solution)/shard_map/ppermute | solution.py:737
  36.2 7.5 %collective-permute-start.9 = (bf16[16,112,128]{2,1,0:T(8,128)(2,1)S(1)}, bf16[16,112,128]{2,1,0:T(8,128)(2,1)S(1)}, u32[]{:S(2)}, u32[]{:S(2)}) collective-permute-start(bf16[16,112,128]{2,1,0:T(8,128)(2,1)S(1)} %get-tuple-element.210), channel_id=1, source_target_pairs={{0,1},{1,0},{2,3},{3,2},{4,5},{5,4},{6,7},{7,6},{8,9},{9,8},{10,11... | collective-permute-start | bytes 1376264 | tf_op jit(solution)/shard_map/ppermute | solution.py:715
  36.3 7.4 %collective-permute-start.7 = (bf16[16,96,128]{2,1,0:T(8,128)(2,1)S(1)}, bf16[16,96,128]{2,1,0:T(8,128)(2,1)S(1)}, u32[]{:S(2)}, u32[]{:S(2)}) collective-permute-start(bf16[16,96,128]{2,1,0:T(8,128)(2,1)S(1)} %get-tuple-element.208), channel_id=1, source_target_pairs={{0,1},{1,0},{2,3},{3,2},{4,5},{5,4},{6,7},{7,6},{8,9},{9,8},{10,11... | collective-permute-start | bytes 1179656 | tf_op jit(solution)/shard_map/ppermute | solution.py:715
  44.0 19.9 %collective-permute-start.13 = (bf16[2,4,304,128]{3,2,1,0:T(8,128)(2,1)S(1)}, bf16[2,4,304,128]{3,2,1,0:T(8,128)(2,1)S(1)}, u32[]{:S(2)}, u32[]{:S(2)}) collective-permute-start(bf16[2,4,304,128]{3,2,1,0:T(8,128)(2,1)S(1)} %get-tuple-element.224), channel_id=1, source_target_pairs={{0,2},{1,5},{2,0},{3,7},{4,6},{5,1},{6,4},{7,3},{8,10},{9,13},{10,... | collective-permute-start | bytes 1867784 | tf_op jit(solution)/shard_map/ppermute | solution.py:737
  46.3 9.6 %collective-permute-start.19 = (bf16[4,272,128]{2,1,0:T(8,128)(2,1)S(1)}, bf16[4,272,128]{2,1,0:T(8,128)(2,1)S(1)}, u32[]{:S(2)}, u32[]{:S(2)}) collective-permute-start(bf16[4,272,128]{2,1,0:T(8,128)(2,1)S(1)} %bitcast.44), channel_id=1, source_target_pairs={{0,4},{1,3},{2,6},{3,1},{4,0},{5,7},{6,2},{7,5},{8,12},{9,11},{10,... | collective-permute-start | bytes 835592 | tf_op jit(solution)/shard_map/ppermute | solution.py:737
  46.6 12.9 %collective-permute-start.16 = (bf16[272,128]{1,0:T(8,128)(2,1)S(1)}, bf16[272,128]{1,0:T(8,128)(2,1)S(1)}, u32[]{:S(2)}, u32[]{:S(2)}) collective-permute-start(bf16[272,128]{1,0:T(8,128)(2,1)S(1)} %get-tuple-element.227), channel_id=1, source_target_pairs={{0,16},{8,24},{16,0},{24,8},{1,17},{9,25},{17,1},{25,9},{2,18},{10... | collective-permute-start | bytes 208904 | tf_op jit(solution)/shard_map/ppermute | solution.py:715
  49.1 14.7 %collective-permute-start.14 = (bf16[112,512]{1,0:T(8,128)(2,1)S(1)}, bf16[112,512]{1,0:T(8,128)(2,1)S(1)}, u32[]{:S(2)}, u32[]{:S(2)}) collective-permute-start(bf16[112,512]{1,0:T(8,128)(2,1)S(1)} %get-tuple-element.225), channel_id=1, source_target_pairs={{0,1},{1,0},{2,3},{3,2},{4,5},{5,4},{6,7},{7,6},{8,9},{9,8},{10,11... | collective-permute-start | bytes 344072 | tf_op jit(solution)/shard_map/ppermute | solution.py:715
  49.2 14.7 %collective-permute-start.15 = (bf16[112,512]{1,0:T(8,128)(2,1)S(1)}, bf16[112,512]{1,0:T(8,128)(2,1)S(1)}, u32[]{:S(2)}, u32[]{:S(2)}) collective-permute-start(bf16[112,512]{1,0:T(8,128)(2,1)S(1)} %get-tuple-element.226), channel_id=1, source_target_pairs={{1,2},{3,4},{5,6},{2,1},{4,3},{6,5},{9,10},{11,12},{13,14},{10,9},... | collective-permute-start | bytes 344072 | tf_op jit(solution)/shard_map/ppermute | solution.py:721
  64.1 18.3 %collective-permute-start.20 = (bf16[4,304,128]{2,1,0:T(8,128)(2,1)S(1)}, bf16[4,304,128]{2,1,0:T(8,128)(2,1)S(1)}, u32[]{:S(2)}, u32[]{:S(2)}) collective-permute-start(bf16[4,304,128]{2,1,0:T(8,128)(2,1)S(1)} %bitcast.43), channel_id=1, source_target_pairs={{0,4},{1,3},{2,6},{3,1},{4,0},{5,7},{6,2},{7,5},{8,12},{9,11},{10,... | collective-permute-start | bytes 933896 | tf_op jit(solution)/shard_map/ppermute | solution.py:737
  64.7 7.2 %collective-permute-start.24 = (bf16[272,128]{1,0:T(8,128)(2,1)S(1)}, bf16[272,128]{1,0:T(8,128)(2,1)S(1)}, u32[]{:S(2)}, u32[]{:S(2)}) collective-permute-start(bf16[272,128]{1,0:T(8,128)(2,1)S(1)} %get-tuple-element.241), channel_id=1, source_target_pairs={{0,16},{8,24},{16,0},{24,8},{1,17},{9,25},{17,1},{25,9},{2,18},{10... | collective-permute-start | bytes 208904 | tf_op jit(solution)/shard_map/ppermute | solution.py:715
  64.7 8.2 %collective-permute-start.25 = (bf16[272,128]{1,0:T(8,128)(2,1)S(1)}, bf16[272,128]{1,0:T(8,128)(2,1)S(1)}, u32[]{:S(2)}, u32[]{:S(2)}) collective-permute-start(bf16[272,128]{1,0:T(8,128)(2,1)S(1)} %get-tuple-element.242), channel_id=1, source_target_pairs={{0,24},{8,16},{16,8},{24,0},{1,25},{9,17},{17,9},{25,1},{2,26},{10... | collective-permute-start | bytes 208904 | tf_op jit(solution)/shard_map/ppermute | solution.py:715
  68.2 8.2 %collective-permute-start.23 = (bf16[272,128]{1,0:T(8,128)(2,1)S(1)}, bf16[272,128]{1,0:T(8,128)(2,1)S(1)}, u32[]{:S(2)}, u32[]{:S(2)}) collective-permute-start(bf16[272,128]{1,0:T(8,128)(2,1)S(1)} %shard_map.336.whole), channel_id=1, source_target_pairs={{0,8},{8,0},{16,24},{24,16},{1,9},{9,1},{17,25},{25,17},{2,10},{10... | collective-permute-start | bytes 208904 | tf_op jit(solution)/shard_map/ppermute | solution.py:715
  72.9 8.2 %collective-permute-start.21 = (bf16[272,128]{1,0:T(8,128)(2,1)S(1)}, bf16[272,128]{1,0:T(8,128)(2,1)S(1)}, u32[]{:S(2)}, u32[]{:S(2)}) collective-permute-start(bf16[272,128]{1,0:T(8,128)(2,1)S(1)} %shard_map.336.whole), channel_id=1, source_target_pairs={{0,16},{8,24},{16,0},{24,8},{1,17},{9,25},{17,1},{25,9},{2,18},{10... | collective-permute-start | bytes 208904 | tf_op jit(solution)/shard_map/ppermute | solution.py:715
  74.3 8.2 %collective-permute-start.33 = (bf16[272,128]{1,0:T(8,128)(2,1)S(1)}, bf16[272,128]{1,0:T(8,128)(2,1)S(1)}, u32[]{:S(2)}, u32[]{:S(2)}) collective-permute-start(bf16[272,128]{1,0:T(8,128)(2,1)S(1)} %shard_map.338.whole), channel_id=1, source_target_pairs={{0,8},{8,0},{16,24},{24,16},{1,9},{9,1},{17,25},{25,17},{2,10},{10... | collective-permute-start | bytes 208904 | tf_op jit(solution)/shard_map/ppermute | solution.py:715
  81.1 9.2 %collective-permute-start.30 = (bf16[1,4,272,128]{3,2,1,0:T(8,128)(2,1)S(1)}, bf16[1,4,272,128]{3,2,1,0:T(8,128)(2,1)S(1)}, u32[]{:S(2)}, u32[]{:S(2)}) collective-permute-start(bf16[1,4,272,128]{3,2,1,0:T(8,128)(2,1)S(1)} %shard_map.339.mine), channel_id=1, source_target_pairs={{0,4},{1,3},{2,6},{3,1},{4,0},{5,7},{6,2},{7,5},{8,12},{9,11},{10,... | collective-permute-start | bytes 835592 | tf_op jit(solution)/shard_map/ppermute | solution.py:737
  84.4 10.4 %collective-permute-start.37 = (bf16[1,4,272,128]{3,2,1,0:T(8,128)(2,1)S(1)}, bf16[1,4,272,128]{3,2,1,0:T(8,128)(2,1)S(1)}, u32[]{:S(2)}, u32[]{:S(2)}) collective-permute-start(bf16[1,4,272,128]{3,2,1,0:T(8,128)(2,1)S(1)} %shard_map.341.mine), channel_id=1, source_target_pairs={{0,4},{1,3},{2,6},{3,1},{4,0},{5,7},{6,2},{7,5},{8,12},{9,11},{10,... | collective-permute-start | bytes 835592 | tf_op jit(solution)/shard_map/ppermute | solution.py:737
  90.4 14.4 %collective-permute-start.40 = (bf16[2,4,272,128]{3,2,1,0:T(8,128)(2,1)S(1)}, bf16[2,4,272,128]{3,2,1,0:T(8,128)(2,1)S(1)}, u32[]{:S(2)}, u32[]{:S(2)}) collective-permute-start(bf16[2,4,272,128]{3,2,1,0:T(8,128)(2,1)S(1)} %shard_map.342.refs_0_), channel_id=1, source_target_pairs={{0,2},{1,5},{2,0},{3,7},{4,6},{5,1},{6,4},{7,3},{8,10},{9,13},{10,... | collective-permute-start | bytes 1671176 | tf_op jit(solution)/shard_map/ppermute | solution.py:737
  94.8 14.1 %collective-permute-start.39 = (bf16[2,4,272,128]{3,2,1,0:T(8,128)(2,1)S(1)}, bf16[2,4,272,128]{3,2,1,0:T(8,128)(2,1)S(1)}, u32[]{:S(2)}, u32[]{:S(2)}) collective-permute-start(bf16[2,4,272,128]{3,2,1,0:T(8,128)(2,1)S(1)} %shard_map.344.refs_0_), channel_id=1, source_target_pairs={{0,2},{1,5},{2,0},{3,7},{4,6},{5,1},{6,4},{7,3},{8,10},{9,13},{10,... | collective-permute-start | bytes 1671176 | tf_op jit(solution)/shard_map/ppermute | solution.py:737
  104.7 8.9 %collective-permute-start.44 = (bf16[2,4,272,128]{3,2,1,0:T(8,128)(2,1)S(1)}, bf16[2,4,272,128]{3,2,1,0:T(8,128)(2,1)S(1)}, u32[]{:S(2)}, u32[]{:S(2)}) collective-permute-start(bf16[2,4,272,128]{3,2,1,0:T(8,128)(2,1)S(1)} %shard_map.344.refs_0_), channel_id=1, source_target_pairs={{0,1},{1,0},{2,3},{3,2},{4,5},{5,4},{6,7},{7,6},{8,9},{9,8},{10,11... | collective-permute-start | bytes 1671176 | tf_op jit(solution)/shard_map/ppermute | solution.py:715
  108.9 7.1 %collective-permute-start.42 = (bf16[2,4,272,128]{3,2,1,0:T(8,128)(2,1)S(1)}, bf16[2,4,272,128]{3,2,1,0:T(8,128)(2,1)S(1)}, u32[]{:S(2)}, u32[]{:S(2)}) collective-permute-start(bf16[2,4,272,128]{3,2,1,0:T(8,128)(2,1)S(1)} %shard_map.342.refs_0_), channel_id=1, source_target_pairs={{0,1},{1,0},{2,3},{3,2},{4,5},{5,4},{6,7},{7,6},{8,9},{9,8},{10,11... | collective-permute-start | bytes 1671176 | tf_op jit(solution)/shard_map/ppermute | solution.py:715
  109.7 9.6 %collective-permute-start.41 = (bf16[2,4,272,128]{3,2,1,0:T(8,128)(2,1)S(1)}, bf16[2,4,272,128]{3,2,1,0:T(8,128)(2,1)S(1)}, u32[]{:S(2)}, u32[]{:S(2)}) collective-permute-start(bf16[2,4,272,128]{3,2,1,0:T(8,128)(2,1)S(1)} %shard_map.346.refs_0_), channel_id=1, source_target_pairs={{0,2},{1,5},{2,0},{3,7},{4,6},{5,1},{6,4},{7,3},{8,10},{9,13},{10,... | collective-permute-start | bytes 1671176 | tf_op jit(solution)/shard_map/ppermute | solution.py:737
  (26 other events, 140.5 us)
